TPU v7x, 32 devices: a whole 2x2x4 slice. The times are simulated.
32 devices in a mesh: parts: 2 (over y), ta: 4 (over z), gz: 2 (over x), sa: 2 (over core).
Axes of the slice: x: 2, y: 2, z: 4, core: 2. Of those that a mesh axis runs over, the one named last changes fastest.
Arguments:
- iterate: float32 [4, 4, 3, 24, 4, 2, 256], P('parts', None, None, 'sa', 'ta', 'gz'), parts along dimension 0, may hold values from -1.2 to 1.2
- source: float32 [4, 4, 3, 24, 4, 2, 256], P('parts', None, None, 'sa', 'ta', 'gz'), parts along dimension 0, may hold values from -6 to 6
- gauge_links: float32 [8, 18, 4, 2, 256], P('parts', None, 'ta', 'gz'), parts along dimension 0, may hold values from -1 to 1, as said below
Outputs:
- residual: float32 [4, 4, 3, 24, 4, 2, 256], P('parts', None, None, 'sa', 'ta', 'gz'), parts along dimension 0
- corrected: float32 [4, 4, 3, 24, 4, 2, 256], P('parts', None, None, 'sa', 'ta', 'gz'), parts along dimension 0
There are 2 independent parts, one for each index of `parts`. A program takes and returns all parts, laid end to end along the dimension named above; each array names one. Nothing has to cross between parts.
Inputs may be any that keep to these rules, and one draw needn't show every extreme that they name: `gauge_links`: each 3 x 3 complex link matrix is special unitary.
All inputs are finite; a program needn't handle non-finite values.
Results may differ from a plain program's by a relative error of at most 0.00026.
Values sent between devices are 32-bit elements; how exact they have to be, the bound alone decides.
No kernel may reach another device: no remote copies, remote signals or barrier semaphores. Data moves between devices by JAX's collectives and lax.ppermute only.
A program may use at most 192 MiB of HBM per device.

v0:
```python
import jax
import jax.numpy as jnp
import numpy as np
from jax import lax
from jax.sharding import PartitionSpec as P

NX = 32
LS = 24
LS8 = 8
ITERS = 3


WALL_HEIGHT = 1.8
OUTER_SCALE = 1.5
OUTER_SHIFT = 0.5
INNER_SCALE = 1.25
INNER_SHIFT = 0.25
QUARK_MASS = 0.05
EPSILON = 1e-06
HIGHEST = lax.Precision.HIGHEST


def padded_2(array, sides, width):
    for axis, dim in sides:
        count, length = (lax.axis_size(axis), array.shape[dim])
        up = [(i, (i + 1) % count) for i in range(count)]
        down = [(j, i) for i, j in up]
        last = lax.slice_in_dim(array, length - width, length, axis=dim)
        first = lax.slice_in_dim(array, 0, width, axis=dim)
        before = lax.ppermute(last, axis, up)
        after = lax.ppermute(first, axis, down)
        array = jnp.concatenate([before, array, after], axis=dim)
    return array


def shifted(block, axis, distance):
    devices = range(lax.axis_size(axis))
    route = [((i - distance) % len(devices), i) for i in devices]
    return lax.ppermute(block, axis, route)


def gamma_tables():
    pauli_list = [
        np.array([[0, 1], [1, 0]], complex),
        np.array([[0, -1j], [1j, 0]], complex),
        np.array([[1, 0], [0, -1]], complex),
    ]
    gammas = []
    for pauli_matrix in pauli_list:
        matrix = np.zeros((4, 4), complex)
        matrix[0:2, 2:4] = -1j * pauli_matrix
        matrix[2:4, 0:2] = 1j * pauli_matrix
        gammas.append(matrix)
    fourth = np.zeros((4, 4), complex)
    fourth[0:2, 2:4] = np.eye(2)
    fourth[2:4, 0:2] = np.eye(2)
    gammas.append(fourth)
    tables = np.zeros((4, 2, 8, 8), np.float32)
    for direction in range(4):
        for sign_slot, sign_value in enumerate((-1.0, 1.0)):
            matrix = np.eye(4) + sign_value * gammas[direction]
            tables[direction, sign_slot, :4, :4] = matrix.real
            tables[direction, sign_slot, :4, 4:] = -matrix.imag
            tables[direction, sign_slot, 4:, :4] = matrix.imag
            tables[direction, sign_slot, 4:, 4:] = matrix.real
    return tables


def spin_apply(matrix, spinor):
    flattened = spinor.reshape((8,) + spinor.shape[2:])
    product = jnp.einsum(
        "pq,q...->p...", jnp.asarray(matrix, spinor.dtype), flattened, precision=HIGHEST
    )
    return product.reshape(spinor.shape)


def color_apply(link_field, spinor, dagger):
    formula = "batzw,sbltzw->saltzw" if dagger else "abtzw,sbltzw->saltzw"

    def contract(matrix_part, spinor_part):
        return jnp.einsum(formula, matrix_part, spinor_part, precision=HIGHEST)

    if dagger:
        real_part = contract(link_field[0], spinor[0]) + contract(link_field[1], spinor[1])
        imag_part = contract(link_field[0], spinor[1]) - contract(link_field[1], spinor[0])
    else:
        real_part = contract(link_field[0], spinor[0]) - contract(link_field[1], spinor[1])
        imag_part = contract(link_field[0], spinor[1]) + contract(link_field[1], spinor[0])
    return jnp.stack([real_part, imag_part])


def along_x(spinor, offset):
    lattice = spinor.reshape(spinor.shape[:-1] + (spinor.shape[-1] // NX, NX))
    return jnp.roll(lattice, -offset, axis=-1).reshape(spinor.shape)


def along_y(spinor, offset):
    lattice = spinor.reshape(spinor.shape[:-1] + (spinor.shape[-1] // NX, NX))
    return jnp.roll(lattice, -offset, axis=-2).reshape(spinor.shape)


def project_plus(spinor):
    return jnp.concatenate([spinor[:, :2], jnp.zeros_like(spinor[:, 2:])], axis=1)


def project_minus(spinor):
    return jnp.concatenate([jnp.zeros_like(spinor[:, :2]), spinor[:, 2:]], axis=1)


def complex_scale(coef_real, coef_imag, spinor):
    return jnp.stack(
        [
            coef_real * spinor[0] - coef_imag * spinor[1],
            coef_real * spinor[1] + coef_imag * spinor[0],
        ]
    )


def padded_rims(padded):
    return (
        padded[:, :, :, :, :1, 1:-1],
        padded[:, :, :, :, -1:, 1:-1],
        padded[:, :, :, :, 1:-1, :1],
        padded[:, :, :, :, 1:-1, -1:],
    )


def time_signs():
    position = lax.axis_index("ta")
    sign_low = jnp.where(position == 0, -1.0, 1.0).astype(jnp.float32)
    sign_high = jnp.where(position == lax.axis_size("ta") - 1, -1.0, 1.0).astype(jnp.float32)
    return (sign_low, sign_high)


def slice_masses():
    position = lax.axis_index("sa")
    mass_low = jnp.where(position == 0, -QUARK_MASS, 1.0).astype(jnp.float32)
    mass_high = jnp.where(position == lax.axis_size("sa") - 1, -QUARK_MASS, 1.0).astype(jnp.float32)
    return (mass_low, mass_high)


def slice_mix(spinor, low_rim, high_rim, mass_low, mass_high):
    lower_part = jnp.concatenate([mass_low * low_rim, spinor[:, :2, :, :-1]], axis=3)
    upper_part = jnp.concatenate([spinor[:, 2:, :, 1:], mass_high * high_rim], axis=3)
    return jnp.concatenate([lower_part, upper_part], axis=1)


def hopping(centre, rims, here_links, down_links, y_forward, y_backward):
    tables = gamma_tables()
    sign_low, sign_high = time_signs()
    low_time, high_time, low_depth, high_depth = rims
    forward = [
        along_x(centre, 1),
        y_forward,
        jnp.concatenate([centre[:, :, :, :, :, 1:], high_depth], axis=5),
        jnp.concatenate([centre[:, :, :, :, 1:], sign_high * high_time], axis=4),
    ]
    backward = [
        along_x(centre, -1),
        y_backward,
        jnp.concatenate([low_depth, centre[:, :, :, :, :, :-1]], axis=5),
        jnp.concatenate([sign_low * low_time, centre[:, :, :, :, :-1]], axis=4),
    ]
    total = (4.0 - WALL_HEIGHT) * centre
    for direction in range(4):
        going = color_apply(here_links[direction], forward[direction], False)
        coming = color_apply(down_links[direction], backward[direction], True)
        total = total - 0.5 * (
            spin_apply(tables[direction, 0], going) + spin_apply(tables[direction, 1], coming)
        )
    return total


def outer_operator(iterate, here_links, down_links):
    mass_low, mass_high = slice_masses()
    with_rims = padded_2(iterate, (("sa", 3),), 1)
    low_rim = with_rims[:, :2, :, :1]
    high_rim = with_rims[:, 2:, :, -1:]
    chiral_mix = slice_mix(iterate, low_rim, high_rim, mass_low, mass_high)
    blended = OUTER_SCALE * iterate + OUTER_SHIFT * chiral_mix
    rims = padded_rims(padded_2(blended, (("ta", 4), ("gz", 5)), 1))
    hopped = hopping(
        blended, rims, here_links, down_links, along_y(blended, 1), along_y(blended, -1)
    )
    return hopped + iterate - chiral_mix


def inner_rows_operator(remainder, here_links, down_links):
    chiral_mix = slice_mix(
        remainder, remainder[:, :2, :, -1:], remainder[:, 2:, :, :1], -QUARK_MASS, -QUARK_MASS
    )
    blended = INNER_SCALE * remainder + INNER_SHIFT * chiral_mix
    rims = padded_rims(padded_2(blended, (("ta", 4), ("gz", 5)), 1))
    row_rims = padded_2(blended, (("sa", 6),), NX)
    y_forward = row_rims[..., 2 * NX :]
    y_backward = row_rims[..., : -2 * NX]
    hopped = hopping(blended, rims, here_links, down_links, y_forward, y_backward)
    return hopped + remainder - chiral_mix


def minimal_residual(inner_source, operator, here_links, down_links):
    correction = jnp.zeros_like(inner_source)
    remainder = inner_source
    for iteration in range(ITERS):
        applied = operator(remainder, here_links, down_links)
        inner_real, inner_imag, weight = lax.psum(
            (
                jnp.sum(applied[0] * remainder[0] + applied[1] * remainder[1]),
                jnp.sum(applied[0] * remainder[1] - applied[1] * remainder[0]),
                jnp.sum(applied * applied),
            ),
            ("ta", "gz", "sa"),
        )
        weight = weight + EPSILON
        alpha_real = inner_real / weight
        alpha_imag = inner_imag / weight
        correction = correction + complex_scale(alpha_real, alpha_imag, remainder)
        remainder = remainder - complex_scale(alpha_real, alpha_imag, applied)
    return correction


def body(iterate, source, gauge_links):
    span = gauge_links.shape[-1]
    link_set = gauge_links.reshape((4, 2, 3, 3) + gauge_links.shape[2:])
    rim_time = shifted(gauge_links[3, :, -1:], "ta", 1)
    rim_depth = shifted(gauge_links[2, :, :, -1:], "gz", 1)
    down_time = jnp.concatenate([rim_time, gauge_links[3, :, :-1]], axis=1).reshape(
        link_set.shape[1:]
    )
    down_depth = jnp.concatenate([rim_depth, gauge_links[2, :, :, :-1]], axis=2).reshape(
        link_set.shape[1:]
    )
    here_links = [link_set[0], link_set[1], link_set[2], link_set[3]]
    down_links = [along_x(link_set[0], -1), along_y(link_set[1], -1), down_depth, down_time]
    residual = source - outer_operator(iterate, here_links, down_links)
    core_index = lax.axis_index("sa")
    local_slices = iterate.shape[3]
    global_slice = core_index * local_slices + jnp.arange(local_slices)
    first_mask = (global_slice == 0).astype(jnp.float32).reshape(-1, 1, 1, 1)
    last_mask = (global_slice == LS - 1).astype(jnp.float32).reshape(-1, 1, 1, 1)
    surface_piece = jnp.where(
        core_index == 0, project_minus(residual[:, :, :, :1]), project_plus(residual[:, :, :, -1:])
    )
    surface_slots = lax.all_to_all(surface_piece, "sa", split_axis=6, concat_axis=3, tiled=True)
    blank = jnp.zeros(surface_slots.shape[:3] + (LS8 - 2,) + surface_slots.shape[4:], jnp.float32)
    inner_source = jnp.concatenate(
        [surface_slots[:, :, :, :1], blank, surface_slots[:, :, :, 1:]], axis=3
    )
    row_width = span // lax.axis_size("sa")
    row_start = core_index * row_width
    here_rows = [
        lax.dynamic_slice_in_dim(link_field, row_start, row_width, 5) for link_field in here_links
    ]
    down_rows = [
        lax.dynamic_slice_in_dim(link_field, row_start, row_width, 5) for link_field in down_links
    ]
    correction = minimal_residual(inner_source, inner_rows_operator, here_rows, down_rows)
    returned = jnp.concatenate(
        [project_minus(correction[:, :, :, :1]), project_plus(correction[:, :, :, -1:])], axis=3
    )
    received = lax.all_to_all(returned, "sa", split_axis=3, concat_axis=6, tiled=True)
    corrected = iterate + received * (first_mask + last_mask)
    return (residual, corrected)


def solution(mesh):
    placed = (
        P("parts", None, None, "sa", "ta", "gz", None),
        P("parts", None, None, "sa", "ta", "gz", None),
        P("parts", None, "ta", "gz", None),
    )
    return jax.shard_map(
        body,
        mesh=mesh,
        in_specs=placed,
        out_specs=(
            P("parts", None, None, "sa", "ta", "gz", None),
            P("parts", None, None, "sa", "ta", "gz", None),
        ),
        check_vma=False,
    )
```

profile of v0, /device:TPU:0, one launch (start us, length us, event | category | flops | bytes accessed | tf_op | source)
XLA Modules:
  0.0 1086.0 jit_solution(6896675682057900639)
XLA Ops:
  56.2 5.3 fusion.371
  65.5 4.1 add_bitcast_fusion.5
  85.9 5.8 fusion.373
  95.7 4.1 subtract_bitcast_fusion.4
  99.8 4.1 add_bitcast_fusion.4
  111.4 4.1 fusion.65
  120.4 5.5 fusion.367
  129.8 5.0 add_bitcast_fusion.7
  134.8 5.0 subtract_bitcast_fusion.7
  144.8 5.3 fusion.369
  150.1 4.2 fusion.368
  154.3 4.1 subtract_bitcast_fusion.6
  158.4 4.1 add_bitcast_fusion.6
  190.4 5.3 fusion.379
  199.7 4.1 add_bitcast_fusion.1
  220.9 5.5 fusion.381
  253.3 5.3 fusion.375
  283.8 5.5 fusion.377
  293.3 4.1 subtract_bitcast_fusion.2
  346.4 4.2 fusion.45
  369.1 4.5 fusion.47
  391.6 4.5 fusion.41
  412.6 4.5 fusion.43
  438.1 4.5 fusion.33
  460.2 4.8 fusion.35
  483.3 4.5 fusion.37
  507.2 4.6 fusion.39
  518.6 31.0 %all-reduce.8 = (f32[]{:T(128)}, f32[]{:T(128)}, f32[]{:T(128)}) all-reduce(f32[]{:T(128)} %get-tuple-element.19, f32[]{:T(128)} %get-tuple-element.49, f32[]{:T(128)} %get-tuple-element.18), channel_id=1, replica_groups=mesh['parts'=2,'ta'=4,'gz'=2,'sa'=2] {'ta','gz','sa'}, use_global_device_ids=true, to_apply=%region_5.6 | all-reduce | flops 3 | bytes 24 | tf_op jit(solution)/shard_map/psum | solution.py:206
  578.4 4.2 fusion.201
  584.9 4.3 fusion.202
  594.4 4.5 fusion.29
  607.3 4.4 fusion.185
  614.0 4.3 fusion.187
  623.5 4.6 fusion.31
  637.4 4.2 fusion.207
  644.2 4.3 fusion.208
  653.7 4.5 fusion.25
  664.3 4.2 fusion.161
  670.7 4.3 fusion.163
  680.4 4.6 fusion.27
  696.4 4.2 fusion.89
  702.8 4.3 fusion.91
  712.5 4.6 fusion.17
  724.8 4.2 fusion.107
  731.2 4.3 fusion.109
  740.7 5.0 fusion.19
  753.3 4.2 fusion.125
  759.6 4.3 fusion.127
  769.1 4.6 fusion.21
  781.3 4.4 fusion.143
  787.9 4.3 fusion.145
  797.4 4.6 fusion.23
  809.5 30.3 %all-reduce.7 = (f32[]{:T(128)}, f32[]{:T(128)}, f32[]{:T(128)}) all-reduce(f32[]{:T(128)} %get-tuple-element.17, f32[]{:T(128)} %get-tuple-element.47, f32[]{:T(128)} %get-tuple-element.16), channel_id=1, replica_groups=mesh['parts'=2,'ta'=4,'gz'=2,'sa'=2] {'ta','gz','sa'}, use_global_device_ids=true, to_apply=%region_11.12 | all-reduce | flops 3 | bytes 24 | tf_op jit(solution)/shard_map/psum | solution.py:206
  872.4 4.2 fusion.199
  878.9 4.3 fusion.200
  888.4 4.5 fusion.13
  906.9 4.3 fusion.183
  915.8 4.5 fusion.15
  930.3 4.3 fusion.206
  939.8 4.2 fusion.9
  953.8 4.6 fusion.159
  962.9 4.2 fusion.11
  1015.6 4.3 fusion.123
  1048.0 30.8 %all-reduce.6 = (f32[]{:T(128)}, f32[]{:T(128)}, f32[]{:T(128)}) all-reduce(f32[]{:T(128)} %get-tuple-element.15, f32[]{:T(128)} %get-tuple-element.43, f32[]{:T(128)} %get-tuple-element.14), channel_id=1, replica_groups=mesh['parts'=2,'ta'=4,'gz'=2,'sa'=2] {'ta','gz','sa'}, use_global_device_ids=true, to_apply=%region_17.18 | all-reduce | flops 3 | bytes 24 | tf_op jit(solution)/shard_map/psum | solution.py:206
  (881 shorter events, 709.3 us)
Async XLA Ops:
  1.4 38.9 %collective-permute-start.1 = (f32[2,4,3,1,1,1,256]{6,1,0,3,2,5,4:T(4,128)S(1)}, f32[2,4,3,1,1,1,256]{6,1,0,3,2,5,4:T(4,128)S(1)}, u32[]{:S(2)}, u32[]{:S(2)}) collective-permute-start(f32[2,4,3,1,1,1,256]{6,1,0,3,2,5,4:T(4,128)S(1)} %copy.2105), channel_id=1, source_target_pairs={{1,0},{0,1},{3,2},{2,3},{5,4},{4,5},{7,6},{6,7},{9,8},{8,9},{11,10... | collective-permute-start | bytes 73736 | tf_op jit(solution)/shard_map/ppermute | solution.py:31
  1.9 38.4 %collective-permute-start = (f32[2,4,3,1,1,1,256]{6,1,0,3,2,5,4:T(4,128)S(1)}, f32[2,4,3,1,1,1,256]{6,1,0,3,2,5,4:T(4,128)S(1)}, u32[]{:S(2)}, u32[]{:S(2)}) collective-permute-start(f32[2,4,3,1,1,1,256]{6,1,0,3,2,5,4:T(4,128)S(1)} %copy.2108), channel_id=1, source_target_pairs={{0,1},{1,0},{2,3},{3,2},{4,5},{5,4},{6,7},{7,6},{8,9},{9,8},{10,11... | collective-permute-start | bytes 73736 | tf_op jit(solution)/shard_map/ppermute | solution.py:30
  3.0 25.9 %collective-permute-start.7 = (f32[18,1,1,256]{3,2,1,0:T(1,128)S(1)}, f32[18,1,1,256]{3,2,1,0:T(1,128)S(1)}, u32[]{:S(2)}, u32[]{:S(2)}) collective-permute-start(f32[18,1,1,256]{3,2,1,0:T(1,128)S(1)} %get-tuple-element.183), channel_id=1, source_target_pairs={{12,0},{0,4},{4,8},{8,12},{13,1},{1,5},{5,9},{9,13},{14,2},{2,6},{... | collective-permute-start | bytes 55304 | tf_op jit(solution)/shard_map/ppermute | solution.py:39
  6.0 23.0 %collective-permute-start.6 = (f32[18,1,1,256]{3,2,1,0:T(1,128)S(1)}, f32[18,1,1,256]{3,2,1,0:T(1,128)S(1)}, u32[]{:S(2)}, u32[]{:S(2)}) collective-permute-start(f32[18,1,1,256]{3,2,1,0:T(1,128)S(1)} %get-tuple-element.181), channel_id=1, source_target_pairs={{2,0},{0,2},{3,1},{1,3},{6,4},{4,6},{7,5},{5,7},{10,8},{8,10},{11,... | collective-permute-start | bytes 55304 | tf_op jit(solution)/shard_map/ppermute | solution.py:39
  10.9 29.5 %copy-start.122 = (f32[2,2,3,11,1,1,256]{6,1,0,3,2,5,4:T(2,128)}, f32[2,2,3,11,1,1,256]{6,1,0,3,2,5,4:T(2,128)S(1)}, u32[]{:S(2)}) copy-start(f32[2,2,3,11,1,1,256]{6,1,0,3,2,5,4:T(2,128)S(1)} %copy.2106) | copy-start | bytes 405508
  11.0 29.4 %copy-start.124 = (f32[2,2,3,11,1,1,256]{6,1,0,3,2,5,4:T(2,128)}, f32[2,2,3,11,1,1,256]{6,1,0,3,2,5,4:T(2,128)S(1)}, u32[]{:S(2)}) copy-start(f32[2,2,3,11,1,1,256]{6,1,0,3,2,5,4:T(2,128)S(1)} %copy.2107) | copy-start | bytes 405508
  29.1 11.3 %copy-start.91 = (f32[2,4,3,12,1,1,256]{6,5,4,3,2,1,0:T(1,128)S(1)}, f32[2,4,3,12,1,1,256]{6,5,4,3,2,1,0:T(1,128)}, u32[]{:S(2)}) copy-start(f32[2,4,3,12,1,1,256]{6,5,4,3,2,1,0:T(1,128)} %param.35) | copy-start | bytes 884740
  41.4 138.7 %collective-permute-start.3 = (f32[2,4,3,12,1,1,256]{6,1,0,3,2,5,4:T(4,128)}, f32[2,4,3,12,1,1,256]{6,1,0,3,2,5,4:T(4,128)}, u32[]{:S(2)}, u32[]{:S(2)}) collective-permute-start(f32[2,4,3,12,1,1,256]{6,1,0,3,2,5,4:T(4,128)} %multiply_add_fusion.1), channel_id=1, source_target_pairs={{4,0},{8,4},{12,8},{0,12},{5,1},{9,5},{13,9},{1,13},{6,2},{10,6},{... | collective-permute-start | bytes 884744 | tf_op jit(solution)/shard_map/ppermute | solution.py:31
  43.6 136.4 %collective-permute-start.2 = (f32[2,4,3,12,1,1,256]{6,1,0,3,2,5,4:T(4,128)}, f32[2,4,3,12,1,1,256]{6,1,0,3,2,5,4:T(4,128)}, u32[]{:S(2)}, u32[]{:S(2)}) collective-permute-start(f32[2,4,3,12,1,1,256]{6,1,0,3,2,5,4:T(4,128)} %multiply_add_fusion.1), channel_id=1, source_target_pairs={{0,4},{4,8},{8,12},{12,0},{1,5},{5,9},{9,13},{13,1},{2,6},{6,10},{... | collective-permute-start | bytes 884744 | tf_op jit(solution)/shard_map/ppermute | solution.py:30
  182.3 64.9 %collective-permute-start.4 = (f32[2,4,3,12,3,1,256]{6,1,0,3,2,5,4:T(4,128)}, f32[2,4,3,12,3,1,256]{6,1,0,3,2,5,4:T(4,128)}, u32[]{:S(2)}, u32[]{:S(2)}) collective-permute-start(f32[2,4,3,12,3,1,256]{6,1,0,3,2,5,4:T(4,128)} %pad_maximum_fusion.8), channel_id=1, source_target_pairs={{2,0},{0,2},{3,1},{1,3},{6,4},{4,6},{7,5},{5,7},{10,8},{8,10},{11,... | collective-permute-start | bytes 2654216 | tf_op jit(solution)/shard_map/ppermute | solution.py:31
  182.7 95.4 %collective-permute-start.5 = (f32[2,4,3,12,3,1,256]{6,1,0,3,2,5,4:T(4,128)}, f32[2,4,3,12,3,1,256]{6,1,0,3,2,5,4:T(4,128)}, u32[]{:S(2)}, u32[]{:S(2)}) collective-permute-start(f32[2,4,3,12,3,1,256]{6,1,0,3,2,5,4:T(4,128)} %pad_maximum_fusion.8), channel_id=1, source_target_pairs={{0,2},{2,0},{1,3},{3,1},{4,6},{6,4},{5,7},{7,5},{8,10},{10,8},{9,1... | collective-permute-start | bytes 2654216 | tf_op jit(solution)/shard_map/ppermute | solution.py:30
  311.8 9.5 copy-start.146
  321.1 484.1 %copy-start.102 = (f32[2,4,3,1,1,1,128]{6,1,5,4,3,2,0:T(4,128)}, f32[2,4,3,1,1,1,128]{6,1,5,4,3,2,0:T(4,128)S(1)}, u32[]{:S(2)}) copy-start(f32[2,4,3,1,1,1,128]{6,1,5,4,3,2,0:T(4,128)S(1)} %get-tuple-element.190) | copy-start | bytes 36868
  321.2 484.1 %copy-start.104 = (f32[2,4,3,1,1,1,128]{6,1,5,4,3,2,0:T(4,128)}, f32[2,4,3,1,1,1,128]{6,1,5,4,3,2,0:T(4,128)S(1)}, u32[]{:S(2)}) copy-start(f32[2,4,3,1,1,1,128]{6,1,5,4,3,2,0:T(4,128)S(1)} %get-tuple-element.193) | copy-start | bytes 36868
  322.0 97.7 %collective-permute-start.10 = (f32[2,4,3,8,1,1,128]{6,3,1,2,5,4,0:T(8,128)S(1)}, f32[2,4,3,8,1,1,128]{6,3,1,2,5,4,0:T(8,128)}, u32[]{:S(2)}, u32[]{:S(2)}) collective-permute-start(f32[2,4,3,8,1,1,128]{6,3,1,2,5,4,0:T(8,128)S(1)} %get-tuple-element.189), channel_id=1, source_target_pairs={{0,4},{4,8},{8,12},{12,0},{1,5},{5,9},{9,13},{13,1},{2,6},{6,10},{... | collective-permute-start | bytes 294920 | tf_op jit(solution)/shard_map/ppermute | solution.py:30
  323.3 96.4 %collective-permute-start.11 = (f32[2,4,3,8,1,1,128]{6,3,1,2,5,4,0:T(8,128)S(1)}, f32[2,4,3,8,1,1,128]{6,3,1,2,5,4,0:T(8,128)}, u32[]{:S(2)}, u32[]{:S(2)}) collective-permute-start(f32[2,4,3,8,1,1,128]{6,3,1,2,5,4,0:T(8,128)S(1)} %get-tuple-element.189), channel_id=1, source_target_pairs={{4,0},{8,4},{12,8},{0,12},{5,1},{9,5},{13,9},{1,13},{6,2},{10,6},{... | collective-permute-start | bytes 294920 | tf_op jit(solution)/shard_map/ppermute | solution.py:31
  331.0 45.8 %collective-permute-start.8 = (f32[2,4,3,8,1,1,32]{6,3,1,2,5,4,0:T(8,128)}, f32[2,4,3,8,1,1,32]{6,3,1,2,5,4,0:T(8,128)}, u32[]{:S(2)}, u32[]{:S(2)}) collective-permute-start(f32[2,4,3,8,1,1,32]{6,3,1,2,5,4,0:T(8,128)} %get-tuple-element.168), channel_id=1, source_target_pairs={{1,0},{0,1},{3,2},{2,3},{5,4},{4,5},{7,6},{6,7},{9,8},{8,9},{11,10... | collective-permute-start | bytes 73736 | tf_op jit(solution)/shard_map/ppermute | solution.py:31
  331.1 45.8 %collective-permute-start.9 = (f32[2,4,3,8,1,1,32]{6,3,1,2,5,4,0:T(8,128)}, f32[2,4,3,8,1,1,32]{6,3,1,2,5,4,0:T(8,128)}, u32[]{:S(2)}, u32[]{:S(2)}) collective-permute-start(f32[2,4,3,8,1,1,32]{6,3,1,2,5,4,0:T(8,128)} %get-tuple-element.169), channel_id=1, source_target_pairs={{0,1},{1,0},{2,3},{3,2},{4,5},{5,4},{6,7},{7,6},{8,9},{9,8},{10,11... | collective-permute-start | bytes 73736 | tf_op jit(solution)/shard_map/ppermute | solution.py:30
  346.4 6.6 copy-start.177
  358.3 6.2 copy-start.27
  369.1 6.7 copy-start.169
  401.4 6.6 copy-start.30
  417.2 9.9 copy-start.11
  421.4 46.9 %collective-permute-start.13 = (f32[2,4,3,8,3,1,128]{6,3,1,2,5,4,0:T(8,128)}, f32[2,4,3,8,3,1,128]{6,3,1,2,5,4,0:T(8,128)}, u32[]{:S(2)}, u32[]{:S(2)}) collective-permute-start(f32[2,4,3,8,3,1,128]{6,3,1,2,5,4,0:T(8,128)} %pad_maximum_fusion.14), channel_id=1, source_target_pairs={{0,2},{2,0},{1,3},{3,1},{4,6},{6,4},{5,7},{7,5},{8,10},{10,8},{9,1... | collective-permute-start | bytes 884744 | tf_op jit(solution)/shard_map/ppermute | solution.py:30
  421.7 70.0 %collective-permute-start.12 = (f32[2,4,3,8,3,1,128]{6,3,1,2,5,4,0:T(8,128)}, f32[2,4,3,8,3,1,128]{6,3,1,2,5,4,0:T(8,128)}, u32[]{:S(2)}, u32[]{:S(2)}) collective-permute-start(f32[2,4,3,8,3,1,128]{6,3,1,2,5,4,0:T(8,128)} %pad_maximum_fusion.14), channel_id=1, source_target_pairs={{2,0},{0,2},{3,1},{1,3},{6,4},{4,6},{7,5},{5,7},{10,8},{8,10},{11,... | collective-permute-start | bytes 884744 | tf_op jit(solution)/shard_map/ppermute | solution.py:31
  427.1 6.2 copy-start.24
  448.7 6.2 copy-start.15
  460.2 7.1 copy-start.154
  464.9 6.9 copy-start.10
  471.8 6.2 copy-start.21
  487.8 7.5 copy-start.9
  495.3 6.7 copy-start.18
  517.1 33.8 %copy-start.110 = (f32[2,4,3,8,128]{4,3,1,2,0:T(8,128)}, f32[2,4,3,8,128]{4,3,1,2,0:T(8,128)S(1)}, u32[]{:S(2)}) copy-start(f32[2,4,3,8,128]{4,3,1,2,0:T(8,128)S(1)} %get-tuple-element.50) | copy-start | bytes 294916
  553.2 6.4 copy-start.120
  553.2 7.1 copy-start.119
  553.9 135.0 %collective-permute-start.16 = (f32[2,4,3,8,1,1,128]{6,3,1,2,5,4,0:T(8,128)}, f32[2,4,3,8,1,1,128]{6,3,1,2,5,4,0:T(8,128)}, u32[]{:S(2)}, u32[]{:S(2)}) collective-permute-start(f32[2,4,3,8,1,1,128]{6,3,1,2,5,4,0:T(8,128)} %fusion.221), channel_id=1, source_target_pairs={{0,4},{4,8},{8,12},{12,0},{1,5},{5,9},{9,13},{13,1},{2,6},{6,10},{... | collective-permute-start | bytes 294920 | tf_op jit(solution)/shard_map/ppermute | solution.py:30
  553.9 135.0 %collective-permute-start.17 = (f32[2,4,3,8,1,1,128]{6,3,1,2,5,4,0:T(8,128)}, f32[2,4,3,8,1,1,128]{6,3,1,2,5,4,0:T(8,128)}, u32[]{:S(2)}, u32[]{:S(2)}) collective-permute-start(f32[2,4,3,8,1,1,128]{6,3,1,2,5,4,0:T(8,128)} %fusion.221), channel_id=1, source_target_pairs={{4,0},{8,4},{12,8},{0,12},{5,1},{9,5},{13,9},{1,13},{6,2},{10,6},{... | collective-permute-start | bytes 294920 | tf_op jit(solution)/shard_map/ppermute | solution.py:31
  574.6 58.8 %collective-permute-start.14 = (f32[2,4,3,8,1,1,32]{6,3,1,2,5,4,0:T(8,128)}, f32[2,4,3,8,1,1,32]{6,3,1,2,5,4,0:T(8,128)}, u32[]{:S(2)}, u32[]{:S(2)}) collective-permute-start(f32[2,4,3,8,1,1,32]{6,3,1,2,5,4,0:T(8,128)} %get-tuple-element.154), channel_id=1, source_target_pairs={{1,0},{0,1},{3,2},{2,3},{5,4},{4,5},{7,6},{6,7},{9,8},{8,9},{11,10... | collective-permute-start | bytes 73736 | tf_op jit(solution)/shard_map/ppermute | solution.py:31
  574.6 58.8 %collective-permute-start.15 = (f32[2,4,3,8,1,1,32]{6,3,1,2,5,4,0:T(8,128)}, f32[2,4,3,8,1,1,32]{6,3,1,2,5,4,0:T(8,128)}, u32[]{:S(2)}, u32[]{:S(2)}) collective-permute-start(f32[2,4,3,8,1,1,32]{6,3,1,2,5,4,0:T(8,128)} %get-tuple-element.155), channel_id=1, source_target_pairs={{0,1},{1,0},{2,3},{3,2},{4,5},{5,4},{6,7},{7,6},{8,9},{9,8},{10,11... | collective-permute-start | bytes 73736 | tf_op jit(solution)/shard_map/ppermute | solution.py:30
  594.4 7.5 copy-start.178
  623.5 7.6 copy-start.170
  653.7 7.5 copy-start.167
  680.4 7.6 copy-start.163
  690.7 58.9 %collective-permute-start.19 = (f32[2,4,3,8,3,1,128]{6,3,1,2,5,4,0:T(8,128)}, f32[2,4,3,8,3,1,128]{6,3,1,2,5,4,0:T(8,128)}, u32[]{:S(2)}, u32[]{:S(2)}) collective-permute-start(f32[2,4,3,8,3,1,128]{6,3,1,2,5,4,0:T(8,128)} %pad_maximum_fusion.15), channel_id=1, source_target_pairs={{0,2},{2,0},{1,3},{3,1},{4,6},{6,4},{5,7},{7,5},{8,10},{10,8},{9,1... | collective-permute-start | bytes 884744 | tf_op jit(solution)/shard_map/ppermute | solution.py:30
  690.7 87.0 %collective-permute-start.18 = (f32[2,4,3,8,3,1,128]{6,3,1,2,5,4,0:T(8,128)}, f32[2,4,3,8,3,1,128]{6,3,1,2,5,4,0:T(8,128)}, u32[]{:S(2)}, u32[]{:S(2)}) collective-permute-start(f32[2,4,3,8,3,1,128]{6,3,1,2,5,4,0:T(8,128)} %pad_maximum_fusion.15), channel_id=1, source_target_pairs={{2,0},{0,2},{3,1},{1,3},{6,4},{4,6},{7,5},{5,7},{10,8},{8,10},{11,... | collective-permute-start | bytes 884744 | tf_op jit(solution)/shard_map/ppermute | solution.py:31
  712.5 7.6 copy-start.159
  740.7 8.0 copy-start.155
  769.1 7.6 copy-start.151
  845.8 123.8 %collective-permute-start.23 = (f32[2,4,3,8,1,1,128]{6,3,1,2,5,4,0:T(8,128)}, f32[2,4,3,8,1,1,128]{6,3,1,2,5,4,0:T(8,128)}, u32[]{:S(2)}, u32[]{:S(2)}) collective-permute-start(f32[2,4,3,8,1,1,128]{6,3,1,2,5,4,0:T(8,128)} %fusion.222), channel_id=1, source_target_pairs={{4,0},{8,4},{12,8},{0,12},{5,1},{9,5},{13,9},{1,13},{6,2},{10,6},{... | collective-permute-start | bytes 294920 | tf_op jit(solution)/shard_map/ppermute | solution.py:31
  845.8 123.8 %collective-permute-start.22 = (f32[2,4,3,8,1,1,128]{6,3,1,2,5,4,0:T(8,128)}, f32[2,4,3,8,1,1,128]{6,3,1,2,5,4,0:T(8,128)}, u32[]{:S(2)}, u32[]{:S(2)}) collective-permute-start(f32[2,4,3,8,1,1,128]{6,3,1,2,5,4,0:T(8,128)} %fusion.222), channel_id=1, source_target_pairs={{0,4},{4,8},{8,12},{12,0},{1,5},{5,9},{9,13},{13,1},{2,6},{6,10},{... | collective-permute-start | bytes 294920 | tf_op jit(solution)/shard_map/ppermute | solution.py:30
  868.7 54.8 %collective-permute-start.20 = (f32[2,4,3,8,1,1,32]{6,3,1,2,5,4,0:T(8,128)}, f32[2,4,3,8,1,1,32]{6,3,1,2,5,4,0:T(8,128)}, u32[]{:S(2)}, u32[]{:S(2)}) collective-permute-start(f32[2,4,3,8,1,1,32]{6,3,1,2,5,4,0:T(8,128)} %get-tuple-element.146), channel_id=1, source_target_pairs={{1,0},{0,1},{3,2},{2,3},{5,4},{4,5},{7,6},{6,7},{9,8},{8,9},{11,10... | collective-permute-start | bytes 73736 | tf_op jit(solution)/shard_map/ppermute | solution.py:31
  868.7 54.8 %collective-permute-start.21 = (f32[2,4,3,8,1,1,32]{6,3,1,2,5,4,0:T(8,128)}, f32[2,4,3,8,1,1,32]{6,3,1,2,5,4,0:T(8,128)}, u32[]{:S(2)}, u32[]{:S(2)}) collective-permute-start(f32[2,4,3,8,1,1,32]{6,3,1,2,5,4,0:T(8,128)} %get-tuple-element.147), channel_id=1, source_target_pairs={{0,1},{1,0},{2,3},{3,2},{4,5},{5,4},{6,7},{7,6},{8,9},{9,8},{10,11... | collective-permute-start | bytes 73736 | tf_op jit(solution)/shard_map/ppermute | solution.py:30
  904.5 6.7 copy-start.29
  915.8 7.0 copy-start.116
  915.8 7.0 copy-start.143
  945.6 6.8 copy-start.135
  971.3 38.5 %collective-permute-start.25 = (f32[2,4,3,8,3,1,128]{6,3,1,2,5,4,0:T(8,128)}, f32[2,4,3,8,3,1,128]{6,3,1,2,5,4,0:T(8,128)}, u32[]{:S(2)}, u32[]{:S(2)}) collective-permute-start(f32[2,4,3,8,3,1,128]{6,3,1,2,5,4,0:T(8,128)} %pad_maximum_fusion.16), channel_id=1, source_target_pairs={{0,2},{2,0},{1,3},{3,1},{4,6},{6,4},{5,7},{7,5},{8,10},{10,8},{9,1... | collective-permute-start | bytes 884744 | tf_op jit(solution)/shard_map/ppermute | solution.py:30
  971.3 58.3 %collective-permute-start.24 = (f32[2,4,3,8,3,1,128]{6,3,1,2,5,4,0:T(8,128)}, f32[2,4,3,8,3,1,128]{6,3,1,2,5,4,0:T(8,128)}, u32[]{:S(2)}, u32[]{:S(2)}) collective-permute-start(f32[2,4,3,8,3,1,128]{6,3,1,2,5,4,0:T(8,128)} %pad_maximum_fusion.16), channel_id=1, source_target_pairs={{2,0},{0,2},{3,1},{1,3},{6,4},{4,6},{7,5},{5,7},{10,8},{8,10},{11,... | collective-permute-start | bytes 884744 | tf_op jit(solution)/shard_map/ppermute | solution.py:31
  1045.6 35.3 %copy-start.136 = (f32[1,4,3,8,1,1,128]{6,3,1,2,5,4,0:T(8,128)S(1)}, f32[1,4,3,8,1,1,128]{6,3,1,2,5,4,0:T(8,128)}, u32[]{:S(2)}) copy-start(f32[1,4,3,8,1,1,128]{6,3,1,2,5,4,0:T(8,128)} %get-tuple-element.135) | copy-start | bytes 147460
  1045.6 35.3 %copy-start.137 = (f32[1,4,3,8,1,1,128]{6,3,1,2,5,4,0:T(8,128)S(1)}, f32[1,4,3,8,1,1,128]{6,3,1,2,5,4,0:T(8,128)}, u32[]{:S(2)}) copy-start(f32[1,4,3,8,1,1,128]{6,3,1,2,5,4,0:T(8,128)} %get-tuple-element.136) | copy-start | bytes 147460
  1045.6 35.3 %copy-start.138 = (f32[1,4,3,8,1,1,128]{6,3,1,2,5,4,0:T(8,128)S(1)}, f32[1,4,3,8,1,1,128]{6,3,1,2,5,4,0:T(8,128)}, u32[]{:S(2)}) copy-start(f32[1,4,3,8,1,1,128]{6,3,1,2,5,4,0:T(8,128)} %get-tuple-element.133) | copy-start | bytes 147460
  1045.6 35.3 %copy-start.139 = (f32[1,4,3,8,1,1,128]{6,3,1,2,5,4,0:T(8,128)S(1)}, f32[1,4,3,8,1,1,128]{6,3,1,2,5,4,0:T(8,128)}, u32[]{:S(2)}) copy-start(f32[1,4,3,8,1,1,128]{6,3,1,2,5,4,0:T(8,128)} %get-tuple-element.134) | copy-start | bytes 147460
  1045.6 39.2 %copy-start.93 = (f32[2,4,3,12,1,1,256]{6,5,4,3,2,1,0:T(1,128)S(1)}, f32[2,4,3,12,1,1,256]{6,5,4,3,2,1,0:T(1,128)}, u32[]{:S(2)}) copy-start(f32[2,4,3,12,1,1,256]{6,5,4,3,2,1,0:T(1,128)} %param.35) | copy-start | bytes 884740
  1045.6 39.1 %copy-start.179 = (f32[12]{0:T(128)S(1)}, f32[12]{0:T(128)}, u32[]{:S(2)}) copy-start(f32[12]{0:T(128)} %fusion.339) | copy-start | bytes 148
  (142 other events, 594.4 us)
where the time goes:
time: 1100 us; the launch traced here: 1090 us
  matrix products  524 us (48%)
  local copies, waits for them, and re-layouts  324 us (29%)
  other arithmetic  102 us (9%)
  blocking collectives  99.6 us (9%)
  starting transfers between devices  27.4 us (2%)
    dot_general x128, matrix products, contract(): return jnp.einsum(formula, matrix_part, spinor_part, precision=HIGHEST)  494 us
    another operation x56, local copies, waits for them, and re-layouts, color_apply(): return jnp.stack([real_part, imag_part])  113 us
    another operation x92, local copies, waits for them, and re-layouts  101 us
    psum x3, blocking collectives, minimal_residual(): lax.psum((jnp.sum(applied[0] * remainder[0] + applied[1] * remainder[1]),...  92.2 us
    another operation x32, other arithmetic, color_apply(): return jnp.stack([real_part, imag_part])  36.2 us
    dot_general x32, matrix products, spin_apply(): jnp.einsum('pq,q...->p...', jnp.asarray(matrix, spinor.dtype), flattened,...  30 us
    slice x10, local copies, waits for them, and re-layouts, color_apply(): spinor[0]  24.5 us
  transfers between devices with their start and end apart: 26, of which 0 were waited for; matrix products, arithmetic and copies ran while one was open for 75% of the time, Pallas kernels for 0%

commit v1 on v0

--- a/solution.py
+++ b/solution.py
@@ -2,6 +2,8 @@
 import jax.numpy as jnp
 import numpy as np
 from jax import lax
+from jax.experimental import pallas as pl
+from jax.experimental.pallas import tpu as pltpu
 from jax.sharding import PartitionSpec as P
 
 NX = 32
@@ -263,14 +265,503 @@
     return (residual, corrected)
 
 
+UPPER = [ri * 12 + sp * 3 + c for ri in range(2) for sp in (0, 1) for c in range(3)]
+LOWER = [ri * 12 + sp * 3 + c for ri in range(2) for sp in (2, 3) for c in range(3)]
+RE, IM = 0, 1
+SPIN = (
+    (((1, 1, IM), (-1, 1, RE)), ((1, 0, IM), (-1, 0, RE))),
+    (((-1, 1, RE), (-1, 1, IM)), ((1, 0, RE), (1, 0, IM))),
+    (((1, 0, IM), (-1, 0, RE)), ((-1, 1, IM), (1, 1, RE))),
+    (((1, 0, RE), (1, 0, IM)), ((1, 1, RE), (1, 1, IM))),
+)
+ROWS = 24
+FIELD = 576
+LINKS = 72
+BLOCK = 144
+MESSAGE = 2 * BLOCK
+VMEM_LIMIT = 48 * 1024 * 1024
+
+
+def number(part, spin, color):
+    return part * 12 + spin * 3 + color
+
+
+def half_spinor(get, direction, side):
+    out = {}
+    for spin in range(2):
+        for part in range(2):
+            sign, from_spin, from_part = SPIN[direction][spin][part]
+            for color in range(3):
+                up = get(number(part, spin, color))
+                low = get(number(from_part, 2 + from_spin, color))
+                out[spin, part, color] = up + low if sign * side > 0 else up - low
+    return out
+
+
+def link_times(link, half, dagger):
+    out = {}
+    for row in range(3):
+        for spin in range(2):
+            real, imag = (None, None)
+            for col in range(3):
+                a, b = (col, row) if dagger else (row, col)
+                ur, ui = (link(RE, a, b), link(IM, a, b))
+                hr, hi = (half[spin, RE, col], half[spin, IM, col])
+                if dagger:
+                    re_new, im_new = (ur * hr + ui * hi, ur * hi - ui * hr)
+                else:
+                    re_new, im_new = (ur * hr - ui * hi, ur * hi + ui * hr)
+                real = re_new if real is None else real + re_new
+                imag = im_new if imag is None else imag + im_new
+            out[spin, RE, row] = real
+            out[spin, IM, row] = imag
+    return out
+
+
+def add_hop(acc, half, direction, side):
+    flip = 1 if direction == 3 else -1
+    for spin in range(2):
+        for part in range(2):
+            sign, from_spin, from_part = SPIN[direction][spin][part]
+            for color in range(3):
+                up = number(part, spin, color)
+                acc[up] = acc[up] + half[spin, part, color]
+                low = number(part, 2 + spin, color)
+                g = half[from_spin, from_part, color]
+                acc[low] = acc[low] + g if sign * side * flip > 0 else acc[low] - g
+    return acc
+
+
+def roll(x, shift, axis):
+    return pltpu.roll(x, shift % x.shape[axis], axis)
+
+
+def lane():
+    return lax.broadcasted_iota(jnp.int32, (8, 128), 1)
+
+
+def sublane():
+    return lax.broadcasted_iota(jnp.int32, (8, 128), 0)
+
+
+def move_x(x, offset):
+    edge = lane() % NX == (NX - 1 if offset > 0 else 0)
+    return jnp.where(edge, roll(x, offset * (NX - 1), 1), roll(x, -offset, 1))
+
+
+def move_y(x, offset):
+    near = roll(x, -offset * NX, 1)
+    far = jnp.where(sublane() % 2 == 0, roll(near, -1, 0), roll(near, 1, 0))
+    edge = lane() // NX == (3 if offset > 0 else 0)
+    return jnp.where(edge, far, near)
+
+
+def move_t(x, offset):
+    return roll(x, -offset * 2, 0)
+
+
+def pairs(x):
+    return jnp.concatenate([x, x, x, x], axis=0)
+
+
+def scaled_links(gauge_ref, tile_ref, slot, direction, scale):
+    for entry in range(18):
+        row = (direction * 18 + entry) * 2
+        tile_ref[slot * 18 + entry] = pairs(gauge_ref[row : row + 2, :]) * scale
+
+
+def tile_link(tile_ref, slot):
+    return lambda part, a, b: tile_ref[slot * 18 + part * 9 + a * 3 + b]
+
+
+def blend_rows(out_ref, here_ref, there_ref, mass_low, mass_high):
+    row = lax.broadcasted_iota(jnp.int32, (ROWS, 128), 0)
+    for comp in range(24):
+        rows = slice(comp * ROWS, (comp + 1) * ROWS)
+        v, other = (here_ref[rows, :], there_ref[rows, :])
+        if comp in UPPER:
+            chi = jnp.where(row < 2, roll(other, 2, 0) * mass_low, roll(v, 2, 0))
+        else:
+            chi = jnp.where(row >= ROWS - 2, roll(other, -2, 0) * mass_high, roll(v, -2, 0))
+        out_ref[rows, :] = OUTER_SCALE * v + OUTER_SHIFT * chi
+
+
+def send_kernel(own_ref, oth_ref, src_own_ref, src_oth_ref, gauge_ref, mt_ref, mz_ref, blk_ref, bl_ref, blo_ref, tile_ref):
+    core = lax.axis_index("sa")
+    last_time = lax.axis_index("ta") == lax.axis_size("ta") - 1
+    time_scale = jnp.where(last_time, 0.5, -0.5).astype(jnp.float32)
+    first = jnp.where(core == 0, -QUARK_MASS, 1.0).astype(jnp.float32)
+    last = jnp.where(core == 0, 1.0, -QUARK_MASS).astype(jnp.float32)
+    blend_rows(bl_ref, own_ref, oth_ref, first, last)
+    blend_rows(blo_ref, oth_ref, own_ref, last, first)
+
+    sign_row = lax.broadcasted_iota(jnp.int32, (LINKS, 128), 0) >= 54
+    link_sign = jnp.where(jnp.logical_and(sign_row, last_time), 0.5, -0.5).astype(jnp.float32)
+    for h in range(2):
+        base = h * BLOCK
+        blk_ref[base : base + LINKS, :] = gauge_ref[pl.ds(h, LINKS, stride=2), :] * link_sign
+
+    def surfaces(bl0_ref, it0_ref, src0_ref, bl1_ref, it1_ref, src1_ref):
+        for h in range(2):
+            base = h * BLOCK + LINKS
+            blk_ref[base : base + 24, :] = bl0_ref[pl.ds(h, 24, stride=ROWS), :]
+            blk_ref[base + 24 : base + 48, :] = bl1_ref[pl.ds(22 + h, 24, stride=ROWS), :]
+            for part in range(2):
+                start = (part * 12 + 6) * ROWS + h
+                value = (
+                    src0_ref[pl.ds(start, 6, stride=ROWS), :]
+                    - it0_ref[pl.ds(start, 6, stride=ROWS), :]
+                    + it0_ref[pl.ds(start + 2, 6, stride=ROWS), :]
+                )
+                blk_ref[base + 48 + part * 6 : base + 54 + part * 6, :] = value
+                start = part * 12 * ROWS + 22 + h
+                value = (
+                    src1_ref[pl.ds(start, 6, stride=ROWS), :]
+                    - it1_ref[pl.ds(start, 6, stride=ROWS), :]
+                    + it1_ref[pl.ds(start - 2, 6, stride=ROWS), :]
+                )
+                blk_ref[base + 60 + part * 6 : base + 66 + part * 6, :] = value
+
+    pl.when(core == 0)(lambda: surfaces(bl_ref, own_ref, src_own_ref, blo_ref, oth_ref, src_oth_ref))
+    pl.when(core == 1)(lambda: surfaces(blo_ref, oth_ref, src_oth_ref, bl_ref, own_ref, src_own_ref))
+
+    scaled_links(gauge_ref, tile_ref, 0, 2, -0.5)
+    scaled_links(gauge_ref, tile_ref, 1, 3, time_scale)
+
+    def store(ref, half, offset, g):
+        for (spin, part, color), value in half.items():
+            ref[pl.ds(offset + (part * 6 + spin * 3 + color) * ROWS + g * 8, 8), :] = value
+
+    def getter(ref, g):
+        return lambda comp: ref[pl.ds(comp * ROWS + g * 8, 8), :]
+
+    for g in range(3):
+        get = getter(bl_ref, g)
+        store(mz_ref, half_spinor(get, 2, -1), 0, g)
+        store(mz_ref, link_times(tile_link(tile_ref, 0), half_spinor(get, 2, 1), True), 288, g)
+
+    def time_up(first_ref, second_ref):
+        for which, ref in enumerate((first_ref, second_ref)):
+            for g in range(3):
+                half = half_spinor(getter(ref, g), 3, 1)
+                store(mt_ref, link_times(tile_link(tile_ref, 1), half, True), which * 288, g)
+
+    def time_down(first_ref, second_ref):
+        for which, ref in enumerate((first_ref, second_ref)):
+            for g in range(3):
+                store(mt_ref, half_spinor(getter(ref, g), 3, -1), which * 288, g)
+
+    pl.when(core == 0)(lambda: time_up(bl_ref, blo_ref))
+    pl.when(core == 1)(lambda: time_down(blo_ref, bl_ref))
+    mt_ref[FIELD : FIELD + MESSAGE, :] = blk_ref[...]
+    mz_ref[FIELD : FIELD + MESSAGE, :] = blk_ref[...]
+
+
+def local_kernel(own_ref, bl_ref, src_ref, gauge_ref, acc_ref, tile_ref):
+    scaled_links(gauge_ref, tile_ref, 0, 0, -0.5)
+    scaled_links(gauge_ref, tile_ref, 1, 1, -0.5)
+
+    def group(g, carry):
+        def rows(comp):
+            return pl.ds(pl.multiple_of(comp * ROWS + g * 8, 8), 8)
+
+        get = lambda comp: bl_ref[rows(comp), :]
+        acc = [0.2 * get(comp) + 4.0 * own_ref[rows(comp), :] - src_ref[rows(comp), :] for comp in range(24)]
+        for direction, move in ((0, move_x), (1, move_y)):
+            link = tile_link(tile_ref, direction)
+            half = {k: move(h, 1) for k, h in half_spinor(get, direction, -1).items()}
+            acc = add_hop(acc, link_times(link, half, False), direction, -1)
+            half = link_times(link, half_spinor(get, direction, 1), True)
+            acc = add_hop(acc, {k: move(h, -1) for k, h in half.items()}, direction, 1)
+        for comp in range(24):
+            acc_ref[rows(comp), :] = acc[comp]
+        return carry
+
+    lax.fori_loop(0, 3, group, 0)
+
+
+def inner_kernel(own_ref, x2_ref, x1a_ref, x1b_ref, x3a_ref, x3b_ref, x4a_ref, x4b_ref, out_ref, gather_ref, link_ref, base_ref, r_ref, a_ref, z_ref, sem):
+    core = lax.axis_index("sa")
+    pick = lambda zero, one: jnp.where(core == 0, zero, one)
+    placed = (
+        (own_ref, 0, 0),
+        (x2_ref, FIELD, 4),
+        (x1a_ref, FIELD, pick(3, 1)),
+        (x1b_ref, FIELD, pick(1, 3)),
+        (x3a_ref, 0, pick(2, 5)),
+        (x3b_ref, 0, pick(5, 2)),
+        (x4a_ref, 0, pick(7, 6)),
+        (x4b_ref, 0, pick(6, 7)),
+    )
+    copies = []
+    for i, (ref, start, slot) in enumerate(placed):
+        to = gather_ref.at[pl.ds(pl.multiple_of(slot * MESSAGE, 8), MESSAGE), :]
+        copies.append(pltpu.make_async_copy(ref.at[pl.ds(start, MESSAGE), :], to, sem.at[i]))
+        copies[-1].start()
+    zero = jnp.zeros((8, 128), jnp.float32)
+    for s in range(8):
+        for comp in range(24):
+            for dz in range(2):
+                r_ref[s, comp, dz] = zero
+    for copy in copies:
+        copy.wait()
+
+    def gathered(comp, dz):
+        return gather_ref[pl.ds(dz * 8 * BLOCK + comp, 8, stride=BLOCK), :]
+
+    for dz in range(2):
+        for entry in range(LINKS):
+            link_ref[entry, dz] = gathered(entry, dz)
+        for comp in range(24):
+            z_ref[0, comp, dz] = gathered(LINKS + comp, dz)
+            z_ref[1, comp, dz] = gathered(LINKS + 24 + comp, dz)
+        for i in range(24):
+            base_ref[i, dz] = gathered(LINKS + 48 + i, dz)
+
+    def hops(slot, dz, acc):
+        def link(direction, at):
+            return lambda part, a, b: link_ref[direction * 18 + part * 9 + a * 3 + b, at]
+
+        here = lambda comp: z_ref[slot, comp, dz]
+        there = lambda comp: z_ref[slot, comp, 1 - dz]
+        for direction, move in ((0, move_x), (1, move_y), (3, move_t)):
+            half = {k: move(h, 1) for k, h in half_spinor(here, direction, -1).items()}
+            acc = add_hop(acc, link_times(link(direction, dz), half, False), direction, -1)
+            half = link_times(link(direction, dz), half_spinor(here, direction, 1), True)
+            acc = add_hop(acc, {k: move(h, -1) for k, h in half.items()}, direction, 1)
+        half = half_spinor(there, 2, -1)
+        acc = add_hop(acc, link_times(link(2, dz), half, False), 2, -1)
+        half = link_times(link(2, 1 - dz), half_spinor(there, 2, 1), True)
+        return add_hop(acc, half, 2, 1)
+
+    def surface(k, carry):
+        for dz in range(2):
+            acc = [2.2 * z_ref[k, comp, dz] for comp in range(24)]
+            acc = hops(k, dz, acc)
+            for comp in range(24):
+                a_ref[k, comp, dz] = acc[comp]
+        return carry
+
+    lax.fori_loop(0, 2, surface, 0)
+    for i, comp in enumerate(LOWER):
+        for dz in range(2):
+            r_ref[0, comp, dz] = base_ref[i, dz] - a_ref[0, comp, dz]
+    for i, comp in enumerate(UPPER):
+        for dz in range(2):
+            r_ref[7, comp, dz] = base_ref[12 + i, dz] - a_ref[1, comp, dz]
+    for i in range(24):
+        out_ref[i] = zero
+
+    def step(iteration, carry):
+        def one(j, sums):
+            s = jnp.where(j <= iteration, j, 8 + iteration - j)
+            before = jnp.where(s == 0, 7, s - 1)
+            after = jnp.where(s == 7, 0, s + 1)
+            low = jnp.where(s == 0, -QUARK_MASS, 1.0).astype(jnp.float32)
+            high = jnp.where(s == 7, -QUARK_MASS, 1.0).astype(jnp.float32)
+            for dz in range(2):
+                for comp in range(24):
+                    chi = r_ref[before, comp, dz] * low if comp in UPPER else r_ref[after, comp, dz] * high
+                    z_ref[0, comp, dz] = INNER_SCALE * r_ref[s, comp, dz] + INNER_SHIFT * chi
+            real, imag, weight = sums
+            for dz in range(2):
+                acc = [6.0 * r_ref[s, comp, dz] - 1.8 * z_ref[0, comp, dz] for comp in range(24)]
+                acc = hops(0, dz, acc)
+                for i in range(12):
+                    ar, ai = (acc[i], acc[i + 12])
+                    rr, ri = (r_ref[s, i, dz], r_ref[s, i + 12, dz])
+                    real = real + ar * rr + ai * ri
+                    imag = imag + ar * ri - ai * rr
+                    weight = weight + ar * ar + ai * ai
+                for comp in range(24):
+                    a_ref[s, comp, dz] = acc[comp]
+            return (real, imag, weight)
+
+        count = 2 * (iteration + 1)
+        real, imag, weight = lax.fori_loop(0, count, one, (zero, zero, zero))
+        total = lambda x: jnp.sum(x, axis=(0, 1), keepdims=True)
+        scale = total(weight) + EPSILON
+        alpha_real = jnp.broadcast_to(total(real) / scale, (8, 128))
+        alpha_imag = jnp.broadcast_to(total(imag) / scale, (8, 128))
+        for slot, (s, comps) in enumerate(((0, LOWER), (7, UPPER))):
+            for i in range(6):
+                rr, ri = (r_ref[s, comps[i], 0], r_ref[s, comps[i + 6], 0])
+                at = slot * 12 + i
+                out_ref[at] = out_ref[at] + alpha_real * rr - alpha_imag * ri
+                out_ref[at + 6] = out_ref[at + 6] + alpha_real * ri + alpha_imag * rr
+
+        def update(j, c):
+            s = jnp.where(j <= iteration, j, 8 + iteration - j)
+            for dz in range(2):
+                for i in range(12):
+                    ar, ai = (a_ref[s, i, dz], a_ref[s, i + 12, dz])
+                    r_ref[s, i, dz] = r_ref[s, i, dz] - (alpha_real * ar - alpha_imag * ai)
+                    r_ref[s, i + 12, dz] = r_ref[s, i + 12, dz] - (alpha_real * ai + alpha_imag * ar)
+            return c
+
+        lax.fori_loop(0, jnp.where(iteration == ITERS - 1, 0, count), update, 0)
+        return carry
+
+    lax.fori_loop(0, ITERS, step, 0)
+
+
+def final_kernel(own_ref, acc_ref, gauge_ref, ta_ref, tb_ref, mz_ref, corr_ref, res_ref, cor_ref, tile_ref):
+    core = lax.axis_index("sa")
+    last_time = lax.axis_index("ta") == lax.axis_size("ta") - 1
+    time_scale = jnp.where(last_time, 0.5, -0.5).astype(jnp.float32)
+    scaled_links(gauge_ref, tile_ref, 0, 2, -0.5)
+    scaled_links(gauge_ref, tile_ref, 1, 3, time_scale)
+
+    def finish(up_ref, down_ref, offset):
+        def group(g, carry):
+            def rows(comp, start=0):
+                return pl.ds(pl.multiple_of(start + comp * ROWS + g * 8, 8), 8)
+
+            def half(ref, start):
+                return {
+                    (spin, part, color): ref[rows(part * 6 + spin * 3 + color, start), :]
+                    for spin in range(2)
+                    for part in range(2)
+                    for color in range(3)
+                }
+
+            acc = [acc_ref[rows(comp), :] for comp in range(24)]
+            acc = add_hop(acc, link_times(tile_link(tile_ref, 0), half(mz_ref, 0), False), 2, -1)
+            acc = add_hop(acc, half(mz_ref, 288), 2, 1)
+            acc = add_hop(acc, link_times(tile_link(tile_ref, 1), half(down_ref, offset), False), 3, -1)
+            acc = add_hop(acc, half(up_ref, offset), 3, 1)
+            for comp in range(24):
+                res_ref[rows(comp), :] = -acc[comp]
+            return carry
+
+        lax.fori_loop(0, 3, group, 0)
+
+    cor_ref[...] = own_ref[...]
+
+    def add_surface(s, comps, first):
+        for i, comp in enumerate(comps):
+            rows = slice(comp * ROWS + 2 * s, comp * ROWS + 2 * s + 2)
+            cor_ref[rows, :] = cor_ref[rows, :] + corr_ref[first + i, 0:2, :]
+
+    @pl.when(core == 0)
+    def _():
+        finish(ta_ref, tb_ref, 0)
+        add_surface(0, LOWER, 0)
+
+    @pl.when(core == 1)
+    def _():
+        finish(tb_ref, ta_ref, 288)
+        add_surface(11, UPPER, 12)
+
+
+def cost(flops, moved):
+    return pl.CostEstimate(flops=flops, bytes_accessed=moved, transcendentals=0)
+
+
+def call(kernel, outs, scratch, in_specs, flops, moved, *args):
+    shapes = [jax.ShapeDtypeStruct(s, jnp.float32) for s in outs]
+    return pl.pallas_call(
+        kernel,
+        out_shape=shapes,
+        in_specs=in_specs,
+        out_specs=[pl.BlockSpec(memory_space=pltpu.VMEM)] * len(outs),
+        scratch_shapes=scratch,
+        cost_estimate=cost(flops, moved),
+        compiler_params=pltpu.CompilerParams(vmem_limit_bytes=VMEM_LIMIT),
+    )(*args)
+
+
+def small_body(iterate, source, gauge_links):
+    whole = iterate.shape
+    own = iterate.reshape(FIELD, 128)
+    src = source.reshape(FIELD, 128)
+    gauge = gauge_links.reshape(2 * LINKS, 128)
+    swap = [(0, 1), (1, 0)]
+    oth = lax.ppermute(own, "sa", swap)
+    src_oth = lax.ppermute(src, "sa", swap)
+    vmem = pl.BlockSpec(memory_space=pltpu.VMEM)
+    anywhere = pl.BlockSpec(memory_space=pl.ANY)
+    f32 = jnp.float32
+    mt, mz, blk, bl = call(
+        send_kernel,
+        [(FIELD + MESSAGE, 128), (FIELD + MESSAGE, 128), (MESSAGE, 128), (FIELD, 128)],
+        [pltpu.VMEM((FIELD, 128), f32), pltpu.VMEM((36, 8, 128), f32)],
+        [vmem] * 5,
+        4_000_000,
+        3_000_000,
+        own, oth, src, src_oth, gauge,
+    )
+
+    def route(where):
+        pairs_out = []
+        for t in range(4):
+            for z in range(2):
+                for s in range(2):
+                    dt, dz = where(s)
+                    to = ((t + dt) % 4) * 4 + ((z + dz) % 2) * 2 + s
+                    pairs_out.append((t * 4 + z * 2 + s, to))
+        return pairs_out
+
+    axes = ("ta", "gz", "sa")
+    x1 = lax.ppermute(mt, axes, route(lambda s: (1, 0) if s == 0 else (-1, 0)))
+    x4 = lax.ppermute(blk, axes, route(lambda s: (1, 1) if s == 0 else (2, 1)))
+    x3 = lax.ppermute(blk, axes, route(lambda s: (2, 0) if s == 0 else (-1, 1)))
+    x2 = lax.ppermute(mz, axes, route(lambda s: (0, 1)))
+    x1b = lax.ppermute(x1, "sa", swap)
+    x3b = lax.ppermute(x3, "sa", swap)
+    x4b = lax.ppermute(x4, "sa", swap)
+    acc = call(
+        local_kernel,
+        [(FIELD, 128)],
+        [pltpu.VMEM((36, 8, 128), f32)],
+        [vmem] * 4,
+        4_000_000,
+        2_000_000,
+        own, bl, src, gauge,
+    )[0]
+    corr = call(
+        inner_kernel,
+        [(24, 8, 128)],
+        [
+            pltpu.VMEM((8 * MESSAGE, 128), f32),
+            pltpu.VMEM((LINKS, 2, 8, 128), f32),
+            pltpu.VMEM((24, 2, 8, 128), f32),
+            pltpu.VMEM((8, 24, 2, 8, 128), f32),
+            pltpu.VMEM((8, 24, 2, 8, 128), f32),
+            pltpu.VMEM((2, 24, 2, 8, 128), f32),
+            pltpu.SemaphoreType.DMA((8,)),
+        ],
+        [anywhere] * 8,
+        40_000_000,
+        2_000_000,
+        blk, x2, x1, x1b, x3, x3b, x4, x4b,
+    )[0]
+    residual, corrected = call(
+        final_kernel,
+        [(FIELD, 128), (FIELD, 128)],
+        [pltpu.VMEM((36, 8, 128), f32)],
+        [vmem] * 7,
+        4_000_000,
+        3_000_000,
+        own, acc, gauge, x1, x1b, x2, corr,
+    )
+    return (residual.reshape(whole), corrected.reshape(whole))
+
+
 def solution(mesh):
     placed = (
         P("parts", None, None, "sa", "ta", "gz", None),
         P("parts", None, None, "sa", "ta", "gz", None),
         P("parts", None, "ta", "gz", None),
     )
+    small = (mesh.shape["ta"], mesh.shape["gz"], mesh.shape["sa"]) == (4, 2, 2)
+
+    def chosen(iterate, source, gauge_links):
+        one_block = iterate.shape[3:] == (12, 1, 1, 256)
+        return (small_body if small and one_block else body)(iterate, source, gauge_links)
+
     return jax.shard_map(
-        body,
+        chosen,
         mesh=mesh,
         in_specs=placed,
         out_specs=(

time: 1100 us -> 47.2 us (0.04); the launches traced: 1090 us -> 47 us
  matrix products: 524 us -> 0 us
  local copies, waits for them, and re-layouts: 324 us -> 2.82 us
  other arithmetic: 102 us -> 0 us
  blocking collectives: 99.6 us -> 0 us
  waiting for transfers between devices: 0.07 us -> 20.7 us
  starting transfers between devices: 27.4 us -> 10.8 us
  Pallas kernels: 0 us -> 12 us
    dot_general x160 -> x0, matrix products: 524 us -> none  [the longest x128 494 us: contract(): return jnp.einsum(formula, matrix_part, spinor_part, precision=HIGHEST)]
    another operation x158 -> x0, local copies, waits for them, and re-layouts: 223 us -> none  [the longest x56 113 us: color_apply(): return jnp.stack([real_part, imag_part])]
    psum x3 -> x0, blocking collectives: 92.2 us -> none  [minimal_residual(): lax.psum((jnp.sum(applied[0] * remainder[0] + applied[1] * remainder[1]),...]
    slice x57 -> x0, local copies, waits for them, and re-layouts: 66.5 us -> none  [the longest x10 24.5 us: color_apply(): spinor[0]]
    another operation x35 -> x0, other arithmetic: 40.7 us -> none  [the longest x32 36.2 us: color_apply(): return jnp.stack([real_part, imag_part])]
    concatenate x31 -> x0, other arithmetic: 32.2 us -> none  [the longest x9 12.7 us: along_x(): return jnp.roll(lattice, -offset, axis=-1).reshape(spinor.shape)]
    ppermute x26 -> x9, waiting for transfers between devices: 0.07 us -> 20.7 us  [the longest x1 11.1 us: small_body(): x1 = lax.ppermute(mt, axes, route(lambda s: (1, 0) if s == 0 else (-1, 0)))]
    ppermute x26 -> x9, starting transfers between devices: 27.4 us -> 10.8 us  [the longest x1 3 us: small_body(): x1 = lax.ppermute(mt, axes, route(lambda s: (1, 0) if s == 0 else (-1, 0)))]
  transfers between devices with their start and end apart: 26 -> 9, of which waited for: 0 -> 6; matrix products, arithmetic and copies ran while one was open for 75% -> 0% of each run, Pallas kernels for 0% -> 1%
where the time goes in v1:
time: 47.2 us; the launch traced here: 47 us
  waiting for transfers between devices  20.7 us (44%)
  Pallas kernels  12 us (25%)
  starting transfers between devices  10.8 us (23%)
  local copies, waits for them, and re-layouts  2.82 us (6%)
  between operations  0.69 us (1%)
    pallas_call x4, Pallas kernels, call(): pl.pallas_call(kernel, out_shape=shapes, in_specs=in_specs, out_specs=[pl...  12 us
    ppermute x1, waiting for transfers between devices, small_body(): x1 = lax.ppermute(mt, axes, route(lambda s: (1, 0) if s == 0 else (-1, 0)))  11.1 us
    ppermute x1, waiting for transfers between devices, small_body(): x3 = lax.ppermute(blk, axes, route(lambda s: (2, 0) if s == 0 else (-1, 1)))  7.15 us
    ppermute x1, starting transfers between devices, small_body(): x1 = lax.ppermute(mt, axes, route(lambda s: (1, 0) if s == 0 else (-1, 0)))  3 us
    unnamed x12, local copies, waits for them, and re-layouts  2.82 us
    ppermute x1, starting transfers between devices, small_body(): x4 = lax.ppermute(blk, axes, route(lambda s: (1, 1) if s == 0 else (2, 1)))  2.5 us
    ppermute x1, starting transfers between devices, small_body(): x4b = lax.ppermute(x4, 'sa', swap)  1.73 us
    ppermute x1, starting transfers between devices, small_body(): x2 = lax.ppermute(mz, axes, route(lambda s: (0, 1)))  1.49 us
  transfers between devices with their start and end apart: 9, of which 6 were waited for; matrix products, arithmetic and copies ran while one was open for 0% of the time, Pallas kernels for 1%

profile of v1, /device:TPU:0, one launch (start us, length us, event | category | flops | bytes accessed | tf_op | source)
XLA Modules:
  0.0 47.0 jit_solution(12471556051022349574)
XLA Ops:
  0.6 0.5 %collective-permute-start = (f32[576,128]{1,0:T(8,128)}, f32[576,128]{1,0:T(8,128)S(1)}, u32[]{:S(2)}, u32[]{:S(2)}) collective-permute-start(f32[576,128]{1,0:T(8,128)} %bitcast.5), channel_id=1, source_target_pairs={{0,1},{1,0},{2,3},{3,2},{4,5},{5,4},{6,7},{7,6},{8,9},{9,8},{10,11... | collective-permute-start | bytes 884744 | tf_op jit(solution)/shard_map/ppermute | solution.py:680
  1.1 0.1 collective-permute-start.1
  1.2 1.3 %collective-permute-done.oth_ref = f32[576,128]{1,0:T(8,128)S(1)} collective-permute-done((f32[576,128]{1,0:T(8,128)}, f32[576,128]{1,0:T(8,128)S(1)}, u32[]{:S(2)}, u32[]{:S(2)}) %collective-permute-start) | collective-permute-done | bytes 294944 | tf_op jit(solution)/shard_map/ppermute | solution.py:680
  2.6 0.4 collective-permute-done.1.src_oth_ref
  3.0 0.0 copy-start
  3.0 1.0 %copy-done = f32[2,4,3,12,1,1,256]{6,5,4,3,2,1,0:T(1,128)S(1)} copy-done((f32[2,4,3,12,1,1,256]{6,5,4,3,2,1,0:T(1,128)S(1)}, f32[2,4,3,12,1,1,256]{6,5,4,3,2,1,0:T(1,128)}, u32[]{:S(2)}) %copy-start) | copy-done | bytes 294936
  4.0 0.0 copy-start.2
  4.0 1.0 %copy-done.2 = f32[2,4,3,12,1,1,256]{6,5,4,3,2,1,0:T(1,128)S(1)} copy-done((f32[2,4,3,12,1,1,256]{6,5,4,3,2,1,0:T(1,128)S(1)}, f32[2,4,3,12,1,1,256]{6,5,4,3,2,1,0:T(1,128)}, u32[]{:S(2)}) %copy-start.2) | copy-done | bytes 294936
  4.9 0.0 copy-start.4
  4.9 0.9 %copy-done.4 = f32[4,18,1,1,256]{4,3,2,1,0:T(1,128)S(1)} copy-done((f32[4,18,1,1,256]{4,3,2,1,0:T(1,128)S(1)}, f32[4,18,1,1,256]{4,3,2,1,0:T(1,128)}, u32[]{:S(2)}) %copy-start.4) | copy-done | bytes 73752
  5.8 0.0 copy-start.3
  5.8 0.0 copy-start.5
  5.8 0.4 shard_map.50
  6.2 3.0 %collective-permute-start.2 = (f32[864,128]{1,0:T(8,128)S(1)}, f32[864,128]{1,0:T(8,128)S(1)}, u32[]{:S(2)}, u32[]{:S(2)}) collective-permute-start(f32[864,128]{1,0:T(8,128)S(1)} %get-tuple-element.9), channel_id=1, source_target_pairs={{0,4},{1,13},{2,6},{3,15},{4,8},{5,1},{6,10},{7,3},{8,12},{9,5},{1... | collective-permute-start | bytes 1327112 | tf_op jit(solution)/shard_map/ppermute | solution.py:706
  9.2 1.5 %collective-permute-start.4 = (f32[864,128]{1,0:T(8,128)S(1)}, f32[864,128]{1,0:T(8,128)S(1)}, u32[]{:S(2)}, u32[]{:S(2)}) collective-permute-start(f32[864,128]{1,0:T(8,128)S(1)} %get-tuple-element.10), channel_id=1, source_target_pairs={{0,2},{1,3},{2,0},{3,1},{4,6},{5,7},{6,4},{7,5},{8,10},{9,11},{10,... | collective-permute-start | bytes 1327112 | tf_op jit(solution)/shard_map/ppermute | solution.py:709
  10.7 11.1 %collective-permute-done.2.x1a_ref.ta_ref = f32[864,128]{1,0:T(8,128)S(1)} collective-permute-done((f32[864,128]{1,0:T(8,128)S(1)}, f32[864,128]{1,0:T(8,128)S(1)}, u32[]{:S(2)}, u32[]{:S(2)}) %collective-permute-start.2) | collective-permute-done | bytes 442400 | tf_op jit(solution)/shard_map/ppermute | solution.py:706
  21.8 0.0 collective-permute-start.3
  21.8 1.5 %collective-permute-start.5 = (f32[288,128]{1,0:T(8,128)S(1)}, f32[288,128]{1,0:T(8,128)S(1)}, u32[]{:S(2)}, u32[]{:S(2)}) collective-permute-start(f32[288,128]{1,0:T(8,128)S(1)} %get-tuple-element.11.own_ref), channel_id=1, source_target_pairs={{0,8},{1,15},{2,10},{3,13},{4,12},{5,3},{6,14},{7,1},{8,0},{9,7},{... | collective-permute-start | bytes 442376 | tf_op jit(solution)/shard_map/ppermute | solution.py:708
  23.3 2.5 %collective-permute-start.7 = (f32[288,128]{1,0:T(8,128)S(1)}, f32[288,128]{1,0:T(8,128)S(1)}, u32[]{:S(2)}, u32[]{:S(2)}) collective-permute-start(f32[288,128]{1,0:T(8,128)S(1)} %get-tuple-element.11.own_ref), channel_id=1, source_target_pairs={{0,6},{1,11},{2,4},{3,9},{4,10},{5,15},{6,8},{7,13},{8,14},{9,3},{... | collective-permute-start | bytes 442376 | tf_op jit(solution)/shard_map/ppermute | solution.py:707
  25.8 7.1 %collective-permute-done.5.x3a_ref = f32[288,128]{1,0:T(8,128)S(1)} collective-permute-done((f32[288,128]{1,0:T(8,128)S(1)}, f32[288,128]{1,0:T(8,128)S(1)}, u32[]{:S(2)}, u32[]{:S(2)}) %collective-permute-start.5) | collective-permute-done | bytes 147488 | tf_op jit(solution)/shard_map/ppermute | solution.py:708
  32.9 0.0 collective-permute-start.6
  32.9 0.2 collective-permute-done.7.x4a_ref
  33.1 1.7 %collective-permute-start.8 = (f32[288,128]{1,0:T(8,128)S(1)}, f32[288,128]{1,0:T(8,128)S(1)}, u32[]{:S(2)}, u32[]{:S(2)}) collective-permute-start(f32[288,128]{1,0:T(8,128)S(1)} %collective-permute-done.7.x4a_ref), channel_id=1, source_target_pairs={{0,1},{1,0},{2,3},{3,2},{4,5},{5,4},{6,7},{7,6},{8,9},{9,8},{10,11... | collective-permute-start | bytes 442376 | tf_op jit(solution)/shard_map/ppermute | solution.py:712
  34.9 0.0 copy-done.3
  34.9 0.0 copy-done.5
  34.9 0.5 %shard_map.51.acc_ref = f32[576,128]{1,0:T(8,128)S(1)} custom-call(f32[576,128]{1,0:T(8,128)S(1)} %bitcast.7, f32[576,128]{1,0:T(8,128)S(1)} %get-tuple-element.8.bl_ref, f32[576,128]{1,0:T(8,128)S(1)} %bitcast.11, f32[144,128]{1,0:T(8,128)S(1)} %bitcast.13), custom_call_target="tpu_custom_call" | custom-call | flops 4000000 | bytes 2000000 | tf_op jit(solution)/shard_map/pallas_call | solution.py:663
  35.4 0.0 copy-start.1
  35.4 0.0 collective-permute-done.6.x3b_ref
  35.4 0.5 %collective-permute-done.8.x4b_ref = f32[288,128]{1,0:T(8,128)S(1)} collective-permute-done((f32[288,128]{1,0:T(8,128)S(1)}, f32[288,128]{1,0:T(8,128)S(1)}, u32[]{:S(2)}, u32[]{:S(2)}) %collective-permute-start.8) | collective-permute-done | bytes 147488 | tf_op jit(solution)/shard_map/ppermute | solution.py:712
  35.9 0.0 collective-permute-done.4.x2_ref.mz_ref
  35.9 0.0 collective-permute-done.3.x1b_ref.tb_ref
  35.9 10.1 %shard_map.52.corr_ref = f32[24,8,128]{2,1,0:T(8,128)S(1)} custom-call(f32[288,128]{1,0:T(8,128)S(1)} %get-tuple-element.11.own_ref, f32[864,128]{1,0:T(8,128)S(1)} %collective-permute-done.4.x2_ref.mz_ref, f32[864,128]{1,0:T(8,128)S(1)} %collective-permute-done.2.x1a_ref.ta_ref, f32[864,128]{1,0:T(8,128)S(1)} %collective-permute-done.3.x1b_ref.tb_ref, ...), custom_call_target="tpu_custom_call" | custom-call | flops 40000000 | bytes 2000000 | tf_op jit(solution)/shard_map/pallas_call | solution.py:663
  46.0 0.0 copy-done.1
  46.0 1.1 %shard_map.53 = (f32[576,128]{1,0:T(8,128)}, f32[576,128]{1,0:T(8,128)}) custom-call(f32[576,128]{1,0:T(8,128)S(1)} %bitcast.8, f32[576,128]{1,0:T(8,128)S(1)} %shard_map.51.acc_ref, f32[144,128]{1,0:T(8,128)S(1)} %bitcast.14, f32[864,128]{1,0:T(8,128)S(1)} %collective-permute-done.2.x1a_ref.ta_ref, f32[864,128]{1,0:T(8,128)S(1)} %collective-permute-done.3.x1b_ref.tb_ref, ...), custom_call_target="tpu_custom_call" | custom-call | flops 4000000 | bytes 3000000 | tf_op jit(solution)/shard_map/pallas_call | solution.py:663
Async XLA Ops:
  0.6 1.9 %collective-permute-start = (f32[576,128]{1,0:T(8,128)}, f32[576,128]{1,0:T(8,128)S(1)}, u32[]{:S(2)}, u32[]{:S(2)}) collective-permute-start(f32[576,128]{1,0:T(8,128)} %bitcast.5), channel_id=1, source_target_pairs={{0,1},{1,0},{2,3},{3,2},{4,5},{5,4},{6,7},{7,6},{8,9},{9,8},{10,11... | collective-permute-start | bytes 884744 | tf_op jit(solution)/shard_map/ppermute | solution.py:680
  1.1 1.8 %collective-permute-start.1 = (f32[576,128]{1,0:T(8,128)}, f32[576,128]{1,0:T(8,128)S(1)}, u32[]{:S(2)}, u32[]{:S(2)}) collective-permute-start(f32[576,128]{1,0:T(8,128)} %bitcast.9), channel_id=1, source_target_pairs={{0,1},{1,0},{2,3},{3,2},{4,5},{5,4},{6,7},{7,6},{8,9},{9,8},{10,11... | collective-permute-start | bytes 884744 | tf_op jit(solution)/shard_map/ppermute | solution.py:681
  3.0 1.0 %copy-start = (f32[2,4,3,12,1,1,256]{6,5,4,3,2,1,0:T(1,128)S(1)}, f32[2,4,3,12,1,1,256]{6,5,4,3,2,1,0:T(1,128)}, u32[]{:S(2)}) copy-start(f32[2,4,3,12,1,1,256]{6,5,4,3,2,1,0:T(1,128)} %param.3) | copy-start | bytes 884740
  4.0 1.0 %copy-start.2 = (f32[2,4,3,12,1,1,256]{6,5,4,3,2,1,0:T(1,128)S(1)}, f32[2,4,3,12,1,1,256]{6,5,4,3,2,1,0:T(1,128)}, u32[]{:S(2)}) copy-start(f32[2,4,3,12,1,1,256]{6,5,4,3,2,1,0:T(1,128)} %param.4) | copy-start | bytes 884740
  4.9 0.9 %copy-start.4 = (f32[4,18,1,1,256]{4,3,2,1,0:T(1,128)S(1)}, f32[4,18,1,1,256]{4,3,2,1,0:T(1,128)}, u32[]{:S(2)}) copy-start(f32[4,18,1,1,256]{4,3,2,1,0:T(1,128)} %param.5) | copy-start | bytes 221188
  5.8 29.1 %copy-start.3 = (f32[2,4,3,12,1,1,256]{6,5,4,3,2,1,0:T(1,128)S(1)}, f32[2,4,3,12,1,1,256]{6,5,4,3,2,1,0:T(1,128)}, u32[]{:S(2)}) copy-start(f32[2,4,3,12,1,1,256]{6,5,4,3,2,1,0:T(1,128)} %param.4) | copy-start | bytes 884740
  5.8 29.1 %copy-start.5 = (f32[4,18,1,1,256]{4,3,2,1,0:T(1,128)S(1)}, f32[4,18,1,1,256]{4,3,2,1,0:T(1,128)}, u32[]{:S(2)}) copy-start(f32[4,18,1,1,256]{4,3,2,1,0:T(1,128)} %param.5) | copy-start | bytes 221188
  6.2 15.6 %collective-permute-start.2 = (f32[864,128]{1,0:T(8,128)S(1)}, f32[864,128]{1,0:T(8,128)S(1)}, u32[]{:S(2)}, u32[]{:S(2)}) collective-permute-start(f32[864,128]{1,0:T(8,128)S(1)} %get-tuple-element.9), channel_id=1, source_target_pairs={{0,4},{1,13},{2,6},{3,15},{4,8},{5,1},{6,10},{7,3},{8,12},{9,5},{1... | collective-permute-start | bytes 1327112 | tf_op jit(solution)/shard_map/ppermute | solution.py:706
  9.2 26.7 %collective-permute-start.4 = (f32[864,128]{1,0:T(8,128)S(1)}, f32[864,128]{1,0:T(8,128)S(1)}, u32[]{:S(2)}, u32[]{:S(2)}) collective-permute-start(f32[864,128]{1,0:T(8,128)S(1)} %get-tuple-element.10), channel_id=1, source_target_pairs={{0,2},{1,3},{2,0},{3,1},{4,6},{5,7},{6,4},{7,5},{8,10},{9,11},{10,... | collective-permute-start | bytes 1327112 | tf_op jit(solution)/shard_map/ppermute | solution.py:709
  21.8 14.1 %collective-permute-start.3 = (f32[864,128]{1,0:T(8,128)S(1)}, f32[864,128]{1,0:T(8,128)S(1)}, u32[]{:S(2)}, u32[]{:S(2)}) collective-permute-start(f32[864,128]{1,0:T(8,128)S(1)} %collective-permute-done.2.x1a_ref.ta_ref), channel_id=1, source_target_pairs={{0,1},{1,0},{2,3},{3,2},{4,5},{5,4},{6,7},{7,6},{8,9},{9,8},{10,11... | collective-permute-start | bytes 1327112 | tf_op jit(solution)/shard_map/ppermute | solution.py:710
  21.8 11.1 %collective-permute-start.5 = (f32[288,128]{1,0:T(8,128)S(1)}, f32[288,128]{1,0:T(8,128)S(1)}, u32[]{:S(2)}, u32[]{:S(2)}) collective-permute-start(f32[288,128]{1,0:T(8,128)S(1)} %get-tuple-element.11.own_ref), channel_id=1, source_target_pairs={{0,8},{1,15},{2,10},{3,13},{4,12},{5,3},{6,14},{7,1},{8,0},{9,7},{... | collective-permute-start | bytes 442376 | tf_op jit(solution)/shard_map/ppermute | solution.py:708
  23.3 9.9 %collective-permute-start.7 = (f32[288,128]{1,0:T(8,128)S(1)}, f32[288,128]{1,0:T(8,128)S(1)}, u32[]{:S(2)}, u32[]{:S(2)}) collective-permute-start(f32[288,128]{1,0:T(8,128)S(1)} %get-tuple-element.11.own_ref), channel_id=1, source_target_pairs={{0,6},{1,11},{2,4},{3,9},{4,10},{5,15},{6,8},{7,13},{8,14},{9,3},{... | collective-permute-start | bytes 442376 | tf_op jit(solution)/shard_map/ppermute | solution.py:707
  32.9 2.5 %collective-permute-start.6 = (f32[288,128]{1,0:T(8,128)S(1)}, f32[288,128]{1,0:T(8,128)S(1)}, u32[]{:S(2)}, u32[]{:S(2)}) collective-permute-start(f32[288,128]{1,0:T(8,128)S(1)} %collective-permute-done.5.x3a_ref), channel_id=1, source_target_pairs={{0,1},{1,0},{2,3},{3,2},{4,5},{5,4},{6,7},{7,6},{8,9},{9,8},{10,11... | collective-permute-start | bytes 442376 | tf_op jit(solution)/shard_map/ppermute | solution.py:711
  33.1 2.7 %collective-permute-start.8 = (f32[288,128]{1,0:T(8,128)S(1)}, f32[288,128]{1,0:T(8,128)S(1)}, u32[]{:S(2)}, u32[]{:S(2)}) collective-permute-start(f32[288,128]{1,0:T(8,128)S(1)} %collective-permute-done.7.x4a_ref), channel_id=1, source_target_pairs={{0,1},{1,0},{2,3},{3,2},{4,5},{5,4},{6,7},{7,6},{8,9},{9,8},{10,11... | collective-permute-start | bytes 442376 | tf_op jit(solution)/shard_map/ppermute | solution.py:712
  35.4 10.6 %copy-start.1 = (f32[2,4,3,12,1,1,256]{6,5,4,3,2,1,0:T(1,128)S(1)}, f32[2,4,3,12,1,1,256]{6,5,4,3,2,1,0:T(1,128)}, u32[]{:S(2)}) copy-start(f32[2,4,3,12,1,1,256]{6,5,4,3,2,1,0:T(1,128)} %param.3) | copy-start | bytes 884740

commit v2 on v1

--- a/solution.py
+++ b/solution.py
@@ -277,7 +277,8 @@
 ROWS = 24
 FIELD = 576
 LINKS = 72
-BLOCK = 144
+SENT = 48
+BLOCK = SENT + 72
 MESSAGE = 2 * BLOCK
 VMEM_LIMIT = 48 * 1024 * 1024
 
@@ -386,6 +387,15 @@
         out_ref[rows, :] = OUTER_SCALE * v + OUTER_SHIFT * chi
 
 
+def stage_kernel(own_ref, src_ref, gauge_ref, own_out, src_out, gauge_out, sem):
+    copies = []
+    for i, (ref, out) in enumerate(((own_ref, own_out), (src_ref, src_out), (gauge_ref, gauge_out))):
+        copies.append(pltpu.make_async_copy(ref, out, sem.at[i]))
+        copies[-1].start()
+    for copy in copies:
+        copy.wait()
+
+
 def send_kernel(own_ref, oth_ref, src_own_ref, src_oth_ref, gauge_ref, mt_ref, mz_ref, blk_ref, bl_ref, blo_ref, tile_ref):
     core = lax.axis_index("sa")
     last_time = lax.axis_index("ta") == lax.axis_size("ta") - 1
@@ -395,15 +405,14 @@
     blend_rows(bl_ref, own_ref, oth_ref, first, last)
     blend_rows(blo_ref, oth_ref, own_ref, last, first)
 
-    sign_row = lax.broadcasted_iota(jnp.int32, (LINKS, 128), 0) >= 54
-    link_sign = jnp.where(jnp.logical_and(sign_row, last_time), 0.5, -0.5).astype(jnp.float32)
     for h in range(2):
-        base = h * BLOCK
-        blk_ref[base : base + LINKS, :] = gauge_ref[pl.ds(h, LINKS, stride=2), :] * link_sign
+        for i in range(8):
+            base = h * BLOCK + i * 6
+            blk_ref[base : base + 6, :] = gauge_ref[pl.ds(i * 18 + h, 6, stride=2), :]
 
     def surfaces(bl0_ref, it0_ref, src0_ref, bl1_ref, it1_ref, src1_ref):
         for h in range(2):
-            base = h * BLOCK + LINKS
+            base = h * BLOCK + SENT
             blk_ref[base : base + 24, :] = bl0_ref[pl.ds(h, 24, stride=ROWS), :]
             blk_ref[base + 24 : base + 48, :] = bl1_ref[pl.ds(22 + h, 24, stride=ROWS), :]
             for part in range(2):
@@ -453,18 +462,28 @@
 
     pl.when(core == 0)(lambda: time_up(bl_ref, blo_ref))
     pl.when(core == 1)(lambda: time_down(blo_ref, bl_ref))
-    mt_ref[FIELD : FIELD + MESSAGE, :] = blk_ref[...]
-    mz_ref[FIELD : FIELD + MESSAGE, :] = blk_ref[...]
-
-
-def local_kernel(own_ref, bl_ref, src_ref, gauge_ref, acc_ref, tile_ref):
-    scaled_links(gauge_ref, tile_ref, 0, 0, -0.5)
-    scaled_links(gauge_ref, tile_ref, 1, 1, -0.5)
+
+
+def halves(ref, rows, start):
+    return {
+        (spin, part, color): ref[rows(part * 6 + spin * 3 + color, start), :]
+        for spin in range(2)
+        for part in range(2)
+        for color in range(3)
+    }
+
+
+def group_rows(g):
+    return lambda comp, start=0: pl.ds(pl.multiple_of(start + comp * ROWS + g * 8, 8), 8)
+
+
+def local_kernel(own_ref, bl_ref, src_ref, gauge_ref, mz_ref, corr_ref, acc_ref, cor_ref, tile_ref):
+    core = lax.axis_index("sa")
+    for direction in range(3):
+        scaled_links(gauge_ref, tile_ref, direction, direction, -0.5)
 
     def group(g, carry):
-        def rows(comp):
-            return pl.ds(pl.multiple_of(comp * ROWS + g * 8, 8), 8)
-
+        rows = group_rows(g)
         get = lambda comp: bl_ref[rows(comp), :]
         acc = [0.2 * get(comp) + 4.0 * own_ref[rows(comp), :] - src_ref[rows(comp), :] for comp in range(24)]
         for direction, move in ((0, move_x), (1, move_y)):
@@ -473,11 +492,22 @@
             acc = add_hop(acc, link_times(link, half, False), direction, -1)
             half = link_times(link, half_spinor(get, direction, 1), True)
             acc = add_hop(acc, {k: move(h, -1) for k, h in half.items()}, direction, 1)
+        acc = add_hop(acc, link_times(tile_link(tile_ref, 2), halves(mz_ref, rows, 0), False), 2, -1)
+        acc = add_hop(acc, halves(mz_ref, rows, 288), 2, 1)
         for comp in range(24):
             acc_ref[rows(comp), :] = acc[comp]
         return carry
 
     lax.fori_loop(0, 3, group, 0)
+    cor_ref[...] = own_ref[...]
+
+    def add_surface(s, comps, first):
+        for i, comp in enumerate(comps):
+            at = slice(comp * ROWS + 2 * s, comp * ROWS + 2 * s + 2)
+            cor_ref[at, :] = cor_ref[at, :] + corr_ref[first + i, 0:2, :]
+
+    pl.when(core == 0)(lambda: add_surface(0, LOWER, 0))
+    pl.when(core == 1)(lambda: add_surface(11, UPPER, 12))
 
 
 def inner_kernel(own_ref, x2_ref, x1a_ref, x1b_ref, x3a_ref, x3b_ref, x4a_ref, x4b_ref, out_ref, gather_ref, link_ref, base_ref, r_ref, a_ref, z_ref, sem):
@@ -485,9 +515,9 @@
     pick = lambda zero, one: jnp.where(core == 0, zero, one)
     placed = (
         (own_ref, 0, 0),
-        (x2_ref, FIELD, 4),
-        (x1a_ref, FIELD, pick(3, 1)),
-        (x1b_ref, FIELD, pick(1, 3)),
+        (x2_ref, 0, 4),
+        (x1a_ref, 0, pick(3, 1)),
+        (x1b_ref, 0, pick(1, 3)),
         (x3a_ref, 0, pick(2, 5)),
         (x3b_ref, 0, pick(5, 2)),
         (x4a_ref, 0, pick(7, 6)),
@@ -506,17 +536,41 @@
     for copy in copies:
         copy.wait()
 
+    time = lax.rem(lax.axis_index("ta") + sublane() // 2, 4)
+    time_scale = jnp.where(time == 3, 0.5, -0.5).astype(jnp.float32)
+
     def gathered(comp, dz):
         return gather_ref[pl.ds(dz * 8 * BLOCK + comp, 8, stride=BLOCK), :]
 
     for dz in range(2):
-        for entry in range(LINKS):
-            link_ref[entry, dz] = gathered(entry, dz)
+        for direction in range(4):
+            scale = time_scale if direction == 3 else -0.5
+            for part in range(2):
+                for i in range(6):
+                    entry = gathered(direction * 12 + part * 6 + i, dz) * (scale if i < 3 else 1.0)
+                    link_ref[direction * 18 + part * 9 + i, dz] = entry
+            for b in range(3):
+                p, q = ((b + 1) % 3, (b + 2) % 3)
+                row = lambda part, a, at: link_ref[direction * 18 + part * 9 + a * 3 + at, dz]
+                real = (
+                    row(RE, 0, p) * row(RE, 1, q) - row(IM, 0, p) * row(IM, 1, q)
+                    - row(RE, 0, q) * row(RE, 1, p) + row(IM, 0, q) * row(IM, 1, p)
+                )
+                imag = (
+                    row(RE, 0, q) * row(IM, 1, p) + row(IM, 0, q) * row(RE, 1, p)
+                    - row(RE, 0, p) * row(IM, 1, q) - row(IM, 0, p) * row(RE, 1, q)
+                )
+                link_ref[direction * 18 + 6 + b, dz] = real
+                link_ref[direction * 18 + 15 + b, dz] = imag
+            for part in range(2):
+                for b in range(3):
+                    at = direction * 18 + part * 9 + 3 + b
+                    link_ref[at, dz] = link_ref[at, dz] * scale
         for comp in range(24):
-            z_ref[0, comp, dz] = gathered(LINKS + comp, dz)
-            z_ref[1, comp, dz] = gathered(LINKS + 24 + comp, dz)
+            z_ref[0, comp, dz] = gathered(SENT + comp, dz)
+            z_ref[1, comp, dz] = gathered(SENT + 24 + comp, dz)
         for i in range(24):
-            base_ref[i, dz] = gathered(LINKS + 48 + i, dz)
+            base_ref[i, dz] = gathered(SENT + 48 + i, dz)
 
     def hops(slot, dz, acc):
         def link(direction, at):
@@ -605,60 +659,32 @@
     lax.fori_loop(0, ITERS, step, 0)
 
 
-def final_kernel(own_ref, acc_ref, gauge_ref, ta_ref, tb_ref, mz_ref, corr_ref, res_ref, cor_ref, tile_ref):
+def final_kernel(acc_ref, gauge_ref, ta_ref, tb_ref, res_ref, tile_ref):
     core = lax.axis_index("sa")
     last_time = lax.axis_index("ta") == lax.axis_size("ta") - 1
-    time_scale = jnp.where(last_time, 0.5, -0.5).astype(jnp.float32)
-    scaled_links(gauge_ref, tile_ref, 0, 2, -0.5)
-    scaled_links(gauge_ref, tile_ref, 1, 3, time_scale)
+    scaled_links(gauge_ref, tile_ref, 0, 3, jnp.where(last_time, 0.5, -0.5).astype(jnp.float32))
 
     def finish(up_ref, down_ref, offset):
         def group(g, carry):
-            def rows(comp, start=0):
-                return pl.ds(pl.multiple_of(start + comp * ROWS + g * 8, 8), 8)
-
-            def half(ref, start):
-                return {
-                    (spin, part, color): ref[rows(part * 6 + spin * 3 + color, start), :]
-                    for spin in range(2)
-                    for part in range(2)
-                    for color in range(3)
-                }
-
+            rows = group_rows(g)
             acc = [acc_ref[rows(comp), :] for comp in range(24)]
-            acc = add_hop(acc, link_times(tile_link(tile_ref, 0), half(mz_ref, 0), False), 2, -1)
-            acc = add_hop(acc, half(mz_ref, 288), 2, 1)
-            acc = add_hop(acc, link_times(tile_link(tile_ref, 1), half(down_ref, offset), False), 3, -1)
-            acc = add_hop(acc, half(up_ref, offset), 3, 1)
+            acc = add_hop(acc, link_times(tile_link(tile_ref, 0), halves(down_ref, rows, offset), False), 3, -1)
+            acc = add_hop(acc, halves(up_ref, rows, offset), 3, 1)
             for comp in range(24):
                 res_ref[rows(comp), :] = -acc[comp]
             return carry
 
         lax.fori_loop(0, 3, group, 0)
 
-    cor_ref[...] = own_ref[...]
-
-    def add_surface(s, comps, first):
-        for i, comp in enumerate(comps):
-            rows = slice(comp * ROWS + 2 * s, comp * ROWS + 2 * s + 2)
-            cor_ref[rows, :] = cor_ref[rows, :] + corr_ref[first + i, 0:2, :]
-
-    @pl.when(core == 0)
-    def _():
-        finish(ta_ref, tb_ref, 0)
-        add_surface(0, LOWER, 0)
-
-    @pl.when(core == 1)
-    def _():
-        finish(tb_ref, ta_ref, 288)
-        add_surface(11, UPPER, 12)
+    pl.when(core == 0)(lambda: finish(ta_ref, tb_ref, 0))
+    pl.when(core == 1)(lambda: finish(tb_ref, ta_ref, 288))
 
 
 def cost(flops, moved):
     return pl.CostEstimate(flops=flops, bytes_accessed=moved, transcendentals=0)
 
 
-def call(kernel, outs, scratch, in_specs, flops, moved, *args):
+def call(kernel, outs, scratch, in_specs, flops, moved, *args, limit=VMEM_LIMIT):
     shapes = [jax.ShapeDtypeStruct(s, jnp.float32) for s in outs]
     return pl.pallas_call(
         kernel,
@@ -667,7 +693,7 @@
         out_specs=[pl.BlockSpec(memory_space=pltpu.VMEM)] * len(outs),
         scratch_shapes=scratch,
         cost_estimate=cost(flops, moved),
-        compiler_params=pltpu.CompilerParams(vmem_limit_bytes=VMEM_LIMIT),
+        compiler_params=pltpu.CompilerParams(vmem_limit_bytes=limit),
     )(*args)
 
 
@@ -682,9 +708,18 @@
     vmem = pl.BlockSpec(memory_space=pltpu.VMEM)
     anywhere = pl.BlockSpec(memory_space=pl.ANY)
     f32 = jnp.float32
+    own, src, gauge = call(
+        stage_kernel,
+        [(FIELD, 128), (FIELD, 128), (2 * LINKS, 128)],
+        [pltpu.SemaphoreType.DMA((3,))],
+        [pl.BlockSpec(memory_space=pltpu.HBM)] * 3,
+        0,
+        1_300_000,
+        own, src, gauge,
+    )
     mt, mz, blk, bl = call(
         send_kernel,
-        [(FIELD + MESSAGE, 128), (FIELD + MESSAGE, 128), (MESSAGE, 128), (FIELD, 128)],
+        [(FIELD, 128), (FIELD, 128), (MESSAGE, 128), (FIELD, 128)],
         [pltpu.VMEM((FIELD, 128), f32), pltpu.VMEM((36, 8, 128), f32)],
         [vmem] * 5,
         4_000_000,
@@ -703,22 +738,16 @@
         return pairs_out
 
     axes = ("ta", "gz", "sa")
-    x1 = lax.ppermute(mt, axes, route(lambda s: (1, 0) if s == 0 else (-1, 0)))
     x4 = lax.ppermute(blk, axes, route(lambda s: (1, 1) if s == 0 else (2, 1)))
     x3 = lax.ppermute(blk, axes, route(lambda s: (2, 0) if s == 0 else (-1, 1)))
-    x2 = lax.ppermute(mz, axes, route(lambda s: (0, 1)))
+    x1 = lax.ppermute(blk, axes, route(lambda s: (1, 0) if s == 0 else (-1, 0)))
+    x2 = lax.ppermute(blk, axes, route(lambda s: (0, 1)))
+    x1, x2, x3, x4, mt, mz = lax.optimization_barrier((x1, x2, x3, x4, mt, mz))
+    ta = lax.ppermute(mt, axes, route(lambda s: (1, 0) if s == 0 else (-1, 0)))
+    tz = lax.ppermute(mz, axes, route(lambda s: (0, 1)))
     x1b = lax.ppermute(x1, "sa", swap)
     x3b = lax.ppermute(x3, "sa", swap)
     x4b = lax.ppermute(x4, "sa", swap)
-    acc = call(
-        local_kernel,
-        [(FIELD, 128)],
-        [pltpu.VMEM((36, 8, 128), f32)],
-        [vmem] * 4,
-        4_000_000,
-        2_000_000,
-        own, bl, src, gauge,
-    )[0]
     corr = call(
         inner_kernel,
         [(24, 8, 128)],
@@ -736,15 +765,26 @@
         2_000_000,
         blk, x2, x1, x1b, x3, x3b, x4, x4b,
     )[0]
-    residual, corrected = call(
+    ta, tz, corr = lax.optimization_barrier((ta, tz, corr))
+    tb = lax.ppermute(ta, "sa", swap)
+    acc, corrected = call(
+        local_kernel,
+        [(FIELD, 128), (FIELD, 128)],
+        [pltpu.VMEM((54, 8, 128), f32)],
+        [vmem] * 6,
+        6_000_000,
+        3_000_000,
+        own, bl, src, gauge, tz, corr,
+    )
+    residual = call(
         final_kernel,
-        [(FIELD, 128), (FIELD, 128)],
-        [pltpu.VMEM((36, 8, 128), f32)],
-        [vmem] * 7,
-        4_000_000,
-        3_000_000,
-        own, acc, gauge, x1, x1b, x2, corr,
-    )
+        [(FIELD, 128)],
+        [pltpu.VMEM((18, 8, 128), f32)],
+        [vmem] * 4,
+        2_000_000,
+        2_000_000,
+        acc, gauge, ta, tb,
+    )[0]
     return (residual.reshape(whole), corrected.reshape(whole))
 
 

time: 47.2 us -> 36.8 us (0.78)
  waiting for transfers between devices: 20.7 us -> 8.78 us
  starting transfers between devices: 10.8 us -> 11.9 us
    ppermute x2 -> x5, waiting for transfers between devices: 11.1 us -> 0.01 us  [the longest x1 0.01 us: small_body(): x2 = lax.ppermute(blk, axes, route(lambda s: (0, 1)))]
    ppermute x1, waiting for transfers between devices: 0.2 us -> 2.98 us  [small_body(): x4 = lax.ppermute(blk, axes, route(lambda s: (1, 1) if s == 0 else (2, 1)))]
    ppermute x1, waiting for transfers between devices: 7.15 us -> 4.78 us  [small_body(): x3 = lax.ppermute(blk, axes, route(lambda s: (2, 0) if s == 0 else (-1, 1)))]
    ppermute x1, starting transfers between devices: 2.5 us -> 3.98 us  [small_body(): x4 = lax.ppermute(blk, axes, route(lambda s: (1, 1) if s == 0 else (2, 1)))]
    ppermute x1, waiting for transfers between devices: 1.34 us -> 0.01 us  [small_body(): oth = lax.ppermute(own, 'sa', swap)]
    ppermute x1, starting transfers between devices: 1.73 us -> 0.45 us  [small_body(): x4b = lax.ppermute(x4, 'sa', swap)]
    ppermute x1, starting transfers between devices: 1.49 us -> 2.59 us  [small_body(): x3 = lax.ppermute(blk, axes, route(lambda s: (2, 0) if s == 0 else (-1, 1)))]
    ppermute x2 -> x5, starting transfers between devices: 4.49 us -> 3.73 us  [the longest x1 2.16 us: small_body(): ta = lax.ppermute(mt, axes, route(lambda s: (1, 0) if s == 0 else (-1, 0)))]
  transfers between devices with their start and end apart: 9 -> 12, of which waited for: 6 -> 5; matrix products, arithmetic and copies ran while one was open for 0% -> 0% of each run, Pallas kernels for 1% -> 31%
where the time goes in v2:
time: 36.8 us; the launch traced here: 36.5 us
  Pallas kernels  12.4 us (34%)
  starting transfers between devices  11.9 us (32%)
  waiting for transfers between devices  8.78 us (24%)
  local copies, waits for them, and re-layouts  2.81 us (8%)
  between operations  0.7 us (2%)
    pallas_call x5, Pallas kernels, call(): pl.pallas_call(kernel, out_shape=shapes, in_specs=in_specs, out_specs=[pl...  12.4 us
    ppermute x1, waiting for transfers between devices, small_body(): x3 = lax.ppermute(blk, axes, route(lambda s: (2, 0) if s == 0 else (-1, 1)))  4.78 us
    ppermute x1, starting transfers between devices, small_body(): x4 = lax.ppermute(blk, axes, route(lambda s: (1, 1) if s == 0 else (2, 1)))  3.98 us
    ppermute x1, waiting for transfers between devices, small_body(): x4 = lax.ppermute(blk, axes, route(lambda s: (1, 1) if s == 0 else (2, 1)))  2.98 us
    unnamed x6, local copies, waits for them, and re-layouts  2.81 us
    ppermute x1, starting transfers between devices, small_body(): x3 = lax.ppermute(blk, axes, route(lambda s: (2, 0) if s == 0 else (-1, 1)))  2.59 us
    ppermute x1, starting transfers between devices, small_body(): ta = lax.ppermute(mt, axes, route(lambda s: (1, 0) if s == 0 else (-1, 0)))  2.16 us
  transfers between devices with their start and end apart: 12, of which 5 were waited for; matrix products, arithmetic and copies ran while one was open for 0% of the time, Pallas kernels for 31%

profile of v2, /device:TPU:0, one launch (start us, length us, event | category | flops | bytes accessed | tf_op | source)
XLA Modules:
  0.0 36.5 jit_solution(2382977913466185908)
XLA Ops:
  0.6 0.5 %collective-permute-start = (f32[576,128]{1,0:T(8,128)}, f32[576,128]{1,0:T(8,128)S(1)}, u32[]{:S(2)}, u32[]{:S(2)}) collective-permute-start(f32[576,128]{1,0:T(8,128)} %bitcast.5), channel_id=1, source_target_pairs={{0,1},{1,0},{2,3},{3,2},{4,5},{5,4},{6,7},{7,6},{8,9},{9,8},{10,11... | collective-permute-start | bytes 884744 | tf_op jit(solution)/shard_map/ppermute | solution.py:706
  1.1 0.1 collective-permute-start.1
  1.2 0.0 copy-start
  1.2 1.0 %copy-done = f32[2,4,3,12,1,1,256]{6,5,4,3,2,1,0:T(1,128)S(1)} copy-done((f32[2,4,3,12,1,1,256]{6,5,4,3,2,1,0:T(1,128)S(1)}, f32[2,4,3,12,1,1,256]{6,5,4,3,2,1,0:T(1,128)}, u32[]{:S(2)}) %copy-start) | copy-done | bytes 294936
  2.2 0.0 copy-start.1
  2.2 1.0 %copy-done.1 = f32[2,4,3,12,1,1,256]{6,5,4,3,2,1,0:T(1,128)S(1)} copy-done((f32[2,4,3,12,1,1,256]{6,5,4,3,2,1,0:T(1,128)S(1)}, f32[2,4,3,12,1,1,256]{6,5,4,3,2,1,0:T(1,128)}, u32[]{:S(2)}) %copy-start.1) | copy-done | bytes 294936
  3.2 0.0 copy-start.2
  3.2 0.9 %copy-done.2 = f32[4,18,1,1,256]{4,3,2,1,0:T(1,128)S(1)} copy-done((f32[4,18,1,1,256]{4,3,2,1,0:T(1,128)S(1)}, f32[4,18,1,1,256]{4,3,2,1,0:T(1,128)}, u32[]{:S(2)}) %copy-start.2) | copy-done | bytes 73752
  4.0 0.2 shard_map.50
  4.3 0.0 collective-permute-done.oth_ref
  4.3 0.0 collective-permute-done.1.src_oth_ref
  4.3 0.4 %shard_map.51 = (f32[576,128]{1,0:T(8,128)S(1)}, f32[576,128]{1,0:T(8,128)S(1)}, f32[240,128]{1,0:T(8,128)S(1)}, f32[576,128]{1,0:T(8,128)S(1)}) custom-call(f32[576,128]{1,0:T(8,128)S(1)} %get-tuple-element.20.own_ref, f32[576,128]{1,0:T(8,128)S(1)} %collective-permute-done.oth_ref, f32[576,128]{1,0:T(8,128)S(1)} %get-tuple-element.21.src_own_ref.src_ref, ...), custom_call_target="tpu_custom_call" | custom-call | flops 4000000 | bytes 3000000 | tf_op jit(solution)/shard_map/pallas_call | solution.py:689
  4.7 4.0 %collective-permute-start.5 = (f32[240,128]{1,0:T(8,128)S(1)}, f32[240,128]{1,0:T(8,128)S(1)}, u32[]{:S(2)}, u32[]{:S(2)}) collective-permute-start(f32[240,128]{1,0:T(8,128)S(1)} %get-tuple-element.24.own_ref), channel_id=1, source_target_pairs={{0,6},{1,11},{2,4},{3,9},{4,10},{5,15},{6,8},{7,13},{8,14},{9,3},{... | collective-permute-start | bytes 368648 | tf_op jit(solution)/shard_map/ppermute | solution.py:741
  8.7 2.6 %collective-permute-start.4 = (f32[240,128]{1,0:T(8,128)S(1)}, f32[240,128]{1,0:T(8,128)S(1)}, u32[]{:S(2)}, u32[]{:S(2)}) collective-permute-start(f32[240,128]{1,0:T(8,128)S(1)} %get-tuple-element.24.own_ref), channel_id=1, source_target_pairs={{0,8},{1,15},{2,10},{3,13},{4,12},{5,3},{6,14},{7,1},{8,0},{9,7},{... | collective-permute-start | bytes 368648 | tf_op jit(solution)/shard_map/ppermute | solution.py:742
  11.3 0.5 %collective-permute-start.3 = (f32[240,128]{1,0:T(8,128)S(1)}, f32[240,128]{1,0:T(8,128)S(1)}, u32[]{:S(2)}, u32[]{:S(2)}) collective-permute-start(f32[240,128]{1,0:T(8,128)S(1)} %get-tuple-element.24.own_ref), channel_id=1, source_target_pairs={{0,2},{1,3},{2,0},{3,1},{4,6},{5,7},{6,4},{7,5},{8,10},{9,11},{10,... | collective-permute-start | bytes 368648 | tf_op jit(solution)/shard_map/ppermute | solution.py:744
  11.8 0.1 collective-permute-start.2
  11.9 3.0 %collective-permute-done.5.x4a_ref = f32[240,128]{1,0:T(8,128)S(1)} collective-permute-done((f32[240,128]{1,0:T(8,128)S(1)}, f32[240,128]{1,0:T(8,128)S(1)}, u32[]{:S(2)}, u32[]{:S(2)}) %collective-permute-start.5) | collective-permute-done | bytes 122912 | tf_op jit(solution)/shard_map/ppermute | solution.py:741
  14.9 4.8 %collective-permute-done.4.x3a_ref = f32[240,128]{1,0:T(8,128)S(1)} collective-permute-done((f32[240,128]{1,0:T(8,128)S(1)}, f32[240,128]{1,0:T(8,128)S(1)}, u32[]{:S(2)}, u32[]{:S(2)}) %collective-permute-start.4) | collective-permute-done | bytes 122912 | tf_op jit(solution)/shard_map/ppermute | solution.py:742
  19.7 0.0 collective-permute-done.3.x2_ref
  19.7 0.0 collective-permute-done.2.x1a_ref
  19.7 2.2 %collective-permute-start.6 = (f32[576,128]{1,0:T(8,128)S(1)}, f32[576,128]{1,0:T(8,128)S(1)}, u32[]{:S(2)}, u32[]{:S(2)}) collective-permute-start(f32[576,128]{1,0:T(8,128)S(1)} %get-tuple-element.27), channel_id=1, source_target_pairs={{0,4},{1,13},{2,6},{3,15},{4,8},{5,1},{6,10},{7,3},{8,12},{9,5},{1... | collective-permute-start | bytes 884744 | tf_op jit(solution)/shard_map/ppermute | solution.py:746
  21.8 0.5 %collective-permute-start.7 = (f32[576,128]{1,0:T(8,128)S(1)}, f32[576,128]{1,0:T(8,128)S(1)}, u32[]{:S(2)}, u32[]{:S(2)}) collective-permute-start(f32[576,128]{1,0:T(8,128)S(1)} %get-tuple-element.28), channel_id=1, source_target_pairs={{0,2},{1,3},{2,0},{3,1},{4,6},{5,7},{6,4},{7,5},{8,10},{9,11},{10,... | collective-permute-start | bytes 884744 | tf_op jit(solution)/shard_map/ppermute | solution.py:747
  22.4 0.5 %collective-permute-start.8 = (f32[240,128]{1,0:T(8,128)S(1)}, f32[240,128]{1,0:T(8,128)S(1)}, u32[]{:S(2)}, u32[]{:S(2)}) collective-permute-start(f32[240,128]{1,0:T(8,128)S(1)} %collective-permute-done.2.x1a_ref), channel_id=1, source_target_pairs={{0,1},{1,0},{2,3},{3,2},{4,5},{5,4},{6,7},{7,6},{8,9},{9,8},{10,11... | collective-permute-start | bytes 368648 | tf_op jit(solution)/shard_map/ppermute | solution.py:748
  22.8 0.1 collective-permute-start.9
  22.9 0.5 %collective-permute-start.10 = (f32[240,128]{1,0:T(8,128)S(1)}, f32[240,128]{1,0:T(8,128)S(1)}, u32[]{:S(2)}, u32[]{:S(2)}) collective-permute-start(f32[240,128]{1,0:T(8,128)S(1)} %collective-permute-done.5.x4a_ref), channel_id=1, source_target_pairs={{0,1},{1,0},{2,3},{3,2},{4,5},{5,4},{6,7},{7,6},{8,9},{9,8},{10,11... | collective-permute-start | bytes 368648 | tf_op jit(solution)/shard_map/ppermute | solution.py:750
  23.3 0.5 %collective-permute-done.8.x1b_ref = f32[240,128]{1,0:T(8,128)S(1)} collective-permute-done((f32[240,128]{1,0:T(8,128)S(1)}, f32[240,128]{1,0:T(8,128)S(1)}, u32[]{:S(2)}, u32[]{:S(2)}) %collective-permute-start.8) | collective-permute-done | bytes 122912 | tf_op jit(solution)/shard_map/ppermute | solution.py:748
  23.8 0.4 collective-permute-done.9.x3b_ref
  24.2 0.2 collective-permute-done.10.x4b_ref
  24.3 9.6 %shard_map.52.corr_ref = f32[24,8,128]{2,1,0:T(8,128)S(1)} custom-call(f32[240,128]{1,0:T(8,128)S(1)} %get-tuple-element.24.own_ref, f32[240,128]{1,0:T(8,128)S(1)} %collective-permute-done.3.x2_ref, f32[240,128]{1,0:T(8,128)S(1)} %collective-permute-done.2.x1a_ref, f32[240,128]{1,0:T(8,128)S(1)} %collective-permute-done.8.x1b_ref, ...), custom_call_target="tpu_custom_call" | custom-call | flops 40000000 | bytes 2000000 | tf_op jit(solution)/shard_map/pallas_call | solution.py:689
  34.0 0.0 collective-permute-done.6.ta_ref
  34.0 0.0 collective-permute-done.7.mz_ref
  34.0 0.4 %collective-permute-start.11 = (f32[576,128]{1,0:T(8,128)S(1)}, f32[576,128]{1,0:T(8,128)S(1)}, u32[]{:S(2)}, u32[]{:S(2)}) collective-permute-start(f32[576,128]{1,0:T(8,128)S(1)} %collective-permute-done.6.ta_ref), channel_id=1, source_target_pairs={{0,1},{1,0},{2,3},{3,2},{4,5},{5,4},{6,7},{7,6},{8,9},{9,8},{10,11... | collective-permute-start | bytes 884744 | tf_op jit(solution)/shard_map/ppermute | solution.py:769
  34.4 1.3 %shard_map.53 = (f32[576,128]{1,0:T(8,128)S(1)}, f32[576,128]{1,0:T(8,128)}) custom-call(f32[576,128]{1,0:T(8,128)S(1)} %get-tuple-element.20.own_ref, f32[576,128]{1,0:T(8,128)S(1)} %get-tuple-element.23.bl_ref, f32[576,128]{1,0:T(8,128)S(1)} %get-tuple-element.21.src_own_ref.src_ref, f32[144,128]{1,0:T(8,128)S(1)} %get-tuple-element.22.gauge_ref, ...), custom_call_target="tpu_custom_call" | custom-call | flops 6000000 | bytes 3000000 | tf_op jit(solution)/shard_map/pallas_call | solution.py:689
  35.7 0.0 collective-permute-done.11.tb_ref
  35.7 0.8 %shard_map.54 = f32[576,128]{1,0:T(8,128)} custom-call(f32[576,128]{1,0:T(8,128)S(1)} %get-tuple-element.35.acc_ref, f32[144,128]{1,0:T(8,128)S(1)} %get-tuple-element.22.gauge_ref, f32[576,128]{1,0:T(8,128)S(1)} %collective-permute-done.6.ta_ref, f32[576,128]{1,0:T(8,128)S(1)} %collective-permute-done.11.tb_ref), custom_call_target="tpu_custom_call" | custom-call | flops 2000000 | bytes 2000000 | tf_op jit(solution)/shard_map/pallas_call | solution.py:689
Async XLA Ops:
  0.6 3.7 %collective-permute-start = (f32[576,128]{1,0:T(8,128)}, f32[576,128]{1,0:T(8,128)S(1)}, u32[]{:S(2)}, u32[]{:S(2)}) collective-permute-start(f32[576,128]{1,0:T(8,128)} %bitcast.5), channel_id=1, source_target_pairs={{0,1},{1,0},{2,3},{3,2},{4,5},{5,4},{6,7},{7,6},{8,9},{9,8},{10,11... | collective-permute-start | bytes 884744 | tf_op jit(solution)/shard_map/ppermute | solution.py:706
  1.1 3.1 %collective-permute-start.1 = (f32[576,128]{1,0:T(8,128)}, f32[576,128]{1,0:T(8,128)S(1)}, u32[]{:S(2)}, u32[]{:S(2)}) collective-permute-start(f32[576,128]{1,0:T(8,128)} %bitcast.7), channel_id=1, source_target_pairs={{0,1},{1,0},{2,3},{3,2},{4,5},{5,4},{6,7},{7,6},{8,9},{9,8},{10,11... | collective-permute-start | bytes 884744 | tf_op jit(solution)/shard_map/ppermute | solution.py:707
  1.2 1.0 %copy-start = (f32[2,4,3,12,1,1,256]{6,5,4,3,2,1,0:T(1,128)S(1)}, f32[2,4,3,12,1,1,256]{6,5,4,3,2,1,0:T(1,128)}, u32[]{:S(2)}) copy-start(f32[2,4,3,12,1,1,256]{6,5,4,3,2,1,0:T(1,128)} %param.3) | copy-start | bytes 884740
  2.2 1.0 %copy-start.1 = (f32[2,4,3,12,1,1,256]{6,5,4,3,2,1,0:T(1,128)S(1)}, f32[2,4,3,12,1,1,256]{6,5,4,3,2,1,0:T(1,128)}, u32[]{:S(2)}) copy-start(f32[2,4,3,12,1,1,256]{6,5,4,3,2,1,0:T(1,128)} %param.4) | copy-start | bytes 884740
  3.2 0.9 %copy-start.2 = (f32[4,18,1,1,256]{4,3,2,1,0:T(1,128)S(1)}, f32[4,18,1,1,256]{4,3,2,1,0:T(1,128)}, u32[]{:S(2)}) copy-start(f32[4,18,1,1,256]{4,3,2,1,0:T(1,128)} %param.5) | copy-start | bytes 221188
  4.7 10.2 %collective-permute-start.5 = (f32[240,128]{1,0:T(8,128)S(1)}, f32[240,128]{1,0:T(8,128)S(1)}, u32[]{:S(2)}, u32[]{:S(2)}) collective-permute-start(f32[240,128]{1,0:T(8,128)S(1)} %get-tuple-element.24.own_ref), channel_id=1, source_target_pairs={{0,6},{1,11},{2,4},{3,9},{4,10},{5,15},{6,8},{7,13},{8,14},{9,3},{... | collective-permute-start | bytes 368648 | tf_op jit(solution)/shard_map/ppermute | solution.py:741
  8.7 11.0 %collective-permute-start.4 = (f32[240,128]{1,0:T(8,128)S(1)}, f32[240,128]{1,0:T(8,128)S(1)}, u32[]{:S(2)}, u32[]{:S(2)}) collective-permute-start(f32[240,128]{1,0:T(8,128)S(1)} %get-tuple-element.24.own_ref), channel_id=1, source_target_pairs={{0,8},{1,15},{2,10},{3,13},{4,12},{5,3},{6,14},{7,1},{8,0},{9,7},{... | collective-permute-start | bytes 368648 | tf_op jit(solution)/shard_map/ppermute | solution.py:742
  11.3 8.4 %collective-permute-start.3 = (f32[240,128]{1,0:T(8,128)S(1)}, f32[240,128]{1,0:T(8,128)S(1)}, u32[]{:S(2)}, u32[]{:S(2)}) collective-permute-start(f32[240,128]{1,0:T(8,128)S(1)} %get-tuple-element.24.own_ref), channel_id=1, source_target_pairs={{0,2},{1,3},{2,0},{3,1},{4,6},{5,7},{6,4},{7,5},{8,10},{9,11},{10,... | collective-permute-start | bytes 368648 | tf_op jit(solution)/shard_map/ppermute | solution.py:744
  11.8 7.9 %collective-permute-start.2 = (f32[240,128]{1,0:T(8,128)S(1)}, f32[240,128]{1,0:T(8,128)S(1)}, u32[]{:S(2)}, u32[]{:S(2)}) collective-permute-start(f32[240,128]{1,0:T(8,128)S(1)} %get-tuple-element.24.own_ref), channel_id=1, source_target_pairs={{0,4},{1,13},{2,6},{3,15},{4,8},{5,1},{6,10},{7,3},{8,12},{9,5},{1... | collective-permute-start | bytes 368648 | tf_op jit(solution)/shard_map/ppermute | solution.py:743
  19.7 14.3 %collective-permute-start.6 = (f32[576,128]{1,0:T(8,128)S(1)}, f32[576,128]{1,0:T(8,128)S(1)}, u32[]{:S(2)}, u32[]{:S(2)}) collective-permute-start(f32[576,128]{1,0:T(8,128)S(1)} %get-tuple-element.27), channel_id=1, source_target_pairs={{0,4},{1,13},{2,6},{3,15},{4,8},{5,1},{6,10},{7,3},{8,12},{9,5},{1... | collective-permute-start | bytes 884744 | tf_op jit(solution)/shard_map/ppermute | solution.py:746
  21.8 12.2 %collective-permute-start.7 = (f32[576,128]{1,0:T(8,128)S(1)}, f32[576,128]{1,0:T(8,128)S(1)}, u32[]{:S(2)}, u32[]{:S(2)}) collective-permute-start(f32[576,128]{1,0:T(8,128)S(1)} %get-tuple-element.28), channel_id=1, source_target_pairs={{0,2},{1,3},{2,0},{3,1},{4,6},{5,7},{6,4},{7,5},{8,10},{9,11},{10,... | collective-permute-start | bytes 884744 | tf_op jit(solution)/shard_map/ppermute | solution.py:747
  22.4 1.4 %collective-permute-start.8 = (f32[240,128]{1,0:T(8,128)S(1)}, f32[240,128]{1,0:T(8,128)S(1)}, u32[]{:S(2)}, u32[]{:S(2)}) collective-permute-start(f32[240,128]{1,0:T(8,128)S(1)} %collective-permute-done.2.x1a_ref), channel_id=1, source_target_pairs={{0,1},{1,0},{2,3},{3,2},{4,5},{5,4},{6,7},{7,6},{8,9},{9,8},{10,11... | collective-permute-start | bytes 368648 | tf_op jit(solution)/shard_map/ppermute | solution.py:748
  22.8 1.3 %collective-permute-start.9 = (f32[240,128]{1,0:T(8,128)S(1)}, f32[240,128]{1,0:T(8,128)S(1)}, u32[]{:S(2)}, u32[]{:S(2)}) collective-permute-start(f32[240,128]{1,0:T(8,128)S(1)} %collective-permute-done.4.x3a_ref), channel_id=1, source_target_pairs={{0,1},{1,0},{2,3},{3,2},{4,5},{5,4},{6,7},{7,6},{8,9},{9,8},{10,11... | collective-permute-start | bytes 368648 | tf_op jit(solution)/shard_map/ppermute | solution.py:749
  22.9 1.5 %collective-permute-start.10 = (f32[240,128]{1,0:T(8,128)S(1)}, f32[240,128]{1,0:T(8,128)S(1)}, u32[]{:S(2)}, u32[]{:S(2)}) collective-permute-start(f32[240,128]{1,0:T(8,128)S(1)} %collective-permute-done.5.x4a_ref), channel_id=1, source_target_pairs={{0,1},{1,0},{2,3},{3,2},{4,5},{5,4},{6,7},{7,6},{8,9},{9,8},{10,11... | collective-permute-start | bytes 368648 | tf_op jit(solution)/shard_map/ppermute | solution.py:750
  34.0 1.7 %collective-permute-start.11 = (f32[576,128]{1,0:T(8,128)S(1)}, f32[576,128]{1,0:T(8,128)S(1)}, u32[]{:S(2)}, u32[]{:S(2)}) collective-permute-start(f32[576,128]{1,0:T(8,128)S(1)} %collective-permute-done.6.ta_ref), channel_id=1, source_target_pairs={{0,1},{1,0},{2,3},{3,2},{4,5},{5,4},{6,7},{7,6},{8,9},{9,8},{10,11... | collective-permute-start | bytes 884744 | tf_op jit(solution)/shard_map/ppermute | solution.py:769

commit v3 on v2

--- a/solution.py
+++ b/solution.py
@@ -280,6 +280,11 @@
 SENT = 48
 BLOCK = SENT + 72
 MESSAGE = 2 * BLOCK
+WHOLE = 6.0
+LINK_SCALE = -0.5 * INNER_SCALE / WHOLE
+MIXED = -1.8 * INNER_SCALE / WHOLE
+MIXED_FIRST = 2.2 * INNER_SCALE / WHOLE - 1.0
+CHI = INNER_SHIFT / INNER_SCALE
 VMEM_LIMIT = 48 * 1024 * 1024
 
 
@@ -319,6 +324,28 @@
     return out
 
 
+def link_times_3(link, half, dagger):
+    mixed = {}
+    for spin in range(2):
+        for col in range(3):
+            real, imag = (half[spin, RE, col], half[spin, IM, col])
+            lead, less = (imag, real - imag) if dagger else (real, imag - real)
+            mixed[spin, col] = (lead, less, real + imag)
+    out = {}
+    for row in range(3):
+        for spin in range(2):
+            sums = None
+            for col in range(3):
+                a, b = (col, row) if dagger else (row, col)
+                lead, less, both = mixed[spin, col]
+                products = (lead * link(2, a, b), less * link(RE, a, b), both * link(IM, a, b))
+                sums = products if sums is None else tuple(p + q for p, q in zip(sums, products))
+            first, second, third = sums
+            out[spin, RE, row] = first + second if dagger else first - third
+            out[spin, IM, row] = first - third if dagger else first + second
+    return out
+
+
 def add_hop(acc, half, direction, side):
     flip = 1 if direction == 3 else -1
     for spin in range(2):
@@ -346,13 +373,13 @@
 
 
 def move_x(x, offset):
-    edge = lane() % NX == (NX - 1 if offset > 0 else 0)
-    return jnp.where(edge, roll(x, offset * (NX - 1), 1), roll(x, -offset, 1))
+    at = lane()
+    return jnp.take_along_axis(x, at - at % NX + (at + offset + NX) % NX, axis=1)
 
 
 def move_y(x, offset):
     near = roll(x, -offset * NX, 1)
-    far = jnp.where(sublane() % 2 == 0, roll(near, -1, 0), roll(near, 1, 0))
+    far = jnp.take_along_axis(near, sublane() + 1 - 2 * (sublane() % 2), axis=0)
     edge = lane() // NX == (3 if offset > 0 else 0)
     return jnp.where(edge, far, near)
 
@@ -369,6 +396,12 @@
     for entry in range(18):
         row = (direction * 18 + entry) * 2
         tile_ref[slot * 18 + entry] = pairs(gauge_ref[row : row + 2, :]) * scale
+
+
+def tree_sum(terms):
+    while len(terms) > 1:
+        terms = [a + b for a, b in zip(terms[::2], terms[1::2])] + terms[len(terms) // 2 * 2 :]
+    return terms[0]
 
 
 def tile_link(tile_ref, slot):
@@ -477,10 +510,9 @@
     return lambda comp, start=0: pl.ds(pl.multiple_of(start + comp * ROWS + g * 8, 8), 8)
 
 
-def local_kernel(own_ref, bl_ref, src_ref, gauge_ref, mz_ref, corr_ref, acc_ref, cor_ref, tile_ref):
-    core = lax.axis_index("sa")
-    for direction in range(3):
-        scaled_links(gauge_ref, tile_ref, direction, direction, -0.5)
+def local_kernel(own_ref, bl_ref, src_ref, gauge_ref, acc_ref, tile_ref):
+    scaled_links(gauge_ref, tile_ref, 0, 0, -0.5)
+    scaled_links(gauge_ref, tile_ref, 1, 1, -0.5)
 
     def group(g, carry):
         rows = group_rows(g)
@@ -492,7 +524,21 @@
             acc = add_hop(acc, link_times(link, half, False), direction, -1)
             half = link_times(link, half_spinor(get, direction, 1), True)
             acc = add_hop(acc, {k: move(h, -1) for k, h in half.items()}, direction, 1)
-        acc = add_hop(acc, link_times(tile_link(tile_ref, 2), halves(mz_ref, rows, 0), False), 2, -1)
+        for comp in range(24):
+            acc_ref[rows(comp), :] = acc[comp]
+        return carry
+
+    lax.fori_loop(0, 3, group, 0)
+
+
+def surface_kernel(own_ref, acc_in, gauge_ref, mz_ref, corr_ref, acc_ref, cor_ref, tile_ref):
+    core = lax.axis_index("sa")
+    scaled_links(gauge_ref, tile_ref, 0, 2, -0.5)
+
+    def group(g, carry):
+        rows = group_rows(g)
+        acc = [acc_in[rows(comp), :] for comp in range(24)]
+        acc = add_hop(acc, link_times(tile_link(tile_ref, 0), halves(mz_ref, rows, 0), False), 2, -1)
         acc = add_hop(acc, halves(mz_ref, rows, 288), 2, 1)
         for comp in range(24):
             acc_ref[rows(comp), :] = acc[comp]
@@ -510,26 +556,26 @@
     pl.when(core == 1)(lambda: add_surface(11, UPPER, 12))
 
 
-def inner_kernel(own_ref, x2_ref, x1a_ref, x1b_ref, x3a_ref, x3b_ref, x4a_ref, x4b_ref, out_ref, gather_ref, link_ref, base_ref, r_ref, a_ref, z_ref, sem):
+def inner_kernel(own_ref, xd_ref, xa_ref, xa2_ref, xb_ref, xb2_ref, xc_ref, xc2_ref, out_ref, gather_ref, link_ref, base_ref, r_ref, a_ref, z_ref, sem):
     core = lax.axis_index("sa")
     pick = lambda zero, one: jnp.where(core == 0, zero, one)
     placed = (
-        (own_ref, 0, 0),
-        (x2_ref, 0, 4),
-        (x1a_ref, 0, pick(3, 1)),
-        (x1b_ref, 0, pick(1, 3)),
-        (x3a_ref, 0, pick(2, 5)),
-        (x3b_ref, 0, pick(5, 2)),
-        (x4a_ref, 0, pick(7, 6)),
-        (x4b_ref, 0, pick(6, 7)),
+        (own_ref, 0),
+        (xd_ref, 4),
+        (xa_ref, pick(3, 7)),
+        (xa2_ref, pick(7, 3)),
+        (xb_ref, pick(1, 5)),
+        (xb2_ref, pick(5, 1)),
+        (xc_ref, pick(2, 6)),
+        (xc2_ref, pick(6, 2)),
     )
     copies = []
-    for i, (ref, start, slot) in enumerate(placed):
+    for i, (ref, slot) in enumerate(placed):
         to = gather_ref.at[pl.ds(pl.multiple_of(slot * MESSAGE, 8), MESSAGE), :]
-        copies.append(pltpu.make_async_copy(ref.at[pl.ds(start, MESSAGE), :], to, sem.at[i]))
+        copies.append(pltpu.make_async_copy(ref, to, sem.at[i]))
         copies[-1].start()
     zero = jnp.zeros((8, 128), jnp.float32)
-    for s in range(8):
+    for s in range(1, 7):
         for comp in range(24):
             for dz in range(2):
                 r_ref[s, comp, dz] = zero
@@ -537,126 +583,130 @@
         copy.wait()
 
     time = lax.rem(lax.axis_index("ta") + sublane() // 2, 4)
-    time_scale = jnp.where(time == 3, 0.5, -0.5).astype(jnp.float32)
+    time_scale = jnp.where(time == 3, -LINK_SCALE, LINK_SCALE).astype(jnp.float32)
 
     def gathered(comp, dz):
         return gather_ref[pl.ds(dz * 8 * BLOCK + comp, 8, stride=BLOCK), :]
 
     for dz in range(2):
         for direction in range(4):
-            scale = time_scale if direction == 3 else -0.5
-            for part in range(2):
-                for i in range(6):
-                    entry = gathered(direction * 12 + part * 6 + i, dz) * (scale if i < 3 else 1.0)
-                    link_ref[direction * 18 + part * 9 + i, dz] = entry
+            scale = time_scale if direction == 3 else LINK_SCALE
+            entry = lambda part, a, b: gathered(direction * 12 + part * 6 + a * 3 + b, dz)
+            rows = {(part, a, b): entry(part, a, b) for part in range(2) for a in range(2) for b in range(3)}
             for b in range(3):
                 p, q = ((b + 1) % 3, (b + 2) % 3)
-                row = lambda part, a, at: link_ref[direction * 18 + part * 9 + a * 3 + at, dz]
-                real = (
-                    row(RE, 0, p) * row(RE, 1, q) - row(IM, 0, p) * row(IM, 1, q)
-                    - row(RE, 0, q) * row(RE, 1, p) + row(IM, 0, q) * row(IM, 1, p)
+                rows[RE, 2, b] = (
+                    rows[RE, 0, p] * rows[RE, 1, q] - rows[IM, 0, p] * rows[IM, 1, q]
+                    - rows[RE, 0, q] * rows[RE, 1, p] + rows[IM, 0, q] * rows[IM, 1, p]
                 )
-                imag = (
-                    row(RE, 0, q) * row(IM, 1, p) + row(IM, 0, q) * row(RE, 1, p)
-                    - row(RE, 0, p) * row(IM, 1, q) - row(IM, 0, p) * row(RE, 1, q)
+                rows[IM, 2, b] = (
+                    rows[RE, 0, q] * rows[IM, 1, p] + rows[IM, 0, q] * rows[RE, 1, p]
+                    - rows[RE, 0, p] * rows[IM, 1, q] - rows[IM, 0, p] * rows[RE, 1, q]
                 )
-                link_ref[direction * 18 + 6 + b, dz] = real
-                link_ref[direction * 18 + 15 + b, dz] = imag
-            for part in range(2):
+            for a in range(3):
                 for b in range(3):
-                    at = direction * 18 + part * 9 + 3 + b
-                    link_ref[at, dz] = link_ref[at, dz] * scale
+                    real, imag = (rows[RE, a, b] * scale, rows[IM, a, b] * scale)
+                    at = direction * 27 + a * 3 + b
+                    link_ref[at, dz] = real
+                    link_ref[at + 9, dz] = imag
+                    link_ref[at + 18, dz] = real + imag
         for comp in range(24):
-            z_ref[0, comp, dz] = gathered(SENT + comp, dz)
-            z_ref[1, comp, dz] = gathered(SENT + 24 + comp, dz)
+            r_ref[0, comp, dz] = gathered(SENT + comp, dz) * (1.0 / INNER_SCALE)
+            r_ref[7, comp, dz] = gathered(SENT + 24 + comp, dz) * (1.0 / INNER_SCALE)
         for i in range(24):
             base_ref[i, dz] = gathered(SENT + 48 + i, dz)
 
     def hops(slot, dz, acc):
         def link(direction, at):
-            return lambda part, a, b: link_ref[direction * 18 + part * 9 + a * 3 + b, at]
+            return lambda part, a, b: link_ref[direction * 27 + part * 9 + a * 3 + b, at]
 
         here = lambda comp: z_ref[slot, comp, dz]
         there = lambda comp: z_ref[slot, comp, 1 - dz]
         for direction, move in ((0, move_x), (1, move_y), (3, move_t)):
             half = {k: move(h, 1) for k, h in half_spinor(here, direction, -1).items()}
-            acc = add_hop(acc, link_times(link(direction, dz), half, False), direction, -1)
-            half = link_times(link(direction, dz), half_spinor(here, direction, 1), True)
+            acc = add_hop(acc, link_times_3(link(direction, dz), half, False), direction, -1)
+            half = link_times_3(link(direction, dz), half_spinor(here, direction, 1), True)
             acc = add_hop(acc, {k: move(h, -1) for k, h in half.items()}, direction, 1)
         half = half_spinor(there, 2, -1)
-        acc = add_hop(acc, link_times(link(2, dz), half, False), 2, -1)
-        half = link_times(link(2, 1 - dz), half_spinor(there, 2, 1), True)
+        acc = add_hop(acc, link_times_3(link(2, dz), half, False), 2, -1)
+        half = link_times_3(link(2, 1 - dz), half_spinor(there, 2, 1), True)
         return add_hop(acc, half, 2, 1)
 
-    def surface(k, carry):
-        for dz in range(2):
-            acc = [2.2 * z_ref[k, comp, dz] for comp in range(24)]
-            acc = hops(k, dz, acc)
-            for comp in range(24):
-                a_ref[k, comp, dz] = acc[comp]
-        return carry
-
-    lax.fori_loop(0, 2, surface, 0)
-    for i, comp in enumerate(LOWER):
-        for dz in range(2):
-            r_ref[0, comp, dz] = base_ref[i, dz] - a_ref[0, comp, dz]
-    for i, comp in enumerate(UPPER):
-        for dz in range(2):
-            r_ref[7, comp, dz] = base_ref[12 + i, dz] - a_ref[1, comp, dz]
     for i in range(24):
         out_ref[i] = zero
 
-    def step(iteration, carry):
-        def one(j, sums):
-            s = jnp.where(j <= iteration, j, 8 + iteration - j)
-            before = jnp.where(s == 0, 7, s - 1)
-            after = jnp.where(s == 7, 0, s + 1)
-            low = jnp.where(s == 0, -QUARK_MASS, 1.0).astype(jnp.float32)
-            high = jnp.where(s == 7, -QUARK_MASS, 1.0).astype(jnp.float32)
-            for dz in range(2):
-                for comp in range(24):
-                    chi = r_ref[before, comp, dz] * low if comp in UPPER else r_ref[after, comp, dz] * high
-                    z_ref[0, comp, dz] = INNER_SCALE * r_ref[s, comp, dz] + INNER_SHIFT * chi
-            real, imag, weight = sums
-            for dz in range(2):
-                acc = [6.0 * r_ref[s, comp, dz] - 1.8 * z_ref[0, comp, dz] for comp in range(24)]
-                acc = hops(0, dz, acc)
-                for i in range(12):
-                    ar, ai = (acc[i], acc[i + 12])
-                    rr, ri = (r_ref[s, i, dz], r_ref[s, i + 12, dz])
-                    real = real + ar * rr + ai * ri
-                    imag = imag + ar * ri - ai * rr
-                    weight = weight + ar * ar + ai * ai
-                for comp in range(24):
-                    a_ref[s, comp, dz] = acc[comp]
-            return (real, imag, weight)
-
-        count = 2 * (iteration + 1)
-        real, imag, weight = lax.fori_loop(0, count, one, (zero, zero, zero))
-        total = lambda x: jnp.sum(x, axis=(0, 1), keepdims=True)
-        scale = total(weight) + EPSILON
-        alpha_real = jnp.broadcast_to(total(real) / scale, (8, 128))
-        alpha_imag = jnp.broadcast_to(total(imag) / scale, (8, 128))
-        for slot, (s, comps) in enumerate(((0, LOWER), (7, UPPER))):
-            for i in range(6):
-                rr, ri = (r_ref[s, comps[i], 0], r_ref[s, comps[i + 6], 0])
-                at = slot * 12 + i
-                out_ref[at] = out_ref[at] + alpha_real * rr - alpha_imag * ri
-                out_ref[at + 6] = out_ref[at + 6] + alpha_real * ri + alpha_imag * rr
-
-        def update(j, c):
-            s = jnp.where(j <= iteration, j, 8 + iteration - j)
+    def stage(at, carry):
+        first = at == 0
+        number_f32 = lambda zero, other: jnp.where(first, zero, other).astype(jnp.float32)
+        mixed_share = number_f32(MIXED_FIRST, MIXED)
+        wall, shift = (number_f32(0.0, -QUARK_MASS * CHI), number_f32(0.0, CHI))
+        count = jnp.where(first, 1, at)
+
+        def pair(j, sums):
+            low_end = jnp.where(j == 0, wall, shift)
+            sides = (
+                (j, jnp.where(j == 0, 7, j - 1), j + 1, low_end, shift),
+                (7 - j, 6 - j, jnp.where(j == 0, 0, 8 - j), shift, low_end),
+            )
+            for slot, (s, before, after, low, high) in enumerate(sides):
+                for dz in range(2):
+                    for comp in range(24):
+                        chi = r_ref[before, comp, dz] * low if comp in UPPER else r_ref[after, comp, dz] * high
+                        z_ref[slot, comp, dz] = r_ref[s, comp, dz] + chi
+            for slot, (s, before, after, low, high) in enumerate(sides):
+                for dz in range(2):
+                    acc = [r_ref[s, comp, dz] + mixed_share * z_ref[slot, comp, dz] for comp in range(24)]
+                    acc = hops(slot, dz, acc)
+                    terms = ([], [], [])
+                    for i in range(12):
+                        ar, ai = (acc[i], acc[i + 12])
+                        rr, ri = (r_ref[s, i, dz], r_ref[s, i + 12, dz])
+                        terms[0].append(ar * rr + ai * ri)
+                        terms[1].append(ar * ri - ai * rr)
+                        terms[2].append(ar * ar + ai * ai)
+                    sums = tuple(total + tree_sum(part) for total, part in zip(sums, terms))
+                    for comp in range(24):
+                        a_ref[s, comp, dz] = acc[comp]
+            return sums
+
+        real, imag, weight = lax.fori_loop(0, count, pair, (zero, zero, zero))
+
+        @pl.when(first)
+        def _():
             for dz in range(2):
                 for i in range(12):
-                    ar, ai = (a_ref[s, i, dz], a_ref[s, i + 12, dz])
-                    r_ref[s, i, dz] = r_ref[s, i, dz] - (alpha_real * ar - alpha_imag * ai)
-                    r_ref[s, i + 12, dz] = r_ref[s, i + 12, dz] - (alpha_real * ai + alpha_imag * ar)
-            return c
-
-        lax.fori_loop(0, jnp.where(iteration == ITERS - 1, 0, count), update, 0)
+                    r_ref[0, LOWER[i], dz] = base_ref[i, dz] - WHOLE * a_ref[0, LOWER[i], dz]
+                    r_ref[0, UPPER[i], dz] = zero
+                    r_ref[7, UPPER[i], dz] = base_ref[12 + i, dz] - WHOLE * a_ref[7, UPPER[i], dz]
+                    r_ref[7, LOWER[i], dz] = zero
+
+        @pl.when(at > 0)
+        def _():
+            total = lambda x: jnp.sum(x, axis=(0, 1), keepdims=True)
+            scale = total(weight) + EPSILON / WHOLE**2
+            alpha_real = jnp.broadcast_to(total(real) / scale, (8, 128))
+            alpha_imag = jnp.broadcast_to(total(imag) / scale, (8, 128))
+            for slot, (s, comps) in enumerate(((0, LOWER), (7, UPPER))):
+                for i in range(6):
+                    rr, ri = (r_ref[s, comps[i], 0], r_ref[s, comps[i + 6], 0])
+                    to = slot * 12 + i
+                    out_ref[to] = out_ref[to] + (alpha_real * rr - alpha_imag * ri) * (1.0 / WHOLE)
+                    out_ref[to + 6] = out_ref[to + 6] + (alpha_real * ri + alpha_imag * rr) * (1.0 / WHOLE)
+
+            def update(j, c):
+                for s in (j, 7 - j):
+                    for dz in range(2):
+                        for i in range(12):
+                            ar, ai = (a_ref[s, i, dz], a_ref[s, i + 12, dz])
+                            r_ref[s, i, dz] = r_ref[s, i, dz] - (alpha_real * ar - alpha_imag * ai)
+                            r_ref[s, i + 12, dz] = r_ref[s, i + 12, dz] - (alpha_real * ai + alpha_imag * ar)
+                return c
+
+            lax.fori_loop(0, jnp.where(at == ITERS, 0, count), update, 0)
+
         return carry
 
-    lax.fori_loop(0, ITERS, step, 0)
+    lax.fori_loop(0, ITERS + 1, stage, 0)
 
 
 def final_kernel(acc_ref, gauge_ref, ta_ref, tb_ref, res_ref, tile_ref):
@@ -715,7 +765,7 @@
         [pl.BlockSpec(memory_space=pltpu.HBM)] * 3,
         0,
         1_300_000,
-        own, src, gauge,
+        *(pltpu.with_memory_space_constraint(a, pltpu.HBM) for a in (own, src, gauge)),
     )
     mt, mz, blk, bl = call(
         send_kernel,
@@ -738,22 +788,32 @@
         return pairs_out
 
     axes = ("ta", "gz", "sa")
-    x4 = lax.ppermute(blk, axes, route(lambda s: (1, 1) if s == 0 else (2, 1)))
-    x3 = lax.ppermute(blk, axes, route(lambda s: (2, 0) if s == 0 else (-1, 1)))
-    x1 = lax.ppermute(blk, axes, route(lambda s: (1, 0) if s == 0 else (-1, 0)))
-    x2 = lax.ppermute(blk, axes, route(lambda s: (0, 1)))
-    x1, x2, x3, x4, mt, mz = lax.optimization_barrier((x1, x2, x3, x4, mt, mz))
+    xd = lax.ppermute(blk, axes, route(lambda s: (0, 1)))
+    xc = lax.ppermute(blk, axes, route(lambda s: (2, s)))
+    xb = lax.ppermute(blk, axes, route(lambda s: (-1, s)))
+    xa = lax.ppermute(blk, axes, route(lambda s: (1, s)))
+    xd, mz = lax.optimization_barrier((xd, mz))
+    tz = lax.ppermute(mz, axes, route(lambda s: (0, 1)))
+    xa, xb, xc, mt = lax.optimization_barrier((xa, xb, xc, mt))
+    xa2 = lax.ppermute(xa, "sa", swap)
+    xb2 = lax.ppermute(xb, "sa", swap)
+    xc2 = lax.ppermute(xc, "sa", swap)
     ta = lax.ppermute(mt, axes, route(lambda s: (1, 0) if s == 0 else (-1, 0)))
-    tz = lax.ppermute(mz, axes, route(lambda s: (0, 1)))
-    x1b = lax.ppermute(x1, "sa", swap)
-    x3b = lax.ppermute(x3, "sa", swap)
-    x4b = lax.ppermute(x4, "sa", swap)
+    acc = call(
+        local_kernel,
+        [(FIELD, 128)],
+        [pltpu.VMEM((36, 8, 128), f32)],
+        [vmem] * 4,
+        4_000_000,
+        3_000_000,
+        own, bl, src, gauge,
+    )[0]
     corr = call(
         inner_kernel,
         [(24, 8, 128)],
         [
             pltpu.VMEM((8 * MESSAGE, 128), f32),
-            pltpu.VMEM((LINKS, 2, 8, 128), f32),
+            pltpu.VMEM((108, 2, 8, 128), f32),
             pltpu.VMEM((24, 2, 8, 128), f32),
             pltpu.VMEM((8, 24, 2, 8, 128), f32),
             pltpu.VMEM((8, 24, 2, 8, 128), f32),
@@ -761,20 +821,20 @@
             pltpu.SemaphoreType.DMA((8,)),
         ],
         [anywhere] * 8,
-        40_000_000,
-        2_000_000,
-        blk, x2, x1, x1b, x3, x3b, x4, x4b,
+        10_000_000_000,
+        1_000_000_000,
+        blk, xd, xa, xa2, xb, xb2, xc, xc2,
     )[0]
     ta, tz, corr = lax.optimization_barrier((ta, tz, corr))
     tb = lax.ppermute(ta, "sa", swap)
     acc, corrected = call(
-        local_kernel,
+        surface_kernel,
         [(FIELD, 128), (FIELD, 128)],
-        [pltpu.VMEM((54, 8, 128), f32)],
-        [vmem] * 6,
-        6_000_000,
+        [pltpu.VMEM((18, 8, 128), f32)],
+        [vmem] * 5,
         3_000_000,
-        own, bl, src, gauge, tz, corr,
+        3_000_000,
+        own, acc, gauge, tz, corr,
     )
     residual = call(
         final_kernel,

time: 36.8 us -> 33.9 us (0.921)
  local copies, waits for them, and re-layouts: 2.81 us -> 0 us
  starting transfers between devices: 11.9 us -> 12.6 us
  waiting for transfers between devices: 8.78 us -> 8.26 us
    unnamed x6 -> x0, local copies, waits for them, and re-layouts: 2.81 us -> none
    ppermute x7, waiting for transfers between devices: 8.77 us -> 7.41 us  [the longest x1 3.9 us: small_body(): xa = lax.ppermute(blk, axes, route(lambda s: (1, s)))]
    ppermute x1, starting transfers between devices: 0.4 us -> 0.95 us  [small_body(): tb = lax.ppermute(ta, 'sa', swap)]
    ppermute x1, waiting for transfers between devices: 0.01 us -> 0.42 us  [small_body(): src_oth = lax.ppermute(src, 'sa', swap)]
    pallas_call x5 -> x6, Pallas kernels: 12.4 us -> 12.2 us  [call(): pl.pallas_call(kernel, out_shape=shapes, in_specs=in_specs, out_specs=[pl...]
  transfers between devices with their start and end apart: 12 -> 12, of which waited for: 5 -> 6; matrix products, arithmetic and copies ran while one was open for 0% -> 0% of each run, Pallas kernels for 31% -> 33%
where the time goes in v3:
time: 33.9 us; the launch traced here: 33.8 us
  starting transfers between devices  12.6 us (37%)
  Pallas kernels  12.2 us (36%)
  waiting for transfers between devices  8.26 us (24%)
  between operations  0.68 us (2%)
    pallas_call x6, Pallas kernels, call(): pl.pallas_call(kernel, out_shape=shapes, in_specs=in_specs, out_specs=[pl...  12.2 us
    ppermute x1, starting transfers between devices, small_body(): xc = lax.ppermute(blk, axes, route(lambda s: (2, s)))  4.02 us
    ppermute x1, waiting for transfers between devices, small_body(): xa = lax.ppermute(blk, axes, route(lambda s: (1, s)))  3.9 us
    ppermute x1, waiting for transfers between devices, small_body(): xc = lax.ppermute(blk, axes, route(lambda s: (2, s)))  3.05 us
    ppermute x1, starting transfers between devices, small_body(): ta = lax.ppermute(mt, axes, route(lambda s: (1, 0) if s == 0 else (-1, 0)))  2.32 us
    ppermute x1, starting transfers between devices, small_body(): xd = lax.ppermute(blk, axes, route(lambda s: (0, 1)))  1.49 us
    ppermute x1, starting transfers between devices, small_body(): xb = lax.ppermute(blk, axes, route(lambda s: (-1, s)))  1.35 us
    ppermute x1, starting transfers between devices, small_body(): tb = lax.ppermute(ta, 'sa', swap)  0.95 us
  transfers between devices with their start and end apart: 12, of which 6 were waited for; matrix products, arithmetic and copies ran while one was open for 0% of the time, Pallas kernels for 33%

profile of v3, /device:TPU:0, one launch (start us, length us, event | category | flops | bytes accessed | tf_op | source)
XLA Modules:
  0.0 33.8 jit_solution(1240288286059093362)
XLA Ops:
  0.6 0.5 %collective-permute-start = (f32[576,128]{1,0:T(8,128)}, f32[576,128]{1,0:T(8,128)S(1)}, u32[]{:S(2)}, u32[]{:S(2)}) collective-permute-start(f32[576,128]{1,0:T(8,128)} %bitcast.6), channel_id=1, source_target_pairs={{0,1},{1,0},{2,3},{3,2},{4,5},{5,4},{6,7},{7,6},{8,9},{9,8},{10,11... | collective-permute-start | bytes 884744 | tf_op jit(solution)/shard_map/ppermute | solution.py:756
  1.1 0.1 collective-permute-start.1
  1.2 1.1 %shard_map.50 = (f32[576,128]{1,0:T(8,128)S(1)}, f32[576,128]{1,0:T(8,128)S(1)}, f32[144,128]{1,0:T(8,128)S(1)}) custom-call(f32[576,128]{1,0:T(8,128)} %bitcast.7, f32[576,128]{1,0:T(8,128)} %bitcast.9, f32[144,128]{1,0:T(8,128)} %bitcast.10), custom_call_target="tpu_custom_call" | custom-call | bytes 1300000 | tf_op jit(solution)/shard_map/pallas_call | solution.py:739
  2.3 0.2 collective-permute-done.oth_ref
  2.6 0.4 %collective-permute-done.1.src_oth_ref = f32[576,128]{1,0:T(8,128)S(1)} collective-permute-done((f32[576,128]{1,0:T(8,128)}, f32[576,128]{1,0:T(8,128)S(1)}, u32[]{:S(2)}, u32[]{:S(2)}) %collective-permute-start.1) | collective-permute-done | bytes 294944 | tf_op jit(solution)/shard_map/ppermute | solution.py:757
  3.0 0.4 %shard_map.51 = (f32[576,128]{1,0:T(8,128)S(1)}, f32[576,128]{1,0:T(8,128)S(1)}, f32[240,128]{1,0:T(8,128)S(1)}, f32[576,128]{1,0:T(8,128)S(1)}) custom-call(f32[576,128]{1,0:T(8,128)S(1)} %get-tuple-element.20.own_ref, f32[576,128]{1,0:T(8,128)S(1)} %collective-permute-done.oth_ref, f32[576,128]{1,0:T(8,128)S(1)} %get-tuple-element.21.src_own_ref.src_ref, ...), custom_call_target="tpu_custom_call" | custom-call | flops 4000000 | bytes 3000000 | tf_op jit(solution)/shard_map/pallas_call | solution.py:739
  3.4 4.0 %collective-permute-start.4 = (f32[240,128]{1,0:T(8,128)S(1)}, f32[240,128]{1,0:T(8,128)S(1)}, u32[]{:S(2)}, u32[]{:S(2)}) collective-permute-start(f32[240,128]{1,0:T(8,128)S(1)} %get-tuple-element.24.own_ref), channel_id=1, source_target_pairs={{0,8},{1,11},{2,10},{3,9},{4,12},{5,15},{6,14},{7,13},{8,0},{9,3},... | collective-permute-start | bytes 368648 | tf_op jit(solution)/shard_map/ppermute | solution.py:792
  7.4 1.3 %collective-permute-start.3 = (f32[240,128]{1,0:T(8,128)S(1)}, f32[240,128]{1,0:T(8,128)S(1)}, u32[]{:S(2)}, u32[]{:S(2)}) collective-permute-start(f32[240,128]{1,0:T(8,128)S(1)} %get-tuple-element.24.own_ref), channel_id=1, source_target_pairs={{0,12},{1,15},{2,14},{3,13},{4,0},{5,3},{6,2},{7,1},{8,4},{9,7},{1... | collective-permute-start | bytes 368648 | tf_op jit(solution)/shard_map/ppermute | solution.py:793
  8.7 0.7 %collective-permute-start.2 = (f32[240,128]{1,0:T(8,128)S(1)}, f32[240,128]{1,0:T(8,128)S(1)}, u32[]{:S(2)}, u32[]{:S(2)}) collective-permute-start(f32[240,128]{1,0:T(8,128)S(1)} %get-tuple-element.24.own_ref), channel_id=1, source_target_pairs={{0,4},{1,7},{2,6},{3,5},{4,8},{5,11},{6,10},{7,9},{8,12},{9,15},{1... | collective-permute-start | bytes 368648 | tf_op jit(solution)/shard_map/ppermute | solution.py:794
  9.4 1.5 %collective-permute-start.6 = (f32[240,128]{1,0:T(8,128)S(1)}, f32[240,128]{1,0:T(8,128)S(1)}, u32[]{:S(2)}, u32[]{:S(2)}) collective-permute-start(f32[240,128]{1,0:T(8,128)S(1)} %get-tuple-element.24.own_ref), channel_id=1, source_target_pairs={{0,2},{1,3},{2,0},{3,1},{4,6},{5,7},{6,4},{7,5},{8,10},{9,11},{10,... | collective-permute-start | bytes 368648 | tf_op jit(solution)/shard_map/ppermute | solution.py:791
  10.9 3.1 %collective-permute-done.4.xc_ref = f32[240,128]{1,0:T(8,128)S(1)} collective-permute-done((f32[240,128]{1,0:T(8,128)S(1)}, f32[240,128]{1,0:T(8,128)S(1)}, u32[]{:S(2)}, u32[]{:S(2)}) %collective-permute-start.4) | collective-permute-done | bytes 122912 | tf_op jit(solution)/shard_map/ppermute | solution.py:792
  14.0 0.4 %collective-permute-done.3.xb_ref = f32[240,128]{1,0:T(8,128)S(1)} collective-permute-done((f32[240,128]{1,0:T(8,128)S(1)}, f32[240,128]{1,0:T(8,128)S(1)}, u32[]{:S(2)}, u32[]{:S(2)}) %collective-permute-start.3) | collective-permute-done | bytes 122912 | tf_op jit(solution)/shard_map/ppermute | solution.py:793
  14.4 3.9 %collective-permute-done.2.xa_ref = f32[240,128]{1,0:T(8,128)S(1)} collective-permute-done((f32[240,128]{1,0:T(8,128)S(1)}, f32[240,128]{1,0:T(8,128)S(1)}, u32[]{:S(2)}, u32[]{:S(2)}) %collective-permute-start.2) | collective-permute-done | bytes 122912 | tf_op jit(solution)/shard_map/ppermute | solution.py:794
  18.3 0.0 collective-permute-start.8
  18.3 0.5 %collective-permute-start.9 = (f32[240,128]{1,0:T(8,128)S(1)}, f32[240,128]{1,0:T(8,128)S(1)}, u32[]{:S(2)}, u32[]{:S(2)}) collective-permute-start(f32[240,128]{1,0:T(8,128)S(1)} %collective-permute-done.3.xb_ref), channel_id=1, source_target_pairs={{0,1},{1,0},{2,3},{3,2},{4,5},{5,4},{6,7},{7,6},{8,9},{9,8},{10,11... | collective-permute-start | bytes 368648 | tf_op jit(solution)/shard_map/ppermute | solution.py:799
  18.8 0.0 collective-permute-start.10
  18.8 0.0 collective-permute-done.6.xd_ref
  18.8 2.3 %collective-permute-start.5 = (f32[576,128]{1,0:T(8,128)S(1)}, f32[576,128]{1,0:T(8,128)S(1)}, u32[]{:S(2)}, u32[]{:S(2)}) collective-permute-start(f32[576,128]{1,0:T(8,128)S(1)} %get-tuple-element.26), channel_id=1, source_target_pairs={{0,4},{1,13},{2,6},{3,15},{4,8},{5,1},{6,10},{7,3},{8,12},{9,5},{1... | collective-permute-start | bytes 884744 | tf_op jit(solution)/shard_map/ppermute | solution.py:801
  21.2 0.7 %collective-permute-start.7 = (f32[576,128]{1,0:T(8,128)S(1)}, f32[576,128]{1,0:T(8,128)S(1)}, u32[]{:S(2)}, u32[]{:S(2)}) collective-permute-start(f32[576,128]{1,0:T(8,128)S(1)} %get-tuple-element.28), channel_id=1, source_target_pairs={{0,2},{1,3},{2,0},{3,1},{4,6},{5,7},{6,4},{7,5},{8,10},{9,11},{10,... | collective-permute-start | bytes 884744 | tf_op jit(solution)/shard_map/ppermute | solution.py:796
  21.8 0.0 collective-permute-done.8.xa2_ref
  21.8 0.0 collective-permute-done.9.xb2_ref
  21.8 0.0 collective-permute-done.10.xc2_ref
  21.9 8.6 %shard_map.53.corr_ref = f32[24,8,128]{2,1,0:T(8,128)S(1)} custom-call(f32[240,128]{1,0:T(8,128)S(1)} %get-tuple-element.24.own_ref, f32[240,128]{1,0:T(8,128)S(1)} %collective-permute-done.6.xd_ref, f32[240,128]{1,0:T(8,128)S(1)} %collective-permute-done.2.xa_ref, f32[240,128]{1,0:T(8,128)S(1)} %collective-permute-done.8.xa2_ref, ...), custom_call_target="tpu_custom_call" | custom-call | flops 10000000000 | bytes 1000000000 | tf_op jit(solution)/shard_map/pallas_call | solution.py:739
  30.5 0.0 collective-permute-done.5.ta_ref
  30.5 0.2 collective-permute-done.7.mz_ref
  30.7 1.0 %collective-permute-start.11 = (f32[576,128]{1,0:T(8,128)S(1)}, f32[576,128]{1,0:T(8,128)S(1)}, u32[]{:S(2)}, u32[]{:S(2)}) collective-permute-start(f32[576,128]{1,0:T(8,128)S(1)} %collective-permute-done.5.ta_ref), channel_id=1, source_target_pairs={{0,1},{1,0},{2,3},{3,2},{4,5},{5,4},{6,7},{7,6},{8,9},{9,8},{10,11... | collective-permute-start | bytes 884744 | tf_op jit(solution)/shard_map/ppermute | solution.py:829
  31.6 0.5 %shard_map.52.acc_in = f32[576,128]{1,0:T(8,128)S(1)} custom-call(f32[576,128]{1,0:T(8,128)S(1)} %get-tuple-element.20.own_ref, f32[576,128]{1,0:T(8,128)S(1)} %get-tuple-element.23.bl_ref, f32[576,128]{1,0:T(8,128)S(1)} %get-tuple-element.21.src_own_ref.src_ref, f32[144,128]{1,0:T(8,128)S(1)} %get-tuple-element.22.gauge_ref), custom_call_target="tpu_custom_call" | custom-call | flops 4000000 | bytes 3000000 | tf_op jit(solution)/shard_map/pallas_call | solution.py:739
  32.1 0.9 %shard_map.54 = (f32[576,128]{1,0:T(8,128)S(1)}, f32[576,128]{1,0:T(8,128)}) custom-call(f32[576,128]{1,0:T(8,128)S(1)} %get-tuple-element.20.own_ref, f32[576,128]{1,0:T(8,128)S(1)} %shard_map.52.acc_in, f32[144,128]{1,0:T(8,128)S(1)} %get-tuple-element.22.gauge_ref, f32[576,128]{1,0:T(8,128)S(1)} %collective-permute-done.7.mz_ref, ...), custom_call_target="tpu_custom_call" | custom-call | flops 3000000 | bytes 3000000 | tf_op jit(solution)/shard_map/pallas_call | solution.py:739
  32.9 0.0 collective-permute-done.11.tb_ref
  32.9 0.8 %shard_map.55 = f32[576,128]{1,0:T(8,128)} custom-call(f32[576,128]{1,0:T(8,128)S(1)} %get-tuple-element.35.acc_ref, f32[144,128]{1,0:T(8,128)S(1)} %get-tuple-element.22.gauge_ref, f32[576,128]{1,0:T(8,128)S(1)} %collective-permute-done.5.ta_ref, f32[576,128]{1,0:T(8,128)S(1)} %collective-permute-done.11.tb_ref), custom_call_target="tpu_custom_call" | custom-call | flops 2000000 | bytes 2000000 | tf_op jit(solution)/shard_map/pallas_call | solution.py:739
Async XLA Ops:
  0.6 1.9 %collective-permute-start = (f32[576,128]{1,0:T(8,128)}, f32[576,128]{1,0:T(8,128)S(1)}, u32[]{:S(2)}, u32[]{:S(2)}) collective-permute-start(f32[576,128]{1,0:T(8,128)} %bitcast.6), channel_id=1, source_target_pairs={{0,1},{1,0},{2,3},{3,2},{4,5},{5,4},{6,7},{7,6},{8,9},{9,8},{10,11... | collective-permute-start | bytes 884744 | tf_op jit(solution)/shard_map/ppermute | solution.py:756
  1.1 1.8 %collective-permute-start.1 = (f32[576,128]{1,0:T(8,128)}, f32[576,128]{1,0:T(8,128)S(1)}, u32[]{:S(2)}, u32[]{:S(2)}) collective-permute-start(f32[576,128]{1,0:T(8,128)} %bitcast.8), channel_id=1, source_target_pairs={{0,1},{1,0},{2,3},{3,2},{4,5},{5,4},{6,7},{7,6},{8,9},{9,8},{10,11... | collective-permute-start | bytes 884744 | tf_op jit(solution)/shard_map/ppermute | solution.py:757
  3.4 10.6 %collective-permute-start.4 = (f32[240,128]{1,0:T(8,128)S(1)}, f32[240,128]{1,0:T(8,128)S(1)}, u32[]{:S(2)}, u32[]{:S(2)}) collective-permute-start(f32[240,128]{1,0:T(8,128)S(1)} %get-tuple-element.24.own_ref), channel_id=1, source_target_pairs={{0,8},{1,11},{2,10},{3,9},{4,12},{5,15},{6,14},{7,13},{8,0},{9,3},... | collective-permute-start | bytes 368648 | tf_op jit(solution)/shard_map/ppermute | solution.py:792
  7.4 7.0 %collective-permute-start.3 = (f32[240,128]{1,0:T(8,128)S(1)}, f32[240,128]{1,0:T(8,128)S(1)}, u32[]{:S(2)}, u32[]{:S(2)}) collective-permute-start(f32[240,128]{1,0:T(8,128)S(1)} %get-tuple-element.24.own_ref), channel_id=1, source_target_pairs={{0,12},{1,15},{2,14},{3,13},{4,0},{5,3},{6,2},{7,1},{8,4},{9,7},{1... | collective-permute-start | bytes 368648 | tf_op jit(solution)/shard_map/ppermute | solution.py:793
  8.7 9.6 %collective-permute-start.2 = (f32[240,128]{1,0:T(8,128)S(1)}, f32[240,128]{1,0:T(8,128)S(1)}, u32[]{:S(2)}, u32[]{:S(2)}) collective-permute-start(f32[240,128]{1,0:T(8,128)S(1)} %get-tuple-element.24.own_ref), channel_id=1, source_target_pairs={{0,4},{1,7},{2,6},{3,5},{4,8},{5,11},{6,10},{7,9},{8,12},{9,15},{1... | collective-permute-start | bytes 368648 | tf_op jit(solution)/shard_map/ppermute | solution.py:794
  9.4 9.4 %collective-permute-start.6 = (f32[240,128]{1,0:T(8,128)S(1)}, f32[240,128]{1,0:T(8,128)S(1)}, u32[]{:S(2)}, u32[]{:S(2)}) collective-permute-start(f32[240,128]{1,0:T(8,128)S(1)} %get-tuple-element.24.own_ref), channel_id=1, source_target_pairs={{0,2},{1,3},{2,0},{3,1},{4,6},{5,7},{6,4},{7,5},{8,10},{9,11},{10,... | collective-permute-start | bytes 368648 | tf_op jit(solution)/shard_map/ppermute | solution.py:791
  18.3 3.5 %collective-permute-start.8 = (f32[240,128]{1,0:T(8,128)S(1)}, f32[240,128]{1,0:T(8,128)S(1)}, u32[]{:S(2)}, u32[]{:S(2)}) collective-permute-start(f32[240,128]{1,0:T(8,128)S(1)} %collective-permute-done.2.xa_ref), channel_id=1, source_target_pairs={{0,1},{1,0},{2,3},{3,2},{4,5},{5,4},{6,7},{7,6},{8,9},{9,8},{10,11... | collective-permute-start | bytes 368648 | tf_op jit(solution)/shard_map/ppermute | solution.py:798
  18.3 3.5 %collective-permute-start.9 = (f32[240,128]{1,0:T(8,128)S(1)}, f32[240,128]{1,0:T(8,128)S(1)}, u32[]{:S(2)}, u32[]{:S(2)}) collective-permute-start(f32[240,128]{1,0:T(8,128)S(1)} %collective-permute-done.3.xb_ref), channel_id=1, source_target_pairs={{0,1},{1,0},{2,3},{3,2},{4,5},{5,4},{6,7},{7,6},{8,9},{9,8},{10,11... | collective-permute-start | bytes 368648 | tf_op jit(solution)/shard_map/ppermute | solution.py:799
  18.8 3.0 %collective-permute-start.10 = (f32[240,128]{1,0:T(8,128)S(1)}, f32[240,128]{1,0:T(8,128)S(1)}, u32[]{:S(2)}, u32[]{:S(2)}) collective-permute-start(f32[240,128]{1,0:T(8,128)S(1)} %collective-permute-done.4.xc_ref), channel_id=1, source_target_pairs={{0,1},{1,0},{2,3},{3,2},{4,5},{5,4},{6,7},{7,6},{8,9},{9,8},{10,11... | collective-permute-start | bytes 368648 | tf_op jit(solution)/shard_map/ppermute | solution.py:800
  18.8 11.7 %collective-permute-start.5 = (f32[576,128]{1,0:T(8,128)S(1)}, f32[576,128]{1,0:T(8,128)S(1)}, u32[]{:S(2)}, u32[]{:S(2)}) collective-permute-start(f32[576,128]{1,0:T(8,128)S(1)} %get-tuple-element.26), channel_id=1, source_target_pairs={{0,4},{1,13},{2,6},{3,15},{4,8},{5,1},{6,10},{7,3},{8,12},{9,5},{1... | collective-permute-start | bytes 884744 | tf_op jit(solution)/shard_map/ppermute | solution.py:801
  21.2 9.5 %collective-permute-start.7 = (f32[576,128]{1,0:T(8,128)S(1)}, f32[576,128]{1,0:T(8,128)S(1)}, u32[]{:S(2)}, u32[]{:S(2)}) collective-permute-start(f32[576,128]{1,0:T(8,128)S(1)} %get-tuple-element.28), channel_id=1, source_target_pairs={{0,2},{1,3},{2,0},{3,1},{4,6},{5,7},{6,4},{7,5},{8,10},{9,11},{10,... | collective-permute-start | bytes 884744 | tf_op jit(solution)/shard_map/ppermute | solution.py:796
  30.7 2.3 %collective-permute-start.11 = (f32[576,128]{1,0:T(8,128)S(1)}, f32[576,128]{1,0:T(8,128)S(1)}, u32[]{:S(2)}, u32[]{:S(2)}) collective-permute-start(f32[576,128]{1,0:T(8,128)S(1)} %collective-permute-done.5.ta_ref), channel_id=1, source_target_pairs={{0,1},{1,0},{2,3},{3,2},{4,5},{5,4},{6,7},{7,6},{8,9},{9,8},{10,11... | collective-permute-start | bytes 884744 | tf_op jit(solution)/shard_map/ppermute | solution.py:829

commit v4 on v3

--- a/solution.py
+++ b/solution.py
@@ -429,7 +429,7 @@
         copy.wait()
 
 
-def send_kernel(own_ref, oth_ref, src_own_ref, src_oth_ref, gauge_ref, mt_ref, mz_ref, blk_ref, bl_ref, blo_ref, tile_ref):
+def send_kernel(own_ref, oth_ref, src_own_ref, src_oth_ref, gauge_ref, up_ref, down_ref, mz_ref, blk_ref, bl_ref, blo_ref, tile_ref):
     core = lax.axis_index("sa")
     last_time = lax.axis_index("ta") == lax.axis_size("ta") - 1
     time_scale = jnp.where(last_time, 0.5, -0.5).astype(jnp.float32)
@@ -481,20 +481,8 @@
         get = getter(bl_ref, g)
         store(mz_ref, half_spinor(get, 2, -1), 0, g)
         store(mz_ref, link_times(tile_link(tile_ref, 0), half_spinor(get, 2, 1), True), 288, g)
-
-    def time_up(first_ref, second_ref):
-        for which, ref in enumerate((first_ref, second_ref)):
-            for g in range(3):
-                half = half_spinor(getter(ref, g), 3, 1)
-                store(mt_ref, link_times(tile_link(tile_ref, 1), half, True), which * 288, g)
-
-    def time_down(first_ref, second_ref):
-        for which, ref in enumerate((first_ref, second_ref)):
-            for g in range(3):
-                store(mt_ref, half_spinor(getter(ref, g), 3, -1), which * 288, g)
-
-    pl.when(core == 0)(lambda: time_up(bl_ref, blo_ref))
-    pl.when(core == 1)(lambda: time_down(blo_ref, bl_ref))
+        store(up_ref, link_times(tile_link(tile_ref, 1), half_spinor(get, 3, 1), True), 0, g)
+        store(down_ref, half_spinor(get, 3, -1), 0, g)
 
 
 def halves(ref, rows, start):
@@ -529,31 +517,6 @@
         return carry
 
     lax.fori_loop(0, 3, group, 0)
-
-
-def surface_kernel(own_ref, acc_in, gauge_ref, mz_ref, corr_ref, acc_ref, cor_ref, tile_ref):
-    core = lax.axis_index("sa")
-    scaled_links(gauge_ref, tile_ref, 0, 2, -0.5)
-
-    def group(g, carry):
-        rows = group_rows(g)
-        acc = [acc_in[rows(comp), :] for comp in range(24)]
-        acc = add_hop(acc, link_times(tile_link(tile_ref, 0), halves(mz_ref, rows, 0), False), 2, -1)
-        acc = add_hop(acc, halves(mz_ref, rows, 288), 2, 1)
-        for comp in range(24):
-            acc_ref[rows(comp), :] = acc[comp]
-        return carry
-
-    lax.fori_loop(0, 3, group, 0)
-    cor_ref[...] = own_ref[...]
-
-    def add_surface(s, comps, first):
-        for i, comp in enumerate(comps):
-            at = slice(comp * ROWS + 2 * s, comp * ROWS + 2 * s + 2)
-            cor_ref[at, :] = cor_ref[at, :] + corr_ref[first + i, 0:2, :]
-
-    pl.when(core == 0)(lambda: add_surface(0, LOWER, 0))
-    pl.when(core == 1)(lambda: add_surface(11, UPPER, 12))
 
 
 def inner_kernel(own_ref, xd_ref, xa_ref, xa2_ref, xb_ref, xb2_ref, xc_ref, xc2_ref, out_ref, gather_ref, link_ref, base_ref, r_ref, a_ref, z_ref, sem):
@@ -709,25 +672,33 @@
     lax.fori_loop(0, ITERS + 1, stage, 0)
 
 
-def final_kernel(acc_ref, gauge_ref, ta_ref, tb_ref, res_ref, tile_ref):
+def final_kernel(own_ref, acc_ref, gauge_ref, up_ref, down_ref, mz_ref, corr_ref, res_ref, cor_ref, tile_ref):
     core = lax.axis_index("sa")
     last_time = lax.axis_index("ta") == lax.axis_size("ta") - 1
-    scaled_links(gauge_ref, tile_ref, 0, 3, jnp.where(last_time, 0.5, -0.5).astype(jnp.float32))
-
-    def finish(up_ref, down_ref, offset):
-        def group(g, carry):
-            rows = group_rows(g)
-            acc = [acc_ref[rows(comp), :] for comp in range(24)]
-            acc = add_hop(acc, link_times(tile_link(tile_ref, 0), halves(down_ref, rows, offset), False), 3, -1)
-            acc = add_hop(acc, halves(up_ref, rows, offset), 3, 1)
-            for comp in range(24):
-                res_ref[rows(comp), :] = -acc[comp]
-            return carry
-
-        lax.fori_loop(0, 3, group, 0)
-
-    pl.when(core == 0)(lambda: finish(ta_ref, tb_ref, 0))
-    pl.when(core == 1)(lambda: finish(tb_ref, ta_ref, 288))
+    scaled_links(gauge_ref, tile_ref, 0, 2, -0.5)
+    scaled_links(gauge_ref, tile_ref, 1, 3, jnp.where(last_time, 0.5, -0.5).astype(jnp.float32))
+
+    def group(g, carry):
+        rows = group_rows(g)
+        acc = [acc_ref[rows(comp), :] for comp in range(24)]
+        acc = add_hop(acc, link_times(tile_link(tile_ref, 0), halves(mz_ref, rows, 0), False), 2, -1)
+        acc = add_hop(acc, halves(mz_ref, rows, 288), 2, 1)
+        acc = add_hop(acc, link_times(tile_link(tile_ref, 1), halves(down_ref, rows, 0), False), 3, -1)
+        acc = add_hop(acc, halves(up_ref, rows, 0), 3, 1)
+        for comp in range(24):
+            res_ref[rows(comp), :] = -acc[comp]
+        return carry
+
+    lax.fori_loop(0, 3, group, 0)
+    cor_ref[...] = own_ref[...]
+
+    def add_surface(s, comps, first):
+        for i, comp in enumerate(comps):
+            at = slice(comp * ROWS + 2 * s, comp * ROWS + 2 * s + 2)
+            cor_ref[at, :] = cor_ref[at, :] + corr_ref[first + i, 0:2, :]
+
+    pl.when(core == 0)(lambda: add_surface(0, LOWER, 0))
+    pl.when(core == 1)(lambda: add_surface(11, UPPER, 12))
 
 
 def cost(flops, moved):
@@ -767,9 +738,9 @@
         1_300_000,
         *(pltpu.with_memory_space_constraint(a, pltpu.HBM) for a in (own, src, gauge)),
     )
-    mt, mz, blk, bl = call(
+    up, down, mz, blk, bl = call(
         send_kernel,
-        [(FIELD, 128), (FIELD, 128), (MESSAGE, 128), (FIELD, 128)],
+        [(FIELD // 2, 128), (FIELD // 2, 128), (FIELD, 128), (MESSAGE, 128), (FIELD, 128)],
         [pltpu.VMEM((FIELD, 128), f32), pltpu.VMEM((36, 8, 128), f32)],
         [vmem] * 5,
         4_000_000,
@@ -792,13 +763,9 @@
     xc = lax.ppermute(blk, axes, route(lambda s: (2, s)))
     xb = lax.ppermute(blk, axes, route(lambda s: (-1, s)))
     xa = lax.ppermute(blk, axes, route(lambda s: (1, s)))
-    xd, mz = lax.optimization_barrier((xd, mz))
     tz = lax.ppermute(mz, axes, route(lambda s: (0, 1)))
-    xa, xb, xc, mt = lax.optimization_barrier((xa, xb, xc, mt))
-    xa2 = lax.ppermute(xa, "sa", swap)
-    xb2 = lax.ppermute(xb, "sa", swap)
-    xc2 = lax.ppermute(xc, "sa", swap)
-    ta = lax.ppermute(mt, axes, route(lambda s: (1, 0) if s == 0 else (-1, 0)))
+    ta = lax.ppermute(up, axes, route(lambda s: (1, 0)))
+    tb = lax.ppermute(down, axes, route(lambda s: (-1, 0)))
     acc = call(
         local_kernel,
         [(FIELD, 128)],
@@ -808,6 +775,10 @@
         3_000_000,
         own, bl, src, gauge,
     )[0]
+    xa, xb, xc, xd, acc = lax.optimization_barrier((xa, xb, xc, xd, acc))
+    xa2 = lax.ppermute(xa, "sa", swap)
+    xb2 = lax.ppermute(xb, "sa", swap)
+    xc2 = lax.ppermute(xc, "sa", swap)
     corr = call(
         inner_kernel,
         [(24, 8, 128)],
@@ -821,30 +792,19 @@
             pltpu.SemaphoreType.DMA((8,)),
         ],
         [anywhere] * 8,
-        10_000_000_000,
+        1_000_000_000,
         1_000_000_000,
         blk, xd, xa, xa2, xb, xb2, xc, xc2,
     )[0]
-    ta, tz, corr = lax.optimization_barrier((ta, tz, corr))
-    tb = lax.ppermute(ta, "sa", swap)
-    acc, corrected = call(
-        surface_kernel,
+    residual, corrected = call(
+        final_kernel,
         [(FIELD, 128), (FIELD, 128)],
-        [pltpu.VMEM((18, 8, 128), f32)],
-        [vmem] * 5,
+        [pltpu.VMEM((36, 8, 128), f32)],
+        [vmem] * 7,
+        4_000_000,
         3_000_000,
-        3_000_000,
-        own, acc, gauge, tz, corr,
-    )
-    residual = call(
-        final_kernel,
-        [(FIELD, 128)],
-        [pltpu.VMEM((18, 8, 128), f32)],
-        [vmem] * 4,
-        2_000_000,
-        2_000_000,
-        acc, gauge, ta, tb,
-    )[0]
+        own, acc, gauge, ta, tb, tz, corr,
+    )
     return (residual.reshape(whole), corrected.reshape(whole))
 
 

time: 33.9 us -> 33.4 us (0.985)
  starting transfers between devices: 12.6 us -> 13.5 us
  waiting for transfers between devices: 8.26 us -> 7.49 us
  Pallas kernels: 12.2 us -> 11.5 us
    ppermute x1, waiting for transfers between devices: 3.9 us -> 0.01 us  [small_body(): xa = lax.ppermute(blk, axes, route(lambda s: (1, s)))]
    ppermute x1, waiting for transfers between devices: 3.05 us -> 6.75 us  [small_body(): xc = lax.ppermute(blk, axes, route(lambda s: (2, s)))]
    ppermute x1, starting transfers between devices: 1.49 us -> 2.92 us  [small_body(): xd = lax.ppermute(blk, axes, route(lambda s: (0, 1)))]
    ppermute x1, starting transfers between devices: 4.02 us -> 2.59 us  [small_body(): xc = lax.ppermute(blk, axes, route(lambda s: (2, s)))]
    pallas_call x6 -> x5, Pallas kernels: 12.2 us -> 11.5 us  [call(): pl.pallas_call(kernel, out_shape=shapes, in_specs=in_specs, out_specs=[pl...]
    ppermute x2, starting transfers between devices: 3.27 us -> 3.82 us  [the longest x1 2.14 us: small_body(): ta = lax.ppermute(up, axes, route(lambda s: (1, 0)))]
    ppermute x1, starting transfers between devices: 0.01 us -> 0.52 us  [small_body(): xa2 = lax.ppermute(xa, 'sa', swap)]
    ppermute x1, starting transfers between devices: 0.51 us -> 0.01 us  [small_body(): xb2 = lax.ppermute(xb, 'sa', swap)]
  transfers between devices with their start and end apart: 12 -> 12, of which waited for: 6 -> 3; matrix products, arithmetic and copies ran while one was open for 0% -> 0% of each run, Pallas kernels for 33% -> 31%
where the time goes in v4:
time: 33.4 us; the launch traced here: 33.2 us
  starting transfers between devices  13.5 us (40%)
  Pallas kernels  11.5 us (34%)
  waiting for transfers between devices  7.49 us (22%)
  between operations  0.7 us (2%)
    pallas_call x5, Pallas kernels, call(): pl.pallas_call(kernel, out_shape=shapes, in_specs=in_specs, out_specs=[pl...  11.5 us
    ppermute x1, waiting for transfers between devices, small_body(): xc = lax.ppermute(blk, axes, route(lambda s: (2, s)))  6.75 us
    ppermute x1, starting transfers between devices, small_body(): xd = lax.ppermute(blk, axes, route(lambda s: (0, 1)))  2.92 us
    ppermute x1, starting transfers between devices, small_body(): xc = lax.ppermute(blk, axes, route(lambda s: (2, s)))  2.59 us
    ppermute x1, starting transfers between devices, small_body(): ta = lax.ppermute(up, axes, route(lambda s: (1, 0)))  2.14 us
    ppermute x1, starting transfers between devices, small_body(): tb = lax.ppermute(down, axes, route(lambda s: (-1, 0)))  1.69 us
    ppermute x1, starting transfers between devices, small_body(): xb = lax.ppermute(blk, axes, route(lambda s: (-1, s)))  1.35 us
    ppermute x1, starting transfers between devices, small_body(): xa = lax.ppermute(blk, axes, route(lambda s: (1, s)))  0.68 us
  transfers between devices with their start and end apart: 12, of which 3 were waited for; matrix products, arithmetic and copies ran while one was open for 0% of the time, Pallas kernels for 31%

profile of v4, /device:TPU:0, one launch (start us, length us, event | category | flops | bytes accessed | tf_op | source)
XLA Modules:
  0.0 33.2 jit_solution(14410454353843055132)
XLA Ops:
  0.6 0.5 %collective-permute-start = (f32[576,128]{1,0:T(8,128)}, f32[576,128]{1,0:T(8,128)S(1)}, u32[]{:S(2)}, u32[]{:S(2)}) collective-permute-start(f32[576,128]{1,0:T(8,128)} %bitcast.5), channel_id=1, source_target_pairs={{0,1},{1,0},{2,3},{3,2},{4,5},{5,4},{6,7},{7,6},{8,9},{9,8},{10,11... | collective-permute-start | bytes 884744 | tf_op jit(solution)/shard_map/ppermute | solution.py:727
  1.1 0.1 collective-permute-start.1
  1.2 1.1 %shard_map.50 = (f32[576,128]{1,0:T(8,128)S(1)}, f32[576,128]{1,0:T(8,128)S(1)}, f32[144,128]{1,0:T(8,128)S(1)}) custom-call(f32[576,128]{1,0:T(8,128)} %bitcast.6, f32[576,128]{1,0:T(8,128)} %bitcast.8, f32[144,128]{1,0:T(8,128)} %bitcast.9), custom_call_target="tpu_custom_call" | custom-call | bytes 1300000 | tf_op jit(solution)/shard_map/pallas_call | solution.py:710
  2.3 0.2 collective-permute-done.oth_ref
  2.6 0.4 %collective-permute-done.1.src_oth_ref = f32[576,128]{1,0:T(8,128)S(1)} collective-permute-done((f32[576,128]{1,0:T(8,128)}, f32[576,128]{1,0:T(8,128)S(1)}, u32[]{:S(2)}, u32[]{:S(2)}) %collective-permute-start.1) | collective-permute-done | bytes 294944 | tf_op jit(solution)/shard_map/ppermute | solution.py:728
  3.0 0.3 shard_map.51
  3.3 2.9 %collective-permute-start.5 = (f32[240,128]{1,0:T(8,128)S(1)}, f32[240,128]{1,0:T(8,128)S(1)}, u32[]{:S(2)}, u32[]{:S(2)}) collective-permute-start(f32[240,128]{1,0:T(8,128)S(1)} %get-tuple-element.20.own_ref), channel_id=1, source_target_pairs={{0,2},{1,3},{2,0},{3,1},{4,6},{5,7},{6,4},{7,5},{8,10},{9,11},{10,... | collective-permute-start | bytes 368648 | tf_op jit(solution)/shard_map/ppermute | solution.py:762
  6.3 2.6 %collective-permute-start.4 = (f32[240,128]{1,0:T(8,128)S(1)}, f32[240,128]{1,0:T(8,128)S(1)}, u32[]{:S(2)}, u32[]{:S(2)}) collective-permute-start(f32[240,128]{1,0:T(8,128)S(1)} %get-tuple-element.20.own_ref), channel_id=1, source_target_pairs={{0,8},{1,11},{2,10},{3,9},{4,12},{5,15},{6,14},{7,13},{8,0},{9,3},... | collective-permute-start | bytes 368648 | tf_op jit(solution)/shard_map/ppermute | solution.py:763
  8.8 1.3 %collective-permute-start.3 = (f32[240,128]{1,0:T(8,128)S(1)}, f32[240,128]{1,0:T(8,128)S(1)}, u32[]{:S(2)}, u32[]{:S(2)}) collective-permute-start(f32[240,128]{1,0:T(8,128)S(1)} %get-tuple-element.20.own_ref), channel_id=1, source_target_pairs={{0,12},{1,15},{2,14},{3,13},{4,0},{5,3},{6,2},{7,1},{8,4},{9,7},{1... | collective-permute-start | bytes 368648 | tf_op jit(solution)/shard_map/ppermute | solution.py:764
  10.2 0.7 %collective-permute-start.2 = (f32[240,128]{1,0:T(8,128)S(1)}, f32[240,128]{1,0:T(8,128)S(1)}, u32[]{:S(2)}, u32[]{:S(2)}) collective-permute-start(f32[240,128]{1,0:T(8,128)S(1)} %get-tuple-element.20.own_ref), channel_id=1, source_target_pairs={{0,4},{1,7},{2,6},{3,5},{4,8},{5,11},{6,10},{7,9},{8,12},{9,15},{1... | collective-permute-start | bytes 368648 | tf_op jit(solution)/shard_map/ppermute | solution.py:765
  10.9 0.5 %collective-permute-start.8 = (f32[576,128]{1,0:T(8,128)S(1)}, f32[576,128]{1,0:T(8,128)S(1)}, u32[]{:S(2)}, u32[]{:S(2)}) collective-permute-start(f32[576,128]{1,0:T(8,128)S(1)} %get-tuple-element.25), channel_id=1, source_target_pairs={{0,2},{1,3},{2,0},{3,1},{4,6},{5,7},{6,4},{7,5},{8,10},{9,11},{10,... | collective-permute-start | bytes 884744 | tf_op jit(solution)/shard_map/ppermute | solution.py:766
  11.4 0.5 %shard_map.52.acc_ref = f32[576,128]{1,0:T(8,128)S(1)} custom-call(f32[576,128]{1,0:T(8,128)S(1)} %get-tuple-element.17.own_ref, f32[576,128]{1,0:T(8,128)S(1)} %get-tuple-element.21.bl_ref, f32[576,128]{1,0:T(8,128)S(1)} %get-tuple-element.18.src_own_ref.src_ref, f32[144,128]{1,0:T(8,128)S(1)} %get-tuple-element.19.gauge_ref), custom_call_target="tpu_custom_call" | custom-call | flops 4000000 | bytes 3000000 | tf_op jit(solution)/shard_map/pallas_call | solution.py:710
  11.9 0.0 collective-permute-done.5.xd_ref
  11.9 6.8 %collective-permute-done.4.xc_ref = f32[240,128]{1,0:T(8,128)S(1)} collective-permute-done((f32[240,128]{1,0:T(8,128)S(1)}, f32[240,128]{1,0:T(8,128)S(1)}, u32[]{:S(2)}, u32[]{:S(2)}) %collective-permute-start.4) | collective-permute-done | bytes 122912 | tf_op jit(solution)/shard_map/ppermute | solution.py:763
  18.6 0.0 collective-permute-done.3.xb_ref
  18.7 0.0 collective-permute-done.2.xa_ref
  18.7 0.5 %collective-permute-start.9 = (f32[240,128]{1,0:T(8,128)S(1)}, f32[240,128]{1,0:T(8,128)S(1)}, u32[]{:S(2)}, u32[]{:S(2)}) collective-permute-start(f32[240,128]{1,0:T(8,128)S(1)} %collective-permute-done.2.xa_ref), channel_id=1, source_target_pairs={{0,1},{1,0},{2,3},{3,2},{4,5},{5,4},{6,7},{7,6},{8,9},{9,8},{10,11... | collective-permute-start | bytes 368648 | tf_op jit(solution)/shard_map/ppermute | solution.py:779
  19.2 0.0 collective-permute-start.10
  19.2 0.5 %collective-permute-start.11 = (f32[240,128]{1,0:T(8,128)S(1)}, f32[240,128]{1,0:T(8,128)S(1)}, u32[]{:S(2)}, u32[]{:S(2)}) collective-permute-start(f32[240,128]{1,0:T(8,128)S(1)} %collective-permute-done.4.xc_ref), channel_id=1, source_target_pairs={{0,1},{1,0},{2,3},{3,2},{4,5},{5,4},{6,7},{7,6},{8,9},{9,8},{10,11... | collective-permute-start | bytes 368648 | tf_op jit(solution)/shard_map/ppermute | solution.py:781
  19.7 2.1 %collective-permute-start.6 = (f32[288,128]{1,0:T(8,128)S(1)}, f32[288,128]{1,0:T(8,128)S(1)}, u32[]{:S(2)}, u32[]{:S(2)}) collective-permute-start(f32[288,128]{1,0:T(8,128)S(1)} %get-tuple-element.23), channel_id=1, source_target_pairs={{0,4},{1,5},{2,6},{3,7},{4,8},{5,9},{6,10},{7,11},{8,12},{9,13},{1... | collective-permute-start | bytes 442376 | tf_op jit(solution)/shard_map/ppermute | solution.py:767
  21.8 0.0 collective-permute-done.9.xa2_ref
  21.8 1.7 %collective-permute-start.7 = (f32[288,128]{1,0:T(8,128)S(1)}, f32[288,128]{1,0:T(8,128)S(1)}, u32[]{:S(2)}, u32[]{:S(2)}) collective-permute-start(f32[288,128]{1,0:T(8,128)S(1)} %get-tuple-element.24), channel_id=1, source_target_pairs={{0,12},{1,13},{2,14},{3,15},{4,0},{5,1},{6,2},{7,3},{8,4},{9,5},{1... | collective-permute-start | bytes 442376 | tf_op jit(solution)/shard_map/ppermute | solution.py:768
  23.5 0.0 collective-permute-done.10.xb2_ref
  23.5 0.0 collective-permute-done.11.xc2_ref
  23.5 8.6 %shard_map.53.corr_ref = f32[24,8,128]{2,1,0:T(8,128)S(1)} custom-call(f32[240,128]{1,0:T(8,128)S(1)} %get-tuple-element.20.own_ref, f32[240,128]{1,0:T(8,128)S(1)} %collective-permute-done.5.xd_ref, f32[240,128]{1,0:T(8,128)S(1)} %collective-permute-done.2.xa_ref, f32[240,128]{1,0:T(8,128)S(1)} %collective-permute-done.9.xa2_ref, ...), custom_call_target="tpu_custom_call" | custom-call | flops 1000000000 | bytes 1000000000 | tf_op jit(solution)/shard_map/pallas_call | solution.py:710
  32.2 0.0 collective-permute-done.6.up_ref
  32.2 0.0 collective-permute-done.7.down_ref
  32.2 0.0 collective-permute-done.8.mz_ref
  32.2 1.1 %shard_map.54 = (f32[576,128]{1,0:T(8,128)}, f32[576,128]{1,0:T(8,128)}) custom-call(f32[576,128]{1,0:T(8,128)S(1)} %get-tuple-element.17.own_ref, f32[576,128]{1,0:T(8,128)S(1)} %shard_map.52.acc_ref, f32[144,128]{1,0:T(8,128)S(1)} %get-tuple-element.19.gauge_ref, f32[288,128]{1,0:T(8,128)S(1)} %collective-permute-done.6.up_ref, ...), custom_call_target="tpu_custom_call" | custom-call | flops 4000000 | bytes 3000000 | tf_op jit(solution)/shard_map/pallas_call | solution.py:710
Async XLA Ops:
  0.6 1.9 %collective-permute-start = (f32[576,128]{1,0:T(8,128)}, f32[576,128]{1,0:T(8,128)S(1)}, u32[]{:S(2)}, u32[]{:S(2)}) collective-permute-start(f32[576,128]{1,0:T(8,128)} %bitcast.5), channel_id=1, source_target_pairs={{0,1},{1,0},{2,3},{3,2},{4,5},{5,4},{6,7},{7,6},{8,9},{9,8},{10,11... | collective-permute-start | bytes 884744 | tf_op jit(solution)/shard_map/ppermute | solution.py:727
  1.1 1.8 %collective-permute-start.1 = (f32[576,128]{1,0:T(8,128)}, f32[576,128]{1,0:T(8,128)S(1)}, u32[]{:S(2)}, u32[]{:S(2)}) collective-permute-start(f32[576,128]{1,0:T(8,128)} %bitcast.7), channel_id=1, source_target_pairs={{0,1},{1,0},{2,3},{3,2},{4,5},{5,4},{6,7},{7,6},{8,9},{9,8},{10,11... | collective-permute-start | bytes 884744 | tf_op jit(solution)/shard_map/ppermute | solution.py:728
  3.3 8.5 %collective-permute-start.5 = (f32[240,128]{1,0:T(8,128)S(1)}, f32[240,128]{1,0:T(8,128)S(1)}, u32[]{:S(2)}, u32[]{:S(2)}) collective-permute-start(f32[240,128]{1,0:T(8,128)S(1)} %get-tuple-element.20.own_ref), channel_id=1, source_target_pairs={{0,2},{1,3},{2,0},{3,1},{4,6},{5,7},{6,4},{7,5},{8,10},{9,11},{10,... | collective-permute-start | bytes 368648 | tf_op jit(solution)/shard_map/ppermute | solution.py:762
  6.3 12.4 %collective-permute-start.4 = (f32[240,128]{1,0:T(8,128)S(1)}, f32[240,128]{1,0:T(8,128)S(1)}, u32[]{:S(2)}, u32[]{:S(2)}) collective-permute-start(f32[240,128]{1,0:T(8,128)S(1)} %get-tuple-element.20.own_ref), channel_id=1, source_target_pairs={{0,8},{1,11},{2,10},{3,9},{4,12},{5,15},{6,14},{7,13},{8,0},{9,3},... | collective-permute-start | bytes 368648 | tf_op jit(solution)/shard_map/ppermute | solution.py:763
  8.8 9.8 %collective-permute-start.3 = (f32[240,128]{1,0:T(8,128)S(1)}, f32[240,128]{1,0:T(8,128)S(1)}, u32[]{:S(2)}, u32[]{:S(2)}) collective-permute-start(f32[240,128]{1,0:T(8,128)S(1)} %get-tuple-element.20.own_ref), channel_id=1, source_target_pairs={{0,12},{1,15},{2,14},{3,13},{4,0},{5,3},{6,2},{7,1},{8,4},{9,7},{1... | collective-permute-start | bytes 368648 | tf_op jit(solution)/shard_map/ppermute | solution.py:764
  10.2 8.5 %collective-permute-start.2 = (f32[240,128]{1,0:T(8,128)S(1)}, f32[240,128]{1,0:T(8,128)S(1)}, u32[]{:S(2)}, u32[]{:S(2)}) collective-permute-start(f32[240,128]{1,0:T(8,128)S(1)} %get-tuple-element.20.own_ref), channel_id=1, source_target_pairs={{0,4},{1,7},{2,6},{3,5},{4,8},{5,11},{6,10},{7,9},{8,12},{9,15},{1... | collective-permute-start | bytes 368648 | tf_op jit(solution)/shard_map/ppermute | solution.py:765
  10.9 21.3 %collective-permute-start.8 = (f32[576,128]{1,0:T(8,128)S(1)}, f32[576,128]{1,0:T(8,128)S(1)}, u32[]{:S(2)}, u32[]{:S(2)}) collective-permute-start(f32[576,128]{1,0:T(8,128)S(1)} %get-tuple-element.25), channel_id=1, source_target_pairs={{0,2},{1,3},{2,0},{3,1},{4,6},{5,7},{6,4},{7,5},{8,10},{9,11},{10,... | collective-permute-start | bytes 884744 | tf_op jit(solution)/shard_map/ppermute | solution.py:766
  18.7 3.2 %collective-permute-start.9 = (f32[240,128]{1,0:T(8,128)S(1)}, f32[240,128]{1,0:T(8,128)S(1)}, u32[]{:S(2)}, u32[]{:S(2)}) collective-permute-start(f32[240,128]{1,0:T(8,128)S(1)} %collective-permute-done.2.xa_ref), channel_id=1, source_target_pairs={{0,1},{1,0},{2,3},{3,2},{4,5},{5,4},{6,7},{7,6},{8,9},{9,8},{10,11... | collective-permute-start | bytes 368648 | tf_op jit(solution)/shard_map/ppermute | solution.py:779
  19.2 4.3 %collective-permute-start.10 = (f32[240,128]{1,0:T(8,128)S(1)}, f32[240,128]{1,0:T(8,128)S(1)}, u32[]{:S(2)}, u32[]{:S(2)}) collective-permute-start(f32[240,128]{1,0:T(8,128)S(1)} %collective-permute-done.3.xb_ref), channel_id=1, source_target_pairs={{0,1},{1,0},{2,3},{3,2},{4,5},{5,4},{6,7},{7,6},{8,9},{9,8},{10,11... | collective-permute-start | bytes 368648 | tf_op jit(solution)/shard_map/ppermute | solution.py:780
  19.2 4.3 %collective-permute-start.11 = (f32[240,128]{1,0:T(8,128)S(1)}, f32[240,128]{1,0:T(8,128)S(1)}, u32[]{:S(2)}, u32[]{:S(2)}) collective-permute-start(f32[240,128]{1,0:T(8,128)S(1)} %collective-permute-done.4.xc_ref), channel_id=1, source_target_pairs={{0,1},{1,0},{2,3},{3,2},{4,5},{5,4},{6,7},{7,6},{8,9},{9,8},{10,11... | collective-permute-start | bytes 368648 | tf_op jit(solution)/shard_map/ppermute | solution.py:781
  19.7 12.4 %collective-permute-start.6 = (f32[288,128]{1,0:T(8,128)S(1)}, f32[288,128]{1,0:T(8,128)S(1)}, u32[]{:S(2)}, u32[]{:S(2)}) collective-permute-start(f32[288,128]{1,0:T(8,128)S(1)} %get-tuple-element.23), channel_id=1, source_target_pairs={{0,4},{1,5},{2,6},{3,7},{4,8},{5,9},{6,10},{7,11},{8,12},{9,13},{1... | collective-permute-start | bytes 442376 | tf_op jit(solution)/shard_map/ppermute | solution.py:767
  21.8 10.3 %collective-permute-start.7 = (f32[288,128]{1,0:T(8,128)S(1)}, f32[288,128]{1,0:T(8,128)S(1)}, u32[]{:S(2)}, u32[]{:S(2)}) collective-permute-start(f32[288,128]{1,0:T(8,128)S(1)} %get-tuple-element.24), channel_id=1, source_target_pairs={{0,12},{1,13},{2,14},{3,15},{4,0},{5,1},{6,2},{7,3},{8,4},{9,5},{1... | collective-permute-start | bytes 442376 | tf_op jit(solution)/shard_map/ppermute | solution.py:768

commit v5 on v4

--- a/solution.py
+++ b/solution.py
@@ -495,7 +495,8 @@
 
 
 def group_rows(g):
-    return lambda comp, start=0: pl.ds(pl.multiple_of(start + comp * ROWS + g * 8, 8), 8)
+    at = lambda row: row if isinstance(g, int) else pl.multiple_of(row, 8)
+    return lambda comp, start=0: pl.ds(at(start + comp * ROWS + g * 8), 8)
 
 
 def local_kernel(own_ref, bl_ref, src_ref, gauge_ref, acc_ref, tile_ref):
@@ -672,13 +673,23 @@
     lax.fori_loop(0, ITERS + 1, stage, 0)
 
 
-def final_kernel(own_ref, acc_ref, gauge_ref, up_ref, down_ref, mz_ref, corr_ref, res_ref, cor_ref, tile_ref):
+def final_kernel(own_ref, acc_ref, gauge_ref, up_ref, down_ref, mz_ref, corr_ref, res_out, cor_out, tile_ref, res_ref, cor_ref, sem):
     core = lax.axis_index("sa")
     last_time = lax.axis_index("ta") == lax.axis_size("ta") - 1
+    cor_ref[...] = own_ref[...]
+
+    def add_surface(s, comps, first):
+        for i, comp in enumerate(comps):
+            at = slice(comp * ROWS + 2 * s, comp * ROWS + 2 * s + 2)
+            cor_ref[at, :] = cor_ref[at, :] + corr_ref[first + i, 0:2, :]
+
+    pl.when(core == 0)(lambda: add_surface(0, LOWER, 0))
+    pl.when(core == 1)(lambda: add_surface(11, UPPER, 12))
+    copies = [pltpu.make_async_copy(cor_ref, cor_out, sem.at[3])]
+    copies[0].start()
     scaled_links(gauge_ref, tile_ref, 0, 2, -0.5)
     scaled_links(gauge_ref, tile_ref, 1, 3, jnp.where(last_time, 0.5, -0.5).astype(jnp.float32))
-
-    def group(g, carry):
+    for g in range(3):
         rows = group_rows(g)
         acc = [acc_ref[rows(comp), :] for comp in range(24)]
         acc = add_hop(acc, link_times(tile_link(tile_ref, 0), halves(mz_ref, rows, 0), False), 2, -1)
@@ -686,32 +697,24 @@
         acc = add_hop(acc, link_times(tile_link(tile_ref, 1), halves(down_ref, rows, 0), False), 3, -1)
         acc = add_hop(acc, halves(up_ref, rows, 0), 3, 1)
         for comp in range(24):
-            res_ref[rows(comp), :] = -acc[comp]
-        return carry
-
-    lax.fori_loop(0, 3, group, 0)
-    cor_ref[...] = own_ref[...]
-
-    def add_surface(s, comps, first):
-        for i, comp in enumerate(comps):
-            at = slice(comp * ROWS + 2 * s, comp * ROWS + 2 * s + 2)
-            cor_ref[at, :] = cor_ref[at, :] + corr_ref[first + i, 0:2, :]
-
-    pl.when(core == 0)(lambda: add_surface(0, LOWER, 0))
-    pl.when(core == 1)(lambda: add_surface(11, UPPER, 12))
+            res_ref[g, comp] = -acc[comp]
+        copies.append(pltpu.make_async_copy(res_ref.at[g], res_out.at[:, g], sem.at[g]))
+        copies[-1].start()
+    for copy in copies:
+        copy.wait()
 
 
 def cost(flops, moved):
     return pl.CostEstimate(flops=flops, bytes_accessed=moved, transcendentals=0)
 
 
-def call(kernel, outs, scratch, in_specs, flops, moved, *args, limit=VMEM_LIMIT):
+def call(kernel, outs, scratch, in_specs, flops, moved, *args, limit=VMEM_LIMIT, out_space=pltpu.VMEM):
     shapes = [jax.ShapeDtypeStruct(s, jnp.float32) for s in outs]
     return pl.pallas_call(
         kernel,
         out_shape=shapes,
         in_specs=in_specs,
-        out_specs=[pl.BlockSpec(memory_space=pltpu.VMEM)] * len(outs),
+        out_specs=[pl.BlockSpec(memory_space=out_space)] * len(outs),
         scratch_shapes=scratch,
         cost_estimate=cost(flops, moved),
         compiler_params=pltpu.CompilerParams(vmem_limit_bytes=limit),
@@ -798,12 +801,18 @@
     )[0]
     residual, corrected = call(
         final_kernel,
-        [(FIELD, 128), (FIELD, 128)],
-        [pltpu.VMEM((36, 8, 128), f32)],
+        [(24, 3, 8, 128), (FIELD, 128)],
+        [
+            pltpu.VMEM((36, 8, 128), f32),
+            pltpu.VMEM((3, 24, 8, 128), f32),
+            pltpu.VMEM((FIELD, 128), f32),
+            pltpu.SemaphoreType.DMA((4,)),
+        ],
         [vmem] * 7,
         4_000_000,
         3_000_000,
         own, acc, gauge, ta, tb, tz, corr,
+        out_space=pltpu.HBM,
     )
     return (residual.reshape(whole), corrected.reshape(whole))
 

time: 33.4 us -> 33.3 us (level)
  no operation moved by 1% of the time
where the time goes in v5:
time: 33.3 us; the launch traced here: 33.1 us
  starting transfers between devices  13.5 us (41%)
  Pallas kernels  11.4 us (34%)
  waiting for transfers between devices  7.49 us (22%)
  between operations  0.7 us (2%)
    pallas_call x5, Pallas kernels, call(): pl.pallas_call(kernel, out_shape=shapes, in_specs=in_specs, out_specs=[pl...  11.4 us
    ppermute x1, waiting for transfers between devices, small_body(): xc = lax.ppermute(blk, axes, route(lambda s: (2, s)))  6.75 us
    ppermute x1, starting transfers between devices, small_body(): xd = lax.ppermute(blk, axes, route(lambda s: (0, 1)))  2.92 us
    ppermute x1, starting transfers between devices, small_body(): xc = lax.ppermute(blk, axes, route(lambda s: (2, s)))  2.59 us
    ppermute x1, starting transfers between devices, small_body(): ta = lax.ppermute(up, axes, route(lambda s: (1, 0)))  2.14 us
    ppermute x1, starting transfers between devices, small_body(): tb = lax.ppermute(down, axes, route(lambda s: (-1, 0)))  1.69 us
    ppermute x1, starting transfers between devices, small_body(): xb = lax.ppermute(blk, axes, route(lambda s: (-1, s)))  1.35 us
    ppermute x1, starting transfers between devices, small_body(): xa = lax.ppermute(blk, axes, route(lambda s: (1, s)))  0.68 us
  transfers between devices with their start and end apart: 12, of which 3 were waited for; matrix products, arithmetic and copies ran while one was open for 0% of the time, Pallas kernels for 31%

profile of v5, /device:TPU:0, one launch (start us, length us, event | category | flops | bytes accessed | tf_op | source)
XLA Modules:
  0.0 33.1 jit_solution(798792161369666463)
XLA Ops:
  0.6 0.5 %collective-permute-start = (f32[576,128]{1,0:T(8,128)}, f32[576,128]{1,0:T(8,128)S(1)}, u32[]{:S(2)}, u32[]{:S(2)}) collective-permute-start(f32[576,128]{1,0:T(8,128)} %bitcast.5), channel_id=1, source_target_pairs={{0,1},{1,0},{2,3},{3,2},{4,5},{5,4},{6,7},{7,6},{8,9},{9,8},{10,11... | collective-permute-start | bytes 884744 | tf_op jit(solution)/shard_map/ppermute | solution.py:730
  1.1 0.1 collective-permute-start.1
  1.2 1.1 %shard_map.50 = (f32[576,128]{1,0:T(8,128)S(1)}, f32[576,128]{1,0:T(8,128)S(1)}, f32[144,128]{1,0:T(8,128)S(1)}) custom-call(f32[576,128]{1,0:T(8,128)} %bitcast.6, f32[576,128]{1,0:T(8,128)} %bitcast.8, f32[144,128]{1,0:T(8,128)} %bitcast.9), custom_call_target="tpu_custom_call" | custom-call | bytes 1300000 | tf_op jit(solution)/shard_map/pallas_call | solution.py:713
  2.3 0.2 collective-permute-done.oth_ref
  2.6 0.4 %collective-permute-done.1.src_oth_ref = f32[576,128]{1,0:T(8,128)S(1)} collective-permute-done((f32[576,128]{1,0:T(8,128)}, f32[576,128]{1,0:T(8,128)S(1)}, u32[]{:S(2)}, u32[]{:S(2)}) %collective-permute-start.1) | collective-permute-done | bytes 294944 | tf_op jit(solution)/shard_map/ppermute | solution.py:731
  3.0 0.3 shard_map.51
  3.3 2.9 %collective-permute-start.5 = (f32[240,128]{1,0:T(8,128)S(1)}, f32[240,128]{1,0:T(8,128)S(1)}, u32[]{:S(2)}, u32[]{:S(2)}) collective-permute-start(f32[240,128]{1,0:T(8,128)S(1)} %get-tuple-element.20.own_ref), channel_id=1, source_target_pairs={{0,2},{1,3},{2,0},{3,1},{4,6},{5,7},{6,4},{7,5},{8,10},{9,11},{10,... | collective-permute-start | bytes 368648 | tf_op jit(solution)/shard_map/ppermute | solution.py:765
  6.3 2.6 %collective-permute-start.4 = (f32[240,128]{1,0:T(8,128)S(1)}, f32[240,128]{1,0:T(8,128)S(1)}, u32[]{:S(2)}, u32[]{:S(2)}) collective-permute-start(f32[240,128]{1,0:T(8,128)S(1)} %get-tuple-element.20.own_ref), channel_id=1, source_target_pairs={{0,8},{1,11},{2,10},{3,9},{4,12},{5,15},{6,14},{7,13},{8,0},{9,3},... | collective-permute-start | bytes 368648 | tf_op jit(solution)/shard_map/ppermute | solution.py:766
  8.8 1.3 %collective-permute-start.3 = (f32[240,128]{1,0:T(8,128)S(1)}, f32[240,128]{1,0:T(8,128)S(1)}, u32[]{:S(2)}, u32[]{:S(2)}) collective-permute-start(f32[240,128]{1,0:T(8,128)S(1)} %get-tuple-element.20.own_ref), channel_id=1, source_target_pairs={{0,12},{1,15},{2,14},{3,13},{4,0},{5,3},{6,2},{7,1},{8,4},{9,7},{1... | collective-permute-start | bytes 368648 | tf_op jit(solution)/shard_map/ppermute | solution.py:767
  10.2 0.7 %collective-permute-start.2 = (f32[240,128]{1,0:T(8,128)S(1)}, f32[240,128]{1,0:T(8,128)S(1)}, u32[]{:S(2)}, u32[]{:S(2)}) collective-permute-start(f32[240,128]{1,0:T(8,128)S(1)} %get-tuple-element.20.own_ref), channel_id=1, source_target_pairs={{0,4},{1,7},{2,6},{3,5},{4,8},{5,11},{6,10},{7,9},{8,12},{9,15},{1... | collective-permute-start | bytes 368648 | tf_op jit(solution)/shard_map/ppermute | solution.py:768
  10.9 0.5 %collective-permute-start.8 = (f32[576,128]{1,0:T(8,128)S(1)}, f32[576,128]{1,0:T(8,128)S(1)}, u32[]{:S(2)}, u32[]{:S(2)}) collective-permute-start(f32[576,128]{1,0:T(8,128)S(1)} %get-tuple-element.25), channel_id=1, source_target_pairs={{0,2},{1,3},{2,0},{3,1},{4,6},{5,7},{6,4},{7,5},{8,10},{9,11},{10,... | collective-permute-start | bytes 884744 | tf_op jit(solution)/shard_map/ppermute | solution.py:769
  11.4 0.5 %shard_map.52.acc_ref = f32[576,128]{1,0:T(8,128)S(1)} custom-call(f32[576,128]{1,0:T(8,128)S(1)} %get-tuple-element.17.own_ref, f32[576,128]{1,0:T(8,128)S(1)} %get-tuple-element.21.bl_ref, f32[576,128]{1,0:T(8,128)S(1)} %get-tuple-element.18.src_own_ref.src_ref, f32[144,128]{1,0:T(8,128)S(1)} %get-tuple-element.19.gauge_ref), custom_call_target="tpu_custom_call" | custom-call | flops 4000000 | bytes 3000000 | tf_op jit(solution)/shard_map/pallas_call | solution.py:713
  11.9 0.0 collective-permute-done.5.xd_ref
  11.9 6.8 %collective-permute-done.4.xc_ref = f32[240,128]{1,0:T(8,128)S(1)} collective-permute-done((f32[240,128]{1,0:T(8,128)S(1)}, f32[240,128]{1,0:T(8,128)S(1)}, u32[]{:S(2)}, u32[]{:S(2)}) %collective-permute-start.4) | collective-permute-done | bytes 122912 | tf_op jit(solution)/shard_map/ppermute | solution.py:766
  18.6 0.0 collective-permute-done.3.xb_ref
  18.7 0.0 collective-permute-done.2.xa_ref
  18.7 0.5 %collective-permute-start.9 = (f32[240,128]{1,0:T(8,128)S(1)}, f32[240,128]{1,0:T(8,128)S(1)}, u32[]{:S(2)}, u32[]{:S(2)}) collective-permute-start(f32[240,128]{1,0:T(8,128)S(1)} %collective-permute-done.2.xa_ref), channel_id=1, source_target_pairs={{0,1},{1,0},{2,3},{3,2},{4,5},{5,4},{6,7},{7,6},{8,9},{9,8},{10,11... | collective-permute-start | bytes 368648 | tf_op jit(solution)/shard_map/ppermute | solution.py:782
  19.2 0.0 collective-permute-start.10
  19.2 0.5 %collective-permute-start.11 = (f32[240,128]{1,0:T(8,128)S(1)}, f32[240,128]{1,0:T(8,128)S(1)}, u32[]{:S(2)}, u32[]{:S(2)}) collective-permute-start(f32[240,128]{1,0:T(8,128)S(1)} %collective-permute-done.4.xc_ref), channel_id=1, source_target_pairs={{0,1},{1,0},{2,3},{3,2},{4,5},{5,4},{6,7},{7,6},{8,9},{9,8},{10,11... | collective-permute-start | bytes 368648 | tf_op jit(solution)/shard_map/ppermute | solution.py:784
  19.7 2.1 %collective-permute-start.6 = (f32[288,128]{1,0:T(8,128)S(1)}, f32[288,128]{1,0:T(8,128)S(1)}, u32[]{:S(2)}, u32[]{:S(2)}) collective-permute-start(f32[288,128]{1,0:T(8,128)S(1)} %get-tuple-element.23), channel_id=1, source_target_pairs={{0,4},{1,5},{2,6},{3,7},{4,8},{5,9},{6,10},{7,11},{8,12},{9,13},{1... | collective-permute-start | bytes 442376 | tf_op jit(solution)/shard_map/ppermute | solution.py:770
  21.8 0.0 collective-permute-done.9.xa2_ref
  21.8 1.7 %collective-permute-start.7 = (f32[288,128]{1,0:T(8,128)S(1)}, f32[288,128]{1,0:T(8,128)S(1)}, u32[]{:S(2)}, u32[]{:S(2)}) collective-permute-start(f32[288,128]{1,0:T(8,128)S(1)} %get-tuple-element.24), channel_id=1, source_target_pairs={{0,12},{1,13},{2,14},{3,15},{4,0},{5,1},{6,2},{7,3},{8,4},{9,5},{1... | collective-permute-start | bytes 442376 | tf_op jit(solution)/shard_map/ppermute | solution.py:771
  23.5 0.0 collective-permute-done.10.xb2_ref
  23.5 0.0 collective-permute-done.11.xc2_ref
  23.5 8.6 %shard_map.53.corr_ref = f32[24,8,128]{2,1,0:T(8,128)S(1)} custom-call(f32[240,128]{1,0:T(8,128)S(1)} %get-tuple-element.20.own_ref, f32[240,128]{1,0:T(8,128)S(1)} %collective-permute-done.5.xd_ref, f32[240,128]{1,0:T(8,128)S(1)} %collective-permute-done.2.xa_ref, f32[240,128]{1,0:T(8,128)S(1)} %collective-permute-done.9.xa2_ref, ...), custom_call_target="tpu_custom_call" | custom-call | flops 1000000000 | bytes 1000000000 | tf_op jit(solution)/shard_map/pallas_call | solution.py:713
  32.2 0.0 collective-permute-done.6.up_ref
  32.2 0.0 collective-permute-done.7.down_ref
  32.2 0.0 collective-permute-done.8.mz_ref
  32.2 0.9 %shard_map.54 = (f32[24,3,8,128]{3,2,1,0:T(8,128)}, f32[576,128]{1,0:T(8,128)}) custom-call(f32[576,128]{1,0:T(8,128)S(1)} %get-tuple-element.17.own_ref, f32[576,128]{1,0:T(8,128)S(1)} %shard_map.52.acc_ref, f32[144,128]{1,0:T(8,128)S(1)} %get-tuple-element.19.gauge_ref, f32[288,128]{1,0:T(8,128)S(1)} %collective-permute-done.6.up_ref, ...), custom_call_target="tpu_custom_call" | custom-call | flops 4000000 | bytes 3000000 | tf_op jit(solution)/shard_map/pallas_call | solution.py:713
Async XLA Ops:
  0.6 1.9 %collective-permute-start = (f32[576,128]{1,0:T(8,128)}, f32[576,128]{1,0:T(8,128)S(1)}, u32[]{:S(2)}, u32[]{:S(2)}) collective-permute-start(f32[576,128]{1,0:T(8,128)} %bitcast.5), channel_id=1, source_target_pairs={{0,1},{1,0},{2,3},{3,2},{4,5},{5,4},{6,7},{7,6},{8,9},{9,8},{10,11... | collective-permute-start | bytes 884744 | tf_op jit(solution)/shard_map/ppermute | solution.py:730
  1.1 1.8 %collective-permute-start.1 = (f32[576,128]{1,0:T(8,128)}, f32[576,128]{1,0:T(8,128)S(1)}, u32[]{:S(2)}, u32[]{:S(2)}) collective-permute-start(f32[576,128]{1,0:T(8,128)} %bitcast.7), channel_id=1, source_target_pairs={{0,1},{1,0},{2,3},{3,2},{4,5},{5,4},{6,7},{7,6},{8,9},{9,8},{10,11... | collective-permute-start | bytes 884744 | tf_op jit(solution)/shard_map/ppermute | solution.py:731
  3.3 8.5 %collective-permute-start.5 = (f32[240,128]{1,0:T(8,128)S(1)}, f32[240,128]{1,0:T(8,128)S(1)}, u32[]{:S(2)}, u32[]{:S(2)}) collective-permute-start(f32[240,128]{1,0:T(8,128)S(1)} %get-tuple-element.20.own_ref), channel_id=1, source_target_pairs={{0,2},{1,3},{2,0},{3,1},{4,6},{5,7},{6,4},{7,5},{8,10},{9,11},{10,... | collective-permute-start | bytes 368648 | tf_op jit(solution)/shard_map/ppermute | solution.py:765
  6.3 12.4 %collective-permute-start.4 = (f32[240,128]{1,0:T(8,128)S(1)}, f32[240,128]{1,0:T(8,128)S(1)}, u32[]{:S(2)}, u32[]{:S(2)}) collective-permute-start(f32[240,128]{1,0:T(8,128)S(1)} %get-tuple-element.20.own_ref), channel_id=1, source_target_pairs={{0,8},{1,11},{2,10},{3,9},{4,12},{5,15},{6,14},{7,13},{8,0},{9,3},... | collective-permute-start | bytes 368648 | tf_op jit(solution)/shard_map/ppermute | solution.py:766
  8.8 9.8 %collective-permute-start.3 = (f32[240,128]{1,0:T(8,128)S(1)}, f32[240,128]{1,0:T(8,128)S(1)}, u32[]{:S(2)}, u32[]{:S(2)}) collective-permute-start(f32[240,128]{1,0:T(8,128)S(1)} %get-tuple-element.20.own_ref), channel_id=1, source_target_pairs={{0,12},{1,15},{2,14},{3,13},{4,0},{5,3},{6,2},{7,1},{8,4},{9,7},{1... | collective-permute-start | bytes 368648 | tf_op jit(solution)/shard_map/ppermute | solution.py:767
  10.2 8.5 %collective-permute-start.2 = (f32[240,128]{1,0:T(8,128)S(1)}, f32[240,128]{1,0:T(8,128)S(1)}, u32[]{:S(2)}, u32[]{:S(2)}) collective-permute-start(f32[240,128]{1,0:T(8,128)S(1)} %get-tuple-element.20.own_ref), channel_id=1, source_target_pairs={{0,4},{1,7},{2,6},{3,5},{4,8},{5,11},{6,10},{7,9},{8,12},{9,15},{1... | collective-permute-start | bytes 368648 | tf_op jit(solution)/shard_map/ppermute | solution.py:768
  10.9 21.3 %collective-permute-start.8 = (f32[576,128]{1,0:T(8,128)S(1)}, f32[576,128]{1,0:T(8,128)S(1)}, u32[]{:S(2)}, u32[]{:S(2)}) collective-permute-start(f32[576,128]{1,0:T(8,128)S(1)} %get-tuple-element.25), channel_id=1, source_target_pairs={{0,2},{1,3},{2,0},{3,1},{4,6},{5,7},{6,4},{7,5},{8,10},{9,11},{10,... | collective-permute-start | bytes 884744 | tf_op jit(solution)/shard_map/ppermute | solution.py:769
  18.7 3.2 %collective-permute-start.9 = (f32[240,128]{1,0:T(8,128)S(1)}, f32[240,128]{1,0:T(8,128)S(1)}, u32[]{:S(2)}, u32[]{:S(2)}) collective-permute-start(f32[240,128]{1,0:T(8,128)S(1)} %collective-permute-done.2.xa_ref), channel_id=1, source_target_pairs={{0,1},{1,0},{2,3},{3,2},{4,5},{5,4},{6,7},{7,6},{8,9},{9,8},{10,11... | collective-permute-start | bytes 368648 | tf_op jit(solution)/shard_map/ppermute | solution.py:782
  19.2 4.3 %collective-permute-start.10 = (f32[240,128]{1,0:T(8,128)S(1)}, f32[240,128]{1,0:T(8,128)S(1)}, u32[]{:S(2)}, u32[]{:S(2)}) collective-permute-start(f32[240,128]{1,0:T(8,128)S(1)} %collective-permute-done.3.xb_ref), channel_id=1, source_target_pairs={{0,1},{1,0},{2,3},{3,2},{4,5},{5,4},{6,7},{7,6},{8,9},{9,8},{10,11... | collective-permute-start | bytes 368648 | tf_op jit(solution)/shard_map/ppermute | solution.py:783
  19.2 4.3 %collective-permute-start.11 = (f32[240,128]{1,0:T(8,128)S(1)}, f32[240,128]{1,0:T(8,128)S(1)}, u32[]{:S(2)}, u32[]{:S(2)}) collective-permute-start(f32[240,128]{1,0:T(8,128)S(1)} %collective-permute-done.4.xc_ref), channel_id=1, source_target_pairs={{0,1},{1,0},{2,3},{3,2},{4,5},{5,4},{6,7},{7,6},{8,9},{9,8},{10,11... | collective-permute-start | bytes 368648 | tf_op jit(solution)/shard_map/ppermute | solution.py:784
  19.7 12.4 %collective-permute-start.6 = (f32[288,128]{1,0:T(8,128)S(1)}, f32[288,128]{1,0:T(8,128)S(1)}, u32[]{:S(2)}, u32[]{:S(2)}) collective-permute-start(f32[288,128]{1,0:T(8,128)S(1)} %get-tuple-element.23), channel_id=1, source_target_pairs={{0,4},{1,5},{2,6},{3,7},{4,8},{5,9},{6,10},{7,11},{8,12},{9,13},{1... | collective-permute-start | bytes 442376 | tf_op jit(solution)/shard_map/ppermute | solution.py:770
  21.8 10.3 %collective-permute-start.7 = (f32[288,128]{1,0:T(8,128)S(1)}, f32[288,128]{1,0:T(8,128)S(1)}, u32[]{:S(2)}, u32[]{:S(2)}) collective-permute-start(f32[288,128]{1,0:T(8,128)S(1)} %get-tuple-element.24), channel_id=1, source_target_pairs={{0,12},{1,13},{2,14},{3,15},{4,0},{5,1},{6,2},{7,3},{8,4},{9,5},{1... | collective-permute-start | bytes 442376 | tf_op jit(solution)/shard_map/ppermute | solution.py:771

commit v6 on v5

--- a/solution.py
+++ b/solution.py
@@ -429,7 +429,7 @@
         copy.wait()
 
 
-def send_kernel(own_ref, oth_ref, src_own_ref, src_oth_ref, gauge_ref, up_ref, down_ref, mz_ref, blk_ref, bl_ref, blo_ref, tile_ref):
+def halo_kernel(own_ref, oth_ref, gauge_ref, up_ref, down_ref, mz_ref, bl_ref, blo_ref, tile_ref):
     core = lax.axis_index("sa")
     last_time = lax.axis_index("ta") == lax.axis_size("ta") - 1
     time_scale = jnp.where(last_time, 0.5, -0.5).astype(jnp.float32)
@@ -438,6 +438,26 @@
     blend_rows(bl_ref, own_ref, oth_ref, first, last)
     blend_rows(blo_ref, oth_ref, own_ref, last, first)
 
+    scaled_links(gauge_ref, tile_ref, 0, 2, -0.5)
+    scaled_links(gauge_ref, tile_ref, 1, 3, time_scale)
+
+    def store(ref, half, offset, g):
+        for (spin, part, color), value in half.items():
+            ref[pl.ds(offset + (part * 6 + spin * 3 + color) * ROWS + g * 8, 8), :] = value
+
+    def getter(ref, g):
+        return lambda comp: ref[pl.ds(comp * ROWS + g * 8, 8), :]
+
+    for g in range(3):
+        get = getter(bl_ref, g)
+        store(mz_ref, half_spinor(get, 2, -1), 0, g)
+        store(mz_ref, link_times(tile_link(tile_ref, 0), half_spinor(get, 2, 1), True), 288, g)
+        store(up_ref, link_times(tile_link(tile_ref, 1), half_spinor(get, 3, 1), True), 0, g)
+        store(down_ref, half_spinor(get, 3, -1), 0, g)
+
+
+def block_kernel(own_ref, oth_ref, src_own_ref, src_oth_ref, gauge_ref, bl_ref, blo_ref, blk_ref):
+    core = lax.axis_index("sa")
     for h in range(2):
         for i in range(8):
             base = h * BLOCK + i * 6
@@ -466,23 +486,6 @@
 
     pl.when(core == 0)(lambda: surfaces(bl_ref, own_ref, src_own_ref, blo_ref, oth_ref, src_oth_ref))
     pl.when(core == 1)(lambda: surfaces(blo_ref, oth_ref, src_oth_ref, bl_ref, own_ref, src_own_ref))
-
-    scaled_links(gauge_ref, tile_ref, 0, 2, -0.5)
-    scaled_links(gauge_ref, tile_ref, 1, 3, time_scale)
-
-    def store(ref, half, offset, g):
-        for (spin, part, color), value in half.items():
-            ref[pl.ds(offset + (part * 6 + spin * 3 + color) * ROWS + g * 8, 8), :] = value
-
-    def getter(ref, g):
-        return lambda comp: ref[pl.ds(comp * ROWS + g * 8, 8), :]
-
-    for g in range(3):
-        get = getter(bl_ref, g)
-        store(mz_ref, half_spinor(get, 2, -1), 0, g)
-        store(mz_ref, link_times(tile_link(tile_ref, 0), half_spinor(get, 2, 1), True), 288, g)
-        store(up_ref, link_times(tile_link(tile_ref, 1), half_spinor(get, 3, 1), True), 0, g)
-        store(down_ref, half_spinor(get, 3, -1), 0, g)
 
 
 def halves(ref, rows, start):
@@ -741,15 +744,24 @@
         1_300_000,
         *(pltpu.with_memory_space_constraint(a, pltpu.HBM) for a in (own, src, gauge)),
     )
-    up, down, mz, blk, bl = call(
-        send_kernel,
-        [(FIELD // 2, 128), (FIELD // 2, 128), (FIELD, 128), (MESSAGE, 128), (FIELD, 128)],
-        [pltpu.VMEM((FIELD, 128), f32), pltpu.VMEM((36, 8, 128), f32)],
-        [vmem] * 5,
+    up, down, mz, bl, blo = call(
+        halo_kernel,
+        [(FIELD // 2, 128), (FIELD // 2, 128), (FIELD, 128), (FIELD, 128), (FIELD, 128)],
+        [pltpu.VMEM((36, 8, 128), f32)],
+        [vmem] * 3,
         4_000_000,
-        3_000_000,
-        own, oth, src, src_oth, gauge,
-    )
+        2_000_000,
+        own, oth, gauge,
+    )
+    blk = call(
+        block_kernel,
+        [(MESSAGE, 128)],
+        [],
+        [vmem] * 7,
+        100_000,
+        300_000,
+        own, oth, src, src_oth, gauge, bl, blo,
+    )[0]
 
     def route(where):
         pairs_out = []

time: 33.3 us -> 33 us (level)
    pallas_call x5 -> x6, Pallas kernels: 11.4 us -> 11.4 us  [call(): pl.pallas_call(kernel, out_shape=shapes, in_specs=in_specs, out_specs=[pl...]
  transfers between devices with their start and end apart: 12 -> 12, of which waited for: 3 -> 3; matrix products, arithmetic and copies ran while one was open for 0% -> 0% of each run, Pallas kernels for 31% -> 32%
where the time goes in v6:
time: 33 us; the launch traced here: 32.8 us
  starting transfers between devices  13.5 us (41%)
  Pallas kernels  11.4 us (35%)
  waiting for transfers between devices  7.17 us (22%)
  between operations  0.7 us (2%)
    pallas_call x6, Pallas kernels, call(): pl.pallas_call(kernel, out_shape=shapes, in_specs=in_specs, out_specs=[pl...  11.4 us
    ppermute x1, waiting for transfers between devices, small_body(): xc = lax.ppermute(blk, axes, route(lambda s: (2, s)))  6.75 us
    ppermute x1, starting transfers between devices, small_body(): xd = lax.ppermute(blk, axes, route(lambda s: (0, 1)))  2.92 us
    ppermute x1, starting transfers between devices, small_body(): xc = lax.ppermute(blk, axes, route(lambda s: (2, s)))  2.59 us
    ppermute x1, starting transfers between devices, small_body(): ta = lax.ppermute(up, axes, route(lambda s: (1, 0)))  2.14 us
    ppermute x1, starting transfers between devices, small_body(): tb = lax.ppermute(down, axes, route(lambda s: (-1, 0)))  1.69 us
    ppermute x1, starting transfers between devices, small_body(): xb = lax.ppermute(blk, axes, route(lambda s: (-1, s)))  1.35 us
    ppermute x1, starting transfers between devices, small_body(): xa = lax.ppermute(blk, axes, route(lambda s: (1, s)))  0.68 us
  transfers between devices with their start and end apart: 12, of which 3 were waited for; matrix products, arithmetic and copies ran while one was open for 0% of the time, Pallas kernels for 32%

profile of v6, /device:TPU:0, one launch (start us, length us, event | category | flops | bytes accessed | tf_op | source)
XLA Modules:
  0.0 32.8 jit_solution(12354019465036061791)
XLA Ops:
  0.6 0.5 %collective-permute-start = (f32[576,128]{1,0:T(8,128)}, f32[576,128]{1,0:T(8,128)S(1)}, u32[]{:S(2)}, u32[]{:S(2)}) collective-permute-start(f32[576,128]{1,0:T(8,128)} %bitcast.5), channel_id=1, source_target_pairs={{0,1},{1,0},{2,3},{3,2},{4,5},{5,4},{6,7},{7,6},{8,9},{9,8},{10,11... | collective-permute-start | bytes 884744 | tf_op jit(solution)/shard_map/ppermute | solution.py:733
  1.1 0.1 collective-permute-start.1
  1.2 1.1 %shard_map.50 = (f32[576,128]{1,0:T(8,128)S(1)}, f32[576,128]{1,0:T(8,128)S(1)}, f32[144,128]{1,0:T(8,128)S(1)}) custom-call(f32[576,128]{1,0:T(8,128)} %bitcast.6, f32[576,128]{1,0:T(8,128)} %bitcast.8, f32[144,128]{1,0:T(8,128)} %bitcast.9), custom_call_target="tpu_custom_call" | custom-call | bytes 1300000 | tf_op jit(solution)/shard_map/pallas_call | solution.py:716
  2.3 0.2 collective-permute-done.oth_ref
  2.6 0.3 shard_map.51
  2.9 0.1 collective-permute-done.1.src_oth_ref
  3.0 2.9 %collective-permute-start.5 = (f32[240,128]{1,0:T(8,128)S(1)}, f32[240,128]{1,0:T(8,128)S(1)}, u32[]{:S(2)}, u32[]{:S(2)}) collective-permute-start(f32[240,128]{1,0:T(8,128)S(1)} %shard_map.52.own_ref), channel_id=1, source_target_pairs={{0,2},{1,3},{2,0},{3,1},{4,6},{5,7},{6,4},{7,5},{8,10},{9,11},{10,... | collective-permute-start | bytes 368648 | tf_op jit(solution)/shard_map/ppermute | solution.py:777
  6.0 2.6 %collective-permute-start.4 = (f32[240,128]{1,0:T(8,128)S(1)}, f32[240,128]{1,0:T(8,128)S(1)}, u32[]{:S(2)}, u32[]{:S(2)}) collective-permute-start(f32[240,128]{1,0:T(8,128)S(1)} %shard_map.52.own_ref), channel_id=1, source_target_pairs={{0,8},{1,11},{2,10},{3,9},{4,12},{5,15},{6,14},{7,13},{8,0},{9,3},... | collective-permute-start | bytes 368648 | tf_op jit(solution)/shard_map/ppermute | solution.py:778
  8.5 1.3 %collective-permute-start.3 = (f32[240,128]{1,0:T(8,128)S(1)}, f32[240,128]{1,0:T(8,128)S(1)}, u32[]{:S(2)}, u32[]{:S(2)}) collective-permute-start(f32[240,128]{1,0:T(8,128)S(1)} %shard_map.52.own_ref), channel_id=1, source_target_pairs={{0,12},{1,15},{2,14},{3,13},{4,0},{5,3},{6,2},{7,1},{8,4},{9,7},{1... | collective-permute-start | bytes 368648 | tf_op jit(solution)/shard_map/ppermute | solution.py:779
  9.9 0.7 %collective-permute-start.2 = (f32[240,128]{1,0:T(8,128)S(1)}, f32[240,128]{1,0:T(8,128)S(1)}, u32[]{:S(2)}, u32[]{:S(2)}) collective-permute-start(f32[240,128]{1,0:T(8,128)S(1)} %shard_map.52.own_ref), channel_id=1, source_target_pairs={{0,4},{1,7},{2,6},{3,5},{4,8},{5,11},{6,10},{7,9},{8,12},{9,15},{1... | collective-permute-start | bytes 368648 | tf_op jit(solution)/shard_map/ppermute | solution.py:780
  10.6 0.5 %collective-permute-start.8 = (f32[576,128]{1,0:T(8,128)S(1)}, f32[576,128]{1,0:T(8,128)S(1)}, u32[]{:S(2)}, u32[]{:S(2)}) collective-permute-start(f32[576,128]{1,0:T(8,128)S(1)} %get-tuple-element.25), channel_id=1, source_target_pairs={{0,2},{1,3},{2,0},{3,1},{4,6},{5,7},{6,4},{7,5},{8,10},{9,11},{10,... | collective-permute-start | bytes 884744 | tf_op jit(solution)/shard_map/ppermute | solution.py:781
  11.1 0.5 %shard_map.53.acc_ref = f32[576,128]{1,0:T(8,128)S(1)} custom-call(f32[576,128]{1,0:T(8,128)S(1)} %get-tuple-element.17.own_ref, f32[576,128]{1,0:T(8,128)S(1)} %get-tuple-element.20.bl_ref, f32[576,128]{1,0:T(8,128)S(1)} %get-tuple-element.18.src_own_ref.src_ref, f32[144,128]{1,0:T(8,128)S(1)} %get-tuple-element.19.gauge_ref), custom_call_target="tpu_custom_call" | custom-call | flops 4000000 | bytes 3000000 | tf_op jit(solution)/shard_map/pallas_call | solution.py:716
  11.6 0.0 collective-permute-done.5.xd_ref
  11.6 6.8 %collective-permute-done.4.xc_ref = f32[240,128]{1,0:T(8,128)S(1)} collective-permute-done((f32[240,128]{1,0:T(8,128)S(1)}, f32[240,128]{1,0:T(8,128)S(1)}, u32[]{:S(2)}, u32[]{:S(2)}) %collective-permute-start.4) | collective-permute-done | bytes 122912 | tf_op jit(solution)/shard_map/ppermute | solution.py:778
  18.3 0.0 collective-permute-done.3.xb_ref
  18.4 0.0 collective-permute-done.2.xa_ref
  18.4 0.5 %collective-permute-start.9 = (f32[240,128]{1,0:T(8,128)S(1)}, f32[240,128]{1,0:T(8,128)S(1)}, u32[]{:S(2)}, u32[]{:S(2)}) collective-permute-start(f32[240,128]{1,0:T(8,128)S(1)} %collective-permute-done.2.xa_ref), channel_id=1, source_target_pairs={{0,1},{1,0},{2,3},{3,2},{4,5},{5,4},{6,7},{7,6},{8,9},{9,8},{10,11... | collective-permute-start | bytes 368648 | tf_op jit(solution)/shard_map/ppermute | solution.py:794
  18.9 0.0 collective-permute-start.10
  18.9 0.5 %collective-permute-start.11 = (f32[240,128]{1,0:T(8,128)S(1)}, f32[240,128]{1,0:T(8,128)S(1)}, u32[]{:S(2)}, u32[]{:S(2)}) collective-permute-start(f32[240,128]{1,0:T(8,128)S(1)} %collective-permute-done.4.xc_ref), channel_id=1, source_target_pairs={{0,1},{1,0},{2,3},{3,2},{4,5},{5,4},{6,7},{7,6},{8,9},{9,8},{10,11... | collective-permute-start | bytes 368648 | tf_op jit(solution)/shard_map/ppermute | solution.py:796
  19.4 2.1 %collective-permute-start.6 = (f32[288,128]{1,0:T(8,128)S(1)}, f32[288,128]{1,0:T(8,128)S(1)}, u32[]{:S(2)}, u32[]{:S(2)}) collective-permute-start(f32[288,128]{1,0:T(8,128)S(1)} %get-tuple-element.23), channel_id=1, source_target_pairs={{0,4},{1,5},{2,6},{3,7},{4,8},{5,9},{6,10},{7,11},{8,12},{9,13},{1... | collective-permute-start | bytes 442376 | tf_op jit(solution)/shard_map/ppermute | solution.py:782
  21.5 0.0 collective-permute-done.9.xa2_ref
  21.6 1.7 %collective-permute-start.7 = (f32[288,128]{1,0:T(8,128)S(1)}, f32[288,128]{1,0:T(8,128)S(1)}, u32[]{:S(2)}, u32[]{:S(2)}) collective-permute-start(f32[288,128]{1,0:T(8,128)S(1)} %get-tuple-element.24), channel_id=1, source_target_pairs={{0,12},{1,13},{2,14},{3,15},{4,0},{5,1},{6,2},{7,3},{8,4},{9,5},{1... | collective-permute-start | bytes 442376 | tf_op jit(solution)/shard_map/ppermute | solution.py:783
  23.2 0.0 collective-permute-done.10.xb2_ref
  23.2 0.0 collective-permute-done.11.xc2_ref
  23.2 8.6 %shard_map.54.corr_ref = f32[24,8,128]{2,1,0:T(8,128)S(1)} custom-call(f32[240,128]{1,0:T(8,128)S(1)} %shard_map.52.own_ref, f32[240,128]{1,0:T(8,128)S(1)} %collective-permute-done.5.xd_ref, f32[240,128]{1,0:T(8,128)S(1)} %collective-permute-done.2.xa_ref, f32[240,128]{1,0:T(8,128)S(1)} %collective-permute-done.9.xa2_ref, ...), custom_call_target="tpu_custom_call" | custom-call | flops 1000000000 | bytes 1000000000 | tf_op jit(solution)/shard_map/pallas_call | solution.py:716
  31.9 0.0 collective-permute-done.6.up_ref
  31.9 0.0 collective-permute-done.7.down_ref
  31.9 0.0 collective-permute-done.8.mz_ref
  31.9 0.9 %shard_map.55 = (f32[24,3,8,128]{3,2,1,0:T(8,128)}, f32[576,128]{1,0:T(8,128)}) custom-call(f32[576,128]{1,0:T(8,128)S(1)} %get-tuple-element.17.own_ref, f32[576,128]{1,0:T(8,128)S(1)} %shard_map.53.acc_ref, f32[144,128]{1,0:T(8,128)S(1)} %get-tuple-element.19.gauge_ref, f32[288,128]{1,0:T(8,128)S(1)} %collective-permute-done.6.up_ref, ...), custom_call_target="tpu_custom_call" | custom-call | flops 4000000 | bytes 3000000 | tf_op jit(solution)/shard_map/pallas_call | solution.py:716
  (1 shorter events, 0.0 us)
Async XLA Ops:
  0.6 1.9 %collective-permute-start = (f32[576,128]{1,0:T(8,128)}, f32[576,128]{1,0:T(8,128)S(1)}, u32[]{:S(2)}, u32[]{:S(2)}) collective-permute-start(f32[576,128]{1,0:T(8,128)} %bitcast.5), channel_id=1, source_target_pairs={{0,1},{1,0},{2,3},{3,2},{4,5},{5,4},{6,7},{7,6},{8,9},{9,8},{10,11... | collective-permute-start | bytes 884744 | tf_op jit(solution)/shard_map/ppermute | solution.py:733
  1.1 1.8 %collective-permute-start.1 = (f32[576,128]{1,0:T(8,128)}, f32[576,128]{1,0:T(8,128)S(1)}, u32[]{:S(2)}, u32[]{:S(2)}) collective-permute-start(f32[576,128]{1,0:T(8,128)} %bitcast.7), channel_id=1, source_target_pairs={{0,1},{1,0},{2,3},{3,2},{4,5},{5,4},{6,7},{7,6},{8,9},{9,8},{10,11... | collective-permute-start | bytes 884744 | tf_op jit(solution)/shard_map/ppermute | solution.py:734
  3.0 8.5 %collective-permute-start.5 = (f32[240,128]{1,0:T(8,128)S(1)}, f32[240,128]{1,0:T(8,128)S(1)}, u32[]{:S(2)}, u32[]{:S(2)}) collective-permute-start(f32[240,128]{1,0:T(8,128)S(1)} %shard_map.52.own_ref), channel_id=1, source_target_pairs={{0,2},{1,3},{2,0},{3,1},{4,6},{5,7},{6,4},{7,5},{8,10},{9,11},{10,... | collective-permute-start | bytes 368648 | tf_op jit(solution)/shard_map/ppermute | solution.py:777
  6.0 12.4 %collective-permute-start.4 = (f32[240,128]{1,0:T(8,128)S(1)}, f32[240,128]{1,0:T(8,128)S(1)}, u32[]{:S(2)}, u32[]{:S(2)}) collective-permute-start(f32[240,128]{1,0:T(8,128)S(1)} %shard_map.52.own_ref), channel_id=1, source_target_pairs={{0,8},{1,11},{2,10},{3,9},{4,12},{5,15},{6,14},{7,13},{8,0},{9,3},... | collective-permute-start | bytes 368648 | tf_op jit(solution)/shard_map/ppermute | solution.py:778
  8.5 9.8 %collective-permute-start.3 = (f32[240,128]{1,0:T(8,128)S(1)}, f32[240,128]{1,0:T(8,128)S(1)}, u32[]{:S(2)}, u32[]{:S(2)}) collective-permute-start(f32[240,128]{1,0:T(8,128)S(1)} %shard_map.52.own_ref), channel_id=1, source_target_pairs={{0,12},{1,15},{2,14},{3,13},{4,0},{5,3},{6,2},{7,1},{8,4},{9,7},{1... | collective-permute-start | bytes 368648 | tf_op jit(solution)/shard_map/ppermute | solution.py:779
  9.9 8.5 %collective-permute-start.2 = (f32[240,128]{1,0:T(8,128)S(1)}, f32[240,128]{1,0:T(8,128)S(1)}, u32[]{:S(2)}, u32[]{:S(2)}) collective-permute-start(f32[240,128]{1,0:T(8,128)S(1)} %shard_map.52.own_ref), channel_id=1, source_target_pairs={{0,4},{1,7},{2,6},{3,5},{4,8},{5,11},{6,10},{7,9},{8,12},{9,15},{1... | collective-permute-start | bytes 368648 | tf_op jit(solution)/shard_map/ppermute | solution.py:780
  10.6 21.3 %collective-permute-start.8 = (f32[576,128]{1,0:T(8,128)S(1)}, f32[576,128]{1,0:T(8,128)S(1)}, u32[]{:S(2)}, u32[]{:S(2)}) collective-permute-start(f32[576,128]{1,0:T(8,128)S(1)} %get-tuple-element.25), channel_id=1, source_target_pairs={{0,2},{1,3},{2,0},{3,1},{4,6},{5,7},{6,4},{7,5},{8,10},{9,11},{10,... | collective-permute-start | bytes 884744 | tf_op jit(solution)/shard_map/ppermute | solution.py:781
  18.4 3.2 %collective-permute-start.9 = (f32[240,128]{1,0:T(8,128)S(1)}, f32[240,128]{1,0:T(8,128)S(1)}, u32[]{:S(2)}, u32[]{:S(2)}) collective-permute-start(f32[240,128]{1,0:T(8,128)S(1)} %collective-permute-done.2.xa_ref), channel_id=1, source_target_pairs={{0,1},{1,0},{2,3},{3,2},{4,5},{5,4},{6,7},{7,6},{8,9},{9,8},{10,11... | collective-permute-start | bytes 368648 | tf_op jit(solution)/shard_map/ppermute | solution.py:794
  18.9 4.3 %collective-permute-start.10 = (f32[240,128]{1,0:T(8,128)S(1)}, f32[240,128]{1,0:T(8,128)S(1)}, u32[]{:S(2)}, u32[]{:S(2)}) collective-permute-start(f32[240,128]{1,0:T(8,128)S(1)} %collective-permute-done.3.xb_ref), channel_id=1, source_target_pairs={{0,1},{1,0},{2,3},{3,2},{4,5},{5,4},{6,7},{7,6},{8,9},{9,8},{10,11... | collective-permute-start | bytes 368648 | tf_op jit(solution)/shard_map/ppermute | solution.py:795
  18.9 4.3 %collective-permute-start.11 = (f32[240,128]{1,0:T(8,128)S(1)}, f32[240,128]{1,0:T(8,128)S(1)}, u32[]{:S(2)}, u32[]{:S(2)}) collective-permute-start(f32[240,128]{1,0:T(8,128)S(1)} %collective-permute-done.4.xc_ref), channel_id=1, source_target_pairs={{0,1},{1,0},{2,3},{3,2},{4,5},{5,4},{6,7},{7,6},{8,9},{9,8},{10,11... | collective-permute-start | bytes 368648 | tf_op jit(solution)/shard_map/ppermute | solution.py:796
  19.4 12.4 %collective-permute-start.6 = (f32[288,128]{1,0:T(8,128)S(1)}, f32[288,128]{1,0:T(8,128)S(1)}, u32[]{:S(2)}, u32[]{:S(2)}) collective-permute-start(f32[288,128]{1,0:T(8,128)S(1)} %get-tuple-element.23), channel_id=1, source_target_pairs={{0,4},{1,5},{2,6},{3,7},{4,8},{5,9},{6,10},{7,11},{8,12},{9,13},{1... | collective-permute-start | bytes 442376 | tf_op jit(solution)/shard_map/ppermute | solution.py:782
  21.6 10.3 %collective-permute-start.7 = (f32[288,128]{1,0:T(8,128)S(1)}, f32[288,128]{1,0:T(8,128)S(1)}, u32[]{:S(2)}, u32[]{:S(2)}) collective-permute-start(f32[288,128]{1,0:T(8,128)S(1)} %get-tuple-element.24), channel_id=1, source_target_pairs={{0,12},{1,13},{2,14},{3,15},{4,0},{5,1},{6,2},{7,3},{8,4},{9,5},{1... | collective-permute-start | bytes 442376 | tf_op jit(solution)/shard_map/ppermute | solution.py:783

commit v7 on v6

--- a/solution.py
+++ b/solution.py
@@ -543,7 +543,7 @@
         copies[-1].start()
     zero = jnp.zeros((8, 128), jnp.float32)
     for s in range(1, 7):
-        for comp in range(24):
+        for comp in {3: LOWER, 4: UPPER}.get(s, range(24)):
             for dz in range(2):
                 r_ref[s, comp, dz] = zero
     for copy in copies:

time: 33 us -> 33 us (level)
  no operation moved by 1% of the time
where the time goes in v7:
time: 33 us; the launch traced here: 32.8 us
  starting transfers between devices  13.5 us (41%)
  Pallas kernels  11.4 us (35%)
  waiting for transfers between devices  7.17 us (22%)
  between operations  0.7 us (2%)
    pallas_call x6, Pallas kernels, call(): pl.pallas_call(kernel, out_shape=shapes, in_specs=in_specs, out_specs=[pl...  11.4 us
    ppermute x1, waiting for transfers between devices, small_body(): xc = lax.ppermute(blk, axes, route(lambda s: (2, s)))  6.75 us
    ppermute x1, starting transfers between devices, small_body(): xd = lax.ppermute(blk, axes, route(lambda s: (0, 1)))  2.92 us
    ppermute x1, starting transfers between devices, small_body(): xc = lax.ppermute(blk, axes, route(lambda s: (2, s)))  2.59 us
    ppermute x1, starting transfers between devices, small_body(): ta = lax.ppermute(up, axes, route(lambda s: (1, 0)))  2.14 us
    ppermute x1, starting transfers between devices, small_body(): tb = lax.ppermute(down, axes, route(lambda s: (-1, 0)))  1.69 us
    ppermute x1, starting transfers between devices, small_body(): xb = lax.ppermute(blk, axes, route(lambda s: (-1, s)))  1.35 us
    ppermute x1, starting transfers between devices, small_body(): xa = lax.ppermute(blk, axes, route(lambda s: (1, s)))  0.68 us
  transfers between devices with their start and end apart: 12, of which 3 were waited for; matrix products, arithmetic and copies ran while one was open for 0% of the time, Pallas kernels for 32%

profile of v7, /device:TPU:0, one launch (start us, length us, event | category | flops | bytes accessed | tf_op | source)
XLA Modules:
  0.0 32.8 jit_solution(10140619036156394247)
XLA Ops:
  0.6 0.5 %collective-permute-start = (f32[576,128]{1,0:T(8,128)}, f32[576,128]{1,0:T(8,128)S(1)}, u32[]{:S(2)}, u32[]{:S(2)}) collective-permute-start(f32[576,128]{1,0:T(8,128)} %bitcast.5), channel_id=1, source_target_pairs={{0,1},{1,0},{2,3},{3,2},{4,5},{5,4},{6,7},{7,6},{8,9},{9,8},{10,11... | collective-permute-start | bytes 884744 | tf_op jit(solution)/shard_map/ppermute | solution.py:733
  1.1 0.1 collective-permute-start.1
  1.2 1.1 %shard_map.50 = (f32[576,128]{1,0:T(8,128)S(1)}, f32[576,128]{1,0:T(8,128)S(1)}, f32[144,128]{1,0:T(8,128)S(1)}) custom-call(f32[576,128]{1,0:T(8,128)} %bitcast.6, f32[576,128]{1,0:T(8,128)} %bitcast.8, f32[144,128]{1,0:T(8,128)} %bitcast.9), custom_call_target="tpu_custom_call" | custom-call | bytes 1300000 | tf_op jit(solution)/shard_map/pallas_call | solution.py:716
  2.3 0.2 collective-permute-done.oth_ref
  2.6 0.3 shard_map.51
  2.9 0.1 collective-permute-done.1.src_oth_ref
  3.0 2.9 %collective-permute-start.5 = (f32[240,128]{1,0:T(8,128)S(1)}, f32[240,128]{1,0:T(8,128)S(1)}, u32[]{:S(2)}, u32[]{:S(2)}) collective-permute-start(f32[240,128]{1,0:T(8,128)S(1)} %shard_map.52.own_ref), channel_id=1, source_target_pairs={{0,2},{1,3},{2,0},{3,1},{4,6},{5,7},{6,4},{7,5},{8,10},{9,11},{10,... | collective-permute-start | bytes 368648 | tf_op jit(solution)/shard_map/ppermute | solution.py:777
  6.0 2.6 %collective-permute-start.4 = (f32[240,128]{1,0:T(8,128)S(1)}, f32[240,128]{1,0:T(8,128)S(1)}, u32[]{:S(2)}, u32[]{:S(2)}) collective-permute-start(f32[240,128]{1,0:T(8,128)S(1)} %shard_map.52.own_ref), channel_id=1, source_target_pairs={{0,8},{1,11},{2,10},{3,9},{4,12},{5,15},{6,14},{7,13},{8,0},{9,3},... | collective-permute-start | bytes 368648 | tf_op jit(solution)/shard_map/ppermute | solution.py:778
  8.5 1.3 %collective-permute-start.3 = (f32[240,128]{1,0:T(8,128)S(1)}, f32[240,128]{1,0:T(8,128)S(1)}, u32[]{:S(2)}, u32[]{:S(2)}) collective-permute-start(f32[240,128]{1,0:T(8,128)S(1)} %shard_map.52.own_ref), channel_id=1, source_target_pairs={{0,12},{1,15},{2,14},{3,13},{4,0},{5,3},{6,2},{7,1},{8,4},{9,7},{1... | collective-permute-start | bytes 368648 | tf_op jit(solution)/shard_map/ppermute | solution.py:779
  9.9 0.7 %collective-permute-start.2 = (f32[240,128]{1,0:T(8,128)S(1)}, f32[240,128]{1,0:T(8,128)S(1)}, u32[]{:S(2)}, u32[]{:S(2)}) collective-permute-start(f32[240,128]{1,0:T(8,128)S(1)} %shard_map.52.own_ref), channel_id=1, source_target_pairs={{0,4},{1,7},{2,6},{3,5},{4,8},{5,11},{6,10},{7,9},{8,12},{9,15},{1... | collective-permute-start | bytes 368648 | tf_op jit(solution)/shard_map/ppermute | solution.py:780
  10.6 0.5 %collective-permute-start.8 = (f32[576,128]{1,0:T(8,128)S(1)}, f32[576,128]{1,0:T(8,128)S(1)}, u32[]{:S(2)}, u32[]{:S(2)}) collective-permute-start(f32[576,128]{1,0:T(8,128)S(1)} %get-tuple-element.25), channel_id=1, source_target_pairs={{0,2},{1,3},{2,0},{3,1},{4,6},{5,7},{6,4},{7,5},{8,10},{9,11},{10,... | collective-permute-start | bytes 884744 | tf_op jit(solution)/shard_map/ppermute | solution.py:781
  11.1 0.5 %shard_map.53.acc_ref = f32[576,128]{1,0:T(8,128)S(1)} custom-call(f32[576,128]{1,0:T(8,128)S(1)} %get-tuple-element.17.own_ref, f32[576,128]{1,0:T(8,128)S(1)} %get-tuple-element.20.bl_ref, f32[576,128]{1,0:T(8,128)S(1)} %get-tuple-element.18.src_own_ref.src_ref, f32[144,128]{1,0:T(8,128)S(1)} %get-tuple-element.19.gauge_ref), custom_call_target="tpu_custom_call" | custom-call | flops 4000000 | bytes 3000000 | tf_op jit(solution)/shard_map/pallas_call | solution.py:716
  11.6 0.0 collective-permute-done.5.xd_ref
  11.6 6.8 %collective-permute-done.4.xc_ref = f32[240,128]{1,0:T(8,128)S(1)} collective-permute-done((f32[240,128]{1,0:T(8,128)S(1)}, f32[240,128]{1,0:T(8,128)S(1)}, u32[]{:S(2)}, u32[]{:S(2)}) %collective-permute-start.4) | collective-permute-done | bytes 122912 | tf_op jit(solution)/shard_map/ppermute | solution.py:778
  18.3 0.0 collective-permute-done.3.xb_ref
  18.4 0.0 collective-permute-done.2.xa_ref
  18.4 0.5 %collective-permute-start.9 = (f32[240,128]{1,0:T(8,128)S(1)}, f32[240,128]{1,0:T(8,128)S(1)}, u32[]{:S(2)}, u32[]{:S(2)}) collective-permute-start(f32[240,128]{1,0:T(8,128)S(1)} %collective-permute-done.2.xa_ref), channel_id=1, source_target_pairs={{0,1},{1,0},{2,3},{3,2},{4,5},{5,4},{6,7},{7,6},{8,9},{9,8},{10,11... | collective-permute-start | bytes 368648 | tf_op jit(solution)/shard_map/ppermute | solution.py:794
  18.9 0.0 collective-permute-start.10
  18.9 0.5 %collective-permute-start.11 = (f32[240,128]{1,0:T(8,128)S(1)}, f32[240,128]{1,0:T(8,128)S(1)}, u32[]{:S(2)}, u32[]{:S(2)}) collective-permute-start(f32[240,128]{1,0:T(8,128)S(1)} %collective-permute-done.4.xc_ref), channel_id=1, source_target_pairs={{0,1},{1,0},{2,3},{3,2},{4,5},{5,4},{6,7},{7,6},{8,9},{9,8},{10,11... | collective-permute-start | bytes 368648 | tf_op jit(solution)/shard_map/ppermute | solution.py:796
  19.4 2.1 %collective-permute-start.6 = (f32[288,128]{1,0:T(8,128)S(1)}, f32[288,128]{1,0:T(8,128)S(1)}, u32[]{:S(2)}, u32[]{:S(2)}) collective-permute-start(f32[288,128]{1,0:T(8,128)S(1)} %get-tuple-element.23), channel_id=1, source_target_pairs={{0,4},{1,5},{2,6},{3,7},{4,8},{5,9},{6,10},{7,11},{8,12},{9,13},{1... | collective-permute-start | bytes 442376 | tf_op jit(solution)/shard_map/ppermute | solution.py:782
  21.5 0.0 collective-permute-done.9.xa2_ref
  21.6 1.7 %collective-permute-start.7 = (f32[288,128]{1,0:T(8,128)S(1)}, f32[288,128]{1,0:T(8,128)S(1)}, u32[]{:S(2)}, u32[]{:S(2)}) collective-permute-start(f32[288,128]{1,0:T(8,128)S(1)} %get-tuple-element.24), channel_id=1, source_target_pairs={{0,12},{1,13},{2,14},{3,15},{4,0},{5,1},{6,2},{7,3},{8,4},{9,5},{1... | collective-permute-start | bytes 442376 | tf_op jit(solution)/shard_map/ppermute | solution.py:783
  23.2 0.0 collective-permute-done.10.xb2_ref
  23.2 0.0 collective-permute-done.11.xc2_ref
  23.2 8.6 %shard_map.54.corr_ref = f32[24,8,128]{2,1,0:T(8,128)S(1)} custom-call(f32[240,128]{1,0:T(8,128)S(1)} %shard_map.52.own_ref, f32[240,128]{1,0:T(8,128)S(1)} %collective-permute-done.5.xd_ref, f32[240,128]{1,0:T(8,128)S(1)} %collective-permute-done.2.xa_ref, f32[240,128]{1,0:T(8,128)S(1)} %collective-permute-done.9.xa2_ref, ...), custom_call_target="tpu_custom_call" | custom-call | flops 1000000000 | bytes 1000000000 | tf_op jit(solution)/shard_map/pallas_call | solution.py:716
  31.8 0.0 collective-permute-done.6.up_ref
  31.9 0.0 collective-permute-done.7.down_ref
  31.9 0.0 collective-permute-done.8.mz_ref
  31.9 0.9 %shard_map.55 = (f32[24,3,8,128]{3,2,1,0:T(8,128)}, f32[576,128]{1,0:T(8,128)}) custom-call(f32[576,128]{1,0:T(8,128)S(1)} %get-tuple-element.17.own_ref, f32[576,128]{1,0:T(8,128)S(1)} %shard_map.53.acc_ref, f32[144,128]{1,0:T(8,128)S(1)} %get-tuple-element.19.gauge_ref, f32[288,128]{1,0:T(8,128)S(1)} %collective-permute-done.6.up_ref, ...), custom_call_target="tpu_custom_call" | custom-call | flops 4000000 | bytes 3000000 | tf_op jit(solution)/shard_map/pallas_call | solution.py:716
  (1 shorter events, 0.0 us)
Async XLA Ops:
  0.6 1.9 %collective-permute-start = (f32[576,128]{1,0:T(8,128)}, f32[576,128]{1,0:T(8,128)S(1)}, u32[]{:S(2)}, u32[]{:S(2)}) collective-permute-start(f32[576,128]{1,0:T(8,128)} %bitcast.5), channel_id=1, source_target_pairs={{0,1},{1,0},{2,3},{3,2},{4,5},{5,4},{6,7},{7,6},{8,9},{9,8},{10,11... | collective-permute-start | bytes 884744 | tf_op jit(solution)/shard_map/ppermute | solution.py:733
  1.1 1.8 %collective-permute-start.1 = (f32[576,128]{1,0:T(8,128)}, f32[576,128]{1,0:T(8,128)S(1)}, u32[]{:S(2)}, u32[]{:S(2)}) collective-permute-start(f32[576,128]{1,0:T(8,128)} %bitcast.7), channel_id=1, source_target_pairs={{0,1},{1,0},{2,3},{3,2},{4,5},{5,4},{6,7},{7,6},{8,9},{9,8},{10,11... | collective-permute-start | bytes 884744 | tf_op jit(solution)/shard_map/ppermute | solution.py:734
  3.0 8.5 %collective-permute-start.5 = (f32[240,128]{1,0:T(8,128)S(1)}, f32[240,128]{1,0:T(8,128)S(1)}, u32[]{:S(2)}, u32[]{:S(2)}) collective-permute-start(f32[240,128]{1,0:T(8,128)S(1)} %shard_map.52.own_ref), channel_id=1, source_target_pairs={{0,2},{1,3},{2,0},{3,1},{4,6},{5,7},{6,4},{7,5},{8,10},{9,11},{10,... | collective-permute-start | bytes 368648 | tf_op jit(solution)/shard_map/ppermute | solution.py:777
  6.0 12.4 %collective-permute-start.4 = (f32[240,128]{1,0:T(8,128)S(1)}, f32[240,128]{1,0:T(8,128)S(1)}, u32[]{:S(2)}, u32[]{:S(2)}) collective-permute-start(f32[240,128]{1,0:T(8,128)S(1)} %shard_map.52.own_ref), channel_id=1, source_target_pairs={{0,8},{1,11},{2,10},{3,9},{4,12},{5,15},{6,14},{7,13},{8,0},{9,3},... | collective-permute-start | bytes 368648 | tf_op jit(solution)/shard_map/ppermute | solution.py:778
  8.5 9.8 %collective-permute-start.3 = (f32[240,128]{1,0:T(8,128)S(1)}, f32[240,128]{1,0:T(8,128)S(1)}, u32[]{:S(2)}, u32[]{:S(2)}) collective-permute-start(f32[240,128]{1,0:T(8,128)S(1)} %shard_map.52.own_ref), channel_id=1, source_target_pairs={{0,12},{1,15},{2,14},{3,13},{4,0},{5,3},{6,2},{7,1},{8,4},{9,7},{1... | collective-permute-start | bytes 368648 | tf_op jit(solution)/shard_map/ppermute | solution.py:779
  9.9 8.5 %collective-permute-start.2 = (f32[240,128]{1,0:T(8,128)S(1)}, f32[240,128]{1,0:T(8,128)S(1)}, u32[]{:S(2)}, u32[]{:S(2)}) collective-permute-start(f32[240,128]{1,0:T(8,128)S(1)} %shard_map.52.own_ref), channel_id=1, source_target_pairs={{0,4},{1,7},{2,6},{3,5},{4,8},{5,11},{6,10},{7,9},{8,12},{9,15},{1... | collective-permute-start | bytes 368648 | tf_op jit(solution)/shard_map/ppermute | solution.py:780
  10.6 21.3 %collective-permute-start.8 = (f32[576,128]{1,0:T(8,128)S(1)}, f32[576,128]{1,0:T(8,128)S(1)}, u32[]{:S(2)}, u32[]{:S(2)}) collective-permute-start(f32[576,128]{1,0:T(8,128)S(1)} %get-tuple-element.25), channel_id=1, source_target_pairs={{0,2},{1,3},{2,0},{3,1},{4,6},{5,7},{6,4},{7,5},{8,10},{9,11},{10,... | collective-permute-start | bytes 884744 | tf_op jit(solution)/shard_map/ppermute | solution.py:781
  18.4 3.2 %collective-permute-start.9 = (f32[240,128]{1,0:T(8,128)S(1)}, f32[240,128]{1,0:T(8,128)S(1)}, u32[]{:S(2)}, u32[]{:S(2)}) collective-permute-start(f32[240,128]{1,0:T(8,128)S(1)} %collective-permute-done.2.xa_ref), channel_id=1, source_target_pairs={{0,1},{1,0},{2,3},{3,2},{4,5},{5,4},{6,7},{7,6},{8,9},{9,8},{10,11... | collective-permute-start | bytes 368648 | tf_op jit(solution)/shard_map/ppermute | solution.py:794
  18.9 4.3 %collective-permute-start.10 = (f32[240,128]{1,0:T(8,128)S(1)}, f32[240,128]{1,0:T(8,128)S(1)}, u32[]{:S(2)}, u32[]{:S(2)}) collective-permute-start(f32[240,128]{1,0:T(8,128)S(1)} %collective-permute-done.3.xb_ref), channel_id=1, source_target_pairs={{0,1},{1,0},{2,3},{3,2},{4,5},{5,4},{6,7},{7,6},{8,9},{9,8},{10,11... | collective-permute-start | bytes 368648 | tf_op jit(solution)/shard_map/ppermute | solution.py:795
  18.9 4.3 %collective-permute-start.11 = (f32[240,128]{1,0:T(8,128)S(1)}, f32[240,128]{1,0:T(8,128)S(1)}, u32[]{:S(2)}, u32[]{:S(2)}) collective-permute-start(f32[240,128]{1,0:T(8,128)S(1)} %collective-permute-done.4.xc_ref), channel_id=1, source_target_pairs={{0,1},{1,0},{2,3},{3,2},{4,5},{5,4},{6,7},{7,6},{8,9},{9,8},{10,11... | collective-permute-start | bytes 368648 | tf_op jit(solution)/shard_map/ppermute | solution.py:796
  19.4 12.4 %collective-permute-start.6 = (f32[288,128]{1,0:T(8,128)S(1)}, f32[288,128]{1,0:T(8,128)S(1)}, u32[]{:S(2)}, u32[]{:S(2)}) collective-permute-start(f32[288,128]{1,0:T(8,128)S(1)} %get-tuple-element.23), channel_id=1, source_target_pairs={{0,4},{1,5},{2,6},{3,7},{4,8},{5,9},{6,10},{7,11},{8,12},{9,13},{1... | collective-permute-start | bytes 442376 | tf_op jit(solution)/shard_map/ppermute | solution.py:782
  21.6 10.3 %collective-permute-start.7 = (f32[288,128]{1,0:T(8,128)S(1)}, f32[288,128]{1,0:T(8,128)S(1)}, u32[]{:S(2)}, u32[]{:S(2)}) collective-permute-start(f32[288,128]{1,0:T(8,128)S(1)} %get-tuple-element.24), channel_id=1, source_target_pairs={{0,12},{1,13},{2,14},{3,15},{4,0},{5,1},{6,2},{7,3},{8,4},{9,5},{1... | collective-permute-start | bytes 442376 | tf_op jit(solution)/shard_map/ppermute | solution.py:783
